TPU v7x, 32 devices: a whole 2x2x4 slice. The times are simulated.
32 devices in a mesh: fsdp: 4 (over z), ctx: 4 (over y, core), tp: 2 (over x).
Axes of the slice: x: 2, y: 2, z: 4, core: 2. Of those that a mesh axis runs over, the one named last changes fastest.
Arguments:
- tokens: bfloat16 [4, 2048, 2048], P('fsdp', ('ctx', 'tp')), may hold values from -6 to 6
- positions: int32 [2048], replicated, may hold values from 0 to 2047, as said below
- cotangent: bfloat16 [4, 2048, 2048], P('fsdp', ('ctx', 'tp')), may hold values from -6 to 6
- norm_gain: bfloat16 [2048], replicated, may hold values from 0.5 to 1.5
- norm_bias: bfloat16 [2048], replicated, may hold values from -1.75 to 1.75
- qkv_weight: bfloat16 [2048, 3, 2048], P(('fsdp', 'ctx'), None, 'tp'), may hold values from -0.125 to 0.125
- qkv_bias: bfloat16 [3, 2048], P(None, 'tp'), may hold values from -1.75 to 1.75
- out_weight: bfloat16 [2048, 2048], P('tp', ('fsdp', 'ctx')), may hold values from -3 to 3
- out_bias: bfloat16 [2048], replicated, may hold values from -1.75 to 1.75
- up_weight: bfloat16 [2048, 8192], P(('fsdp', 'ctx'), 'tp'), may hold values from -0.125 to 0.125
- up_bias: bfloat16 [8192], P('tp'), may hold values from -1.75 to 1.75
- down_weight: bfloat16 [8192, 2048], P('tp', ('fsdp', 'ctx')), may hold values from -0.0625 to 0.0625
- down_bias: bfloat16 [2048], replicated, may hold values from -1.75 to 1.75
Outputs:
- layer_output: bfloat16 [4, 2048, 2048], P('fsdp', ('ctx', 'tp'))
- tokens_grad: float32 [4, 2048, 2048], P('fsdp', ('ctx', 'tp'))
- norm_gain_grad: float32 [2048], replicated
- norm_bias_grad: float32 [2048], replicated
- qkv_weight_grad: float32 [2048, 3, 2048], P(('fsdp', 'ctx'), None, 'tp')
- qkv_bias_grad: float32 [3, 2048], P(None, 'tp')
- out_weight_grad: float32 [2048, 2048], P('tp', ('fsdp', 'ctx'))
- out_bias_grad: float32 [2048], replicated
- up_weight_grad: float32 [2048, 8192], P(('fsdp', 'ctx'), 'tp')
- up_bias_grad: float32 [8192], P('tp')
- down_weight_grad: float32 [8192, 2048], P('tp', ('fsdp', 'ctx'))
- down_bias_grad: float32 [2048], replicated
Inputs may be any that keep to these rules, and one draw needn't show every extreme that they name: The sequence is cut into 8 groups of 256 consecutive positions; each block of 512 stored rows holds group k and group 2 * 4 - 1 - k, each in ascending order; which k lies in which block and the two groups' order vary with the seed; every position appears once.
All inputs are finite; a program needn't handle non-finite values.
Results may differ from a plain program's by a relative error of at most 0.014.
Values may be sent and summed in bfloat16 or wider, within the bound.
No kernel may reach another device: no remote copies, remote signals or barrier semaphores. Data moves between devices by JAX's collectives and lax.ppermute only.
A program may use at most 256 MiB of HBM per device.

v0:
```python
import jax
import jax.numpy as jnp
from jax import lax
from jax.sharding import PartitionSpec as P

D = 2048
HEAD_DIM = 64
ROT = 32


EPSILON = 1e-05
MASKED = -1e30


def turning(places):
    halfway = ROT // 2
    frequencies = 10000.0 ** (-(jnp.arange(halfway, dtype=jnp.float32) * 2.0 / ROT))
    angle_table = places.astype(jnp.float32)[:, None] * frequencies[None, :]
    return (jnp.cos(angle_table)[:, None, :], jnp.sin(angle_table)[:, None, :])


def rotate(values, cosine_table, sine_table):
    halfway = ROT // 2
    first_half = values[..., :halfway]
    second_half = values[..., halfway:ROT]
    return jnp.concatenate(
        [
            first_half * cosine_table - second_half * sine_table,
            second_half * cosine_table + first_half * sine_table,
            values[..., ROT:],
        ],
        axis=-1,
    )


def blocked(values, block_rows):
    shaped = values.reshape(
        (values.shape[0], values.shape[1] // block_rows, block_rows) + values.shape[2:]
    )
    return jnp.moveaxis(shaped, 1, 0)


def unblocked(values):
    moved_axes = jnp.moveaxis(values, 0, 1)
    return moved_axes.reshape(
        (moved_axes.shape[0], moved_axes.shape[1] * moved_axes.shape[2]) + moved_axes.shape[3:]
    )


def tile_scores(query_block, key_block, query_places, key_places):
    scores = jnp.einsum(
        "sqhd,skhd->shqk", query_block, key_block, preferred_element_type=jnp.float32
    ) * HEAD_DIM ** (-0.5)
    causal = (query_places[:, None] >= key_places[None, :])[None, None]
    return (jnp.where(causal, scores, MASKED), causal)


def attend(queries, keys_all, values_all, query_places, key_places):
    query_rows = min(512, queries.shape[1])
    key_rows = min(512, keys_all.shape[1])
    key_items = (
        blocked(keys_all, key_rows),
        blocked(values_all, key_rows),
        key_places.reshape(-1, key_rows),
    )

    def attend_per_query(block_pair):
        query_block, own_places = block_pair
        row_shape = (query_block.shape[0], query_block.shape[2], query_block.shape[1])
        newest = jnp.max(own_places)

        def attend_key_step(running, key_triple):
            key_block, value_block, other_places = key_triple

            def attend_compute():
                running_max, running_sum, summed = running
                scores, causal = tile_scores(query_block, key_block, own_places, other_places)
                new_max = jnp.maximum(running_max, jnp.max(scores, axis=-1))
                exponentials = jnp.where(causal, jnp.exp(scores - new_max[..., None]), 0.0)
                factor = jnp.exp(running_max - new_max)
                new_sum = running_sum * factor + jnp.sum(exponentials, axis=-1)
                new_summed = summed * jnp.swapaxes(factor, 1, 2)[..., None] + jnp.einsum(
                    "shqk,skhd->sqhd",
                    exponentials.astype(jnp.bfloat16),
                    value_block,
                    preferred_element_type=jnp.float32,
                )
                return (new_max, new_sum, new_summed)

            return (lax.cond(jnp.min(other_places) > newest, lambda: running, attend_compute), None)

        initial = (
            jnp.full(row_shape, MASKED, jnp.float32),
            jnp.zeros(row_shape, jnp.float32),
            jnp.zeros(query_block.shape, jnp.float32),
        )
        (final_max, final_sum, summed), unused = lax.scan(attend_key_step, initial, key_items)
        result = summed / jnp.swapaxes(final_sum, 1, 2)[..., None]
        return (result, jnp.swapaxes(final_max + jnp.log(final_sum), 1, 2))

    results, log_sums = lax.map(
        attend_per_query, (blocked(queries, query_rows), query_places.reshape(-1, query_rows))
    )
    return (unblocked(results), unblocked(log_sums))


def tile_grads(query_block, grad_block, key_block, value_block, log_rows, own_places, other_places):
    scores, causal = tile_scores(query_block, key_block, own_places, other_places)
    probabilities = jnp.where(causal, jnp.exp(scores - log_rows), 0.0)
    prob_grads = jnp.einsum(
        "sqhd,skhd->shqk", grad_block, value_block, preferred_element_type=jnp.float32
    )
    return (probabilities, prob_grads)


def attention_grads(
    queries, out_grads, log_sums, delta_rows_all, query_places, keys_all, values_all, key_places
):
    score_scale = HEAD_DIM ** (-0.5)
    query_rows = min(512, queries.shape[1])
    key_rows = min(512, keys_all.shape[1])
    key_items = (
        blocked(keys_all, key_rows),
        blocked(values_all, key_rows),
        key_places.reshape(-1, key_rows),
    )

    def attention_per_query(key_totals, block_items):
        query_block, grad_block, log_block, delta_block, own_places = block_items
        log_rows = jnp.swapaxes(log_block, 1, 2)[..., None]
        delta_rows = jnp.swapaxes(delta_block, 1, 2)[..., None]
        newest = jnp.max(own_places)
        tile_shape = (query_block.shape[0], key_rows) + query_block.shape[2:]

        def attention_key_step(query_total, key_triple):
            key_block, value_block, other_places = key_triple

            def attention_compute():
                probabilities, prob_grads = tile_grads(
                    query_block,
                    grad_block,
                    key_block,
                    value_block,
                    log_rows,
                    own_places,
                    other_places,
                )
                score_grads = (probabilities * (prob_grads - delta_rows)).astype(jnp.bfloat16)
                new_total = query_total + jnp.einsum(
                    "shqk,skhd->sqhd", score_grads, key_block, preferred_element_type=jnp.float32
                )
                tile_parts = ()
                tile_parts = (
                    jnp.einsum(
                        "shqk,sqhd->skhd",
                        score_grads,
                        query_block,
                        preferred_element_type=jnp.float32,
                    ),
                    jnp.einsum(
                        "shqk,sqhd->skhd",
                        probabilities.astype(jnp.bfloat16),
                        grad_block,
                        preferred_element_type=jnp.float32,
                    ),
                )
                return (new_total, tile_parts)

            def skipped():
                tile_parts = ()
                tile_parts = (
                    jnp.zeros(tile_shape, jnp.float32),
                    jnp.zeros(tile_shape, jnp.float32),
                )
                return (query_total, tile_parts)

            return lax.cond(jnp.min(other_places) > newest, skipped, attention_compute)

        start_total = jnp.zeros(query_block.shape, jnp.float32)
        query_total, tile_parts = lax.scan(attention_key_step, start_total, key_items)
        key_totals = (
            key_totals[0] + unblocked(tile_parts[0]),
            key_totals[1] + unblocked(tile_parts[1]),
        )
        return (key_totals, query_total * score_scale)

    zero_keys = jnp.zeros(keys_all.shape, jnp.float32)
    start_keys = (zero_keys, zero_keys)
    key_totals, query_parts = lax.scan(
        attention_per_query,
        start_keys,
        (
            blocked(queries, query_rows),
            blocked(out_grads, query_rows),
            blocked(log_sums, query_rows),
            blocked(delta_rows_all, query_rows),
            query_places.reshape(-1, query_rows),
        ),
    )
    query_grads = unblocked(query_parts)
    key_grads = (key_totals[0] * score_scale, key_totals[1])
    return (query_grads, key_grads)


def on_device(
    tokens,
    positions,
    cotangent,
    norm_gain,
    norm_bias,
    qkv_weight,
    qkv_bias,
    out_weight,
    out_bias,
    up_weight,
    up_bias,
    down_weight,
    down_bias,
):
    seq_count = tokens.shape[0]
    local_width = qkv_weight.shape[2]
    local_heads = local_width // HEAD_DIM
    ctx_rows = tokens.shape[1] * lax.axis_size("tp")
    own_places = lax.dynamic_slice_in_dim(positions, lax.axis_index("ctx") * ctx_rows, ctx_rows)
    inputs = tokens.astype(jnp.float32)
    row_mean = jnp.mean(inputs, axis=-1, keepdims=True)
    centered = inputs - row_mean
    inverse = lax.rsqrt(jnp.mean(centered * centered, axis=-1, keepdims=True) + EPSILON)
    unit_rows = centered * inverse
    normed_low = (unit_rows * norm_gain + norm_bias).astype(jnp.bfloat16)
    normed_all = lax.all_gather(normed_low, "tp", axis=1, tiled=True)
    qkv_full, up_full = (
        lax.all_gather(qkv_weight, ("fsdp", "ctx"), axis=0, tiled=True),
        lax.all_gather(up_weight, ("fsdp", "ctx"), axis=0, tiled=True),
    )
    normed_flat = normed_all.reshape(seq_count * ctx_rows, D)
    qkv_matrix = qkv_full.reshape(D, 3 * local_width)
    mixed_qkv = jnp.dot(
        normed_flat, qkv_matrix, preferred_element_type=jnp.float32
    ) + qkv_bias.reshape(3 * local_width)
    hidden = jnp.dot(normed_flat, up_full, preferred_element_type=jnp.float32) + up_bias
    mixed_qkv = mixed_qkv.reshape(seq_count, ctx_rows, 3, local_heads, HEAD_DIM)
    cosine_table, sine_table = turning(own_places)
    queries = rotate(mixed_qkv[:, :, 0], cosine_table, sine_table).astype(jnp.bfloat16)
    keys_own = rotate(mixed_qkv[:, :, 1], cosine_table, sine_table).astype(jnp.bfloat16)
    values_own = mixed_qkv[:, :, 2].astype(jnp.bfloat16)
    keys_all, values_all = (
        lax.all_gather(
            keys_own.reshape(seq_count, ctx_rows, local_width), "ctx", axis=1, tiled=True
        ),
        lax.all_gather(
            values_own.reshape(seq_count, ctx_rows, local_width), "ctx", axis=1, tiled=True
        ),
    )
    keys_all = keys_all.reshape(seq_count, -1, local_heads, HEAD_DIM)
    values_all = values_all.reshape(seq_count, -1, local_heads, HEAD_DIM)
    attended, log_sums = attend(queries, keys_all, values_all, own_places, positions)
    attended_low = attended.reshape(seq_count * ctx_rows, local_width).astype(jnp.bfloat16)
    activated_low = jax.nn.gelu(hidden, approximate=True).astype(jnp.bfloat16)
    out_full, down_full = (
        lax.all_gather(out_weight, ("fsdp", "ctx"), axis=1, tiled=True),
        lax.all_gather(down_weight, ("fsdp", "ctx"), axis=1, tiled=True),
    )
    tp_partial = jnp.dot(attended_low, out_full, preferred_element_type=jnp.float32) + jnp.dot(
        activated_low, down_full, preferred_element_type=jnp.float32
    )
    branch_sum = lax.psum_scatter(
        tp_partial.reshape(seq_count, ctx_rows, D).astype(jnp.bfloat16),
        "tp",
        scatter_dimension=1,
        tiled=True,
    ).astype(jnp.float32)
    layer_output = (inputs + branch_sum + out_bias + down_bias).astype(jnp.bfloat16)
    grad_all = lax.all_gather(cotangent, "tp", axis=1, tiled=True)
    grad_flat = grad_all.reshape(seq_count * ctx_rows, D)
    out_terms = (
        jnp.einsum("nc,nf->cf", attended_low, grad_flat, preferred_element_type=jnp.float32),
        jnp.einsum("nc,nf->cf", activated_low, grad_flat, preferred_element_type=jnp.float32),
    )
    out_weight_grad, down_weight_grad = (
        lax.psum_scatter(
            out_terms[0].astype(jnp.bfloat16), ("fsdp", "ctx"), scatter_dimension=1, tiled=True
        ).astype(jnp.float32),
        lax.psum_scatter(
            out_terms[1].astype(jnp.bfloat16), ("fsdp", "ctx"), scatter_dimension=1, tiled=True
        ).astype(jnp.float32),
    )
    attended_grad = jnp.einsum(
        "nf,cf->nc", grad_flat, out_full, preferred_element_type=jnp.float32
    ).astype(jnp.bfloat16)
    activated_grad = jnp.einsum(
        "nf,cf->nc", grad_flat, down_full, preferred_element_type=jnp.float32
    )
    unused, gelu_pull = jax.vjp(lambda values: jax.nn.gelu(values, approximate=True), hidden)
    hidden_grad = gelu_pull(activated_grad)[0].astype(jnp.bfloat16)
    out_grads = attended_grad.reshape(seq_count, ctx_rows, local_heads, HEAD_DIM)
    deltas_own = jnp.sum(out_grads.astype(jnp.float32) * attended, axis=-1)
    query_grads, key_grads = attention_grads(
        queries, out_grads, log_sums, deltas_own, own_places, keys_all, values_all, positions
    )
    keys_grad, values_grad = (
        lax.psum_scatter(
            key_grads[0].reshape(seq_count, -1, local_width).astype(jnp.bfloat16),
            "ctx",
            scatter_dimension=1,
            tiled=True,
        ).astype(jnp.float32),
        lax.psum_scatter(
            key_grads[1].reshape(seq_count, -1, local_width).astype(jnp.bfloat16),
            "ctx",
            scatter_dimension=1,
            tiled=True,
        ).astype(jnp.float32),
    )
    keys_grad = keys_grad.reshape(seq_count, ctx_rows, local_heads, HEAD_DIM)
    values_grad = values_grad.reshape(seq_count, ctx_rows, local_heads, HEAD_DIM)
    qkv_grad = jnp.stack(
        [
            rotate(query_grads, cosine_table, -sine_table),
            rotate(keys_grad, cosine_table, -sine_table),
            values_grad,
        ],
        axis=2,
    )
    qkv_grad = qkv_grad.astype(jnp.bfloat16).reshape(seq_count * ctx_rows, 3 * local_width)
    bias_parts = (
        jnp.sum(qkv_grad, axis=0, dtype=jnp.float32).reshape(3, local_width),
        jnp.sum(hidden_grad, axis=0, dtype=jnp.float32),
    )
    qkv_bias_grad, up_bias_grad = lax.psum((bias_parts[0], bias_parts[1]), ("fsdp", "ctx"))
    in_grads = lax.psum_scatter(
        jnp.concatenate(
            [
                jnp.einsum("nc,nf->cf", normed_flat, qkv_grad, preferred_element_type=jnp.float32),
                jnp.einsum(
                    "nc,nf->cf", normed_flat, hidden_grad, preferred_element_type=jnp.float32
                ),
            ],
            axis=1,
        ).astype(jnp.bfloat16),
        ("fsdp", "ctx"),
        scatter_dimension=0,
        tiled=True,
    ).astype(jnp.float32)
    qkv_weight_grad = in_grads[:, : 3 * local_width].reshape(-1, 3, local_width)
    up_weight_grad = in_grads[:, 3 * local_width :]
    normed_part = jnp.einsum(
        "nc,fc->nf", qkv_grad, qkv_matrix, preferred_element_type=jnp.float32
    ) + jnp.einsum("nc,fc->nf", hidden_grad, up_full, preferred_element_type=jnp.float32)
    normed_back = lax.psum_scatter(
        normed_part.reshape(seq_count, ctx_rows, D).astype(jnp.bfloat16),
        "tp",
        scatter_dimension=1,
        tiled=True,
    ).astype(jnp.float32)
    unit_grad = normed_back * norm_gain
    tokens_grad = cotangent.astype(jnp.float32) + inverse * (
        unit_grad
        - jnp.mean(unit_grad, axis=-1, keepdims=True)
        - unit_rows * jnp.mean(unit_grad * unit_rows, axis=-1, keepdims=True)
    )
    gain_parts = (
        jnp.sum(normed_back * unit_rows, axis=(0, 1)),
        jnp.sum(normed_back, axis=(0, 1)),
        jnp.sum(cotangent, axis=(0, 1), dtype=jnp.float32),
    )
    gain_grad, shift_grad, bias_grad = lax.psum(
        (gain_parts[0], gain_parts[1], gain_parts[2]), ("fsdp", "ctx", "tp")
    )
    return (
        layer_output,
        tokens_grad,
        gain_grad,
        shift_grad,
        qkv_weight_grad,
        qkv_bias_grad,
        out_weight_grad,
        bias_grad,
        up_weight_grad,
        up_bias_grad,
        down_weight_grad,
        bias_grad,
    )


def solution(mesh):
    placed = (
        P("fsdp", ("ctx", "tp"), None),
        P(),
        P("fsdp", ("ctx", "tp"), None),
        P(),
        P(),
        P(("fsdp", "ctx"), None, "tp"),
        P(None, "tp"),
        P("tp", ("fsdp", "ctx")),
        P(),
        P(("fsdp", "ctx"), "tp"),
        P("tp"),
        P("tp", ("fsdp", "ctx")),
        P(),
    )
    return jax.shard_map(
        on_device,
        mesh=mesh,
        in_specs=placed,
        out_specs=(
            P("fsdp", ("ctx", "tp"), None),
            P("fsdp", ("ctx", "tp"), None),
            P(),
            P(),
            P(("fsdp", "ctx"), None, "tp"),
            P(None, "tp"),
            P("tp", ("fsdp", "ctx")),
            P(),
            P(("fsdp", "ctx"), "tp"),
            P("tp"),
            P("tp", ("fsdp", "ctx")),
            P(),
        ),
        check_vma=False,
    )
```

profile of v0, /device:TPU:0, one launch (start us, length us, event | category | flops | bytes accessed | tf_op | source)
XLA Modules:
  0.0 1313.1 jit_solution(9697365128696372634)
XLA Ops:
  18.6 32.4 %all-gather.9.cloned.1.call-done = bf16[1,512,2048]{2,1,0:T(8,128)(2,1)} async-done(((bf16[1,256,2048]{2,1,0:T(8,128)(2,1)}), bf16[1,512,2048]{2,1,0:T(8,128)(2,1)}) %all-gather.9.cloned.1.call-update) | async-done | bytes 2097168 | tf_op jit(solution)/shard_map/all_gather | solution.py:231
  51.1 106.7 %all-gather.11.cloned.1.call-done = bf16[2048,3,1024]{0,2,1:T(8,128)(2,1)} async-done(((bf16[128,3,1024]{0,2,1:T(8,128)(2,1)}), bf16[2048,3,1024]{0,2,1:T(8,128)(2,1)}) %all-gather.11.cloned.1.call-update) | async-done | bytes 12582928 | tf_op jit(solution)/shard_map/all_gather | solution.py:233
  190.6 55.3 %all-gather.17.cloned.1.call-done = bf16[1024,2048]{1,0:T(8,128)(2,1)} async-done(((bf16[1024,128]{1,0:T(8,128)(2,1)}), bf16[1024,2048]{1,0:T(8,128)(2,1)}) %all-gather.17.cloned.1.call-update) | async-done | bytes 4194320 | tf_op jit(solution)/shard_map/all_gather | solution.py:261
  253.6 27.0 %all-gather.13.cloned.1.call-done = bf16[1,2048,1024]{1,2,0:T(8,128)(2,1)} async-done(((bf16[1,512,1024]{1,2,0:T(8,128)(2,1)}), bf16[1,2048,1024]{1,2,0:T(8,128)(2,1)}) %all-gather.13.cloned.1.call-update) | async-done | bytes 4194320 | tf_op jit(solution)/shard_map/all_gather | solution.py:248
  294.0 23.1 %all-gather.15.cloned.1.call-done = bf16[1,2048,1024]{1,2,0:T(8,128)(2,1)} async-done(((bf16[1,512,1024]{1,2,0:T(8,128)(2,1)}), bf16[1,2048,1024]{1,2,0:T(8,128)(2,1)}) %all-gather.15.cloned.1.call-update) | async-done | bytes 4194320 | tf_op jit(solution)/shard_map/all_gather | solution.py:251
  330.7 64.5 %while.52 = (s32[]{:T(128)}, f32[1,16,512]{2,1,0:T(8,128)S(1)}, f32[1,16,512]{2,1,0:T(8,128)S(1)}, f32[1,512,16,64]{1,3,2,0:T(8,128)S(1)}, s32[4,512]{1,0:T(4,12...) while((s32[]{:T(128)}, f32[1,16,512]{2,1,0:T(8,128)S(1)}, ...), condition=%wide.region_9.10_spmd, body=%wide.region_3.9_spmd.sunk | while | flops 1129603584 | bytes 59254016 | solution.py:97
  398.1 180.9 %while.53 = (s32[]{:T(128)}, f32[1,512,16,64]{1,3,2,0:T(8,128)S(1)}, f32[4,1,512,16,64]{2,4,3,1,0:T(8,128)}, bf16[4,1,512,16,64]{2,4,3,1,0:T(8,128)(2,1)}, s32[4...) while((s32[]{:T(128)}, ...), condition=%wide.region_16.17_spmd, body=%wide.region_12.16_spmd.sunk | while | flops 2735473152 | bytes 104704296 | solution.py:180
  400.4 38.2 %conditional.5 = (f32[1,512,16,64]{1,3,2,0:T(8,128)S(1)}, f32[1,1,512,16,64]{2,4,3,1,0:T(8,128)}, f32[1,1,512,16,64]{2,4,3,1,0:T(8,128)}) conditional(s32[]{:T(128)} %convert_element_type.359, (bf16[4,1,512,16,64]{2,4,3,1,0:T(8,128)(2,1)}, s32[]{:T(128)}, s32[512]{0:T(512)S(1)}, s32[1,512]{1,0:T(1,128)S(1)}, ...), branch_computations={%region_14.14_spmd, %region_15.15_spmd} | conditional | flops 2735472640 | bytes 96310840 | solution.py:177
  445.2 38.8 %conditional.5 = (f32[1,512,16,64]{1,3,2,0:T(8,128)S(1)}, f32[1,1,512,16,64]{2,4,3,1,0:T(8,128)}, f32[1,1,512,16,64]{2,4,3,1,0:T(8,128)}) conditional(s32[]{:T(128)} %convert_element_type.359, (bf16[4,1,512,16,64]{2,4,3,1,0:T(8,128)(2,1)}, s32[]{:T(128)}, s32[512]{0:T(512)S(1)}, s32[1,512]{1,0:T(1,128)S(1)}, ...), branch_computations={%region_14.14_spmd, %region_15.15_spmd} | conditional | flops 2735472640 | bytes 96310840 | solution.py:177
  490.3 39.5 %conditional.5 = (f32[1,512,16,64]{1,3,2,0:T(8,128)S(1)}, f32[1,1,512,16,64]{2,4,3,1,0:T(8,128)}, f32[1,1,512,16,64]{2,4,3,1,0:T(8,128)}) conditional(s32[]{:T(128)} %convert_element_type.359, (bf16[4,1,512,16,64]{2,4,3,1,0:T(8,128)(2,1)}, s32[]{:T(128)}, s32[512]{0:T(512)S(1)}, s32[1,512]{1,0:T(1,128)S(1)}, ...), branch_computations={%region_14.14_spmd, %region_15.15_spmd} | conditional | flops 2735472640 | bytes 96310840 | solution.py:177
  536.1 38.4 %conditional.5 = (f32[1,512,16,64]{1,3,2,0:T(8,128)S(1)}, f32[1,1,512,16,64]{2,4,3,1,0:T(8,128)}, f32[1,1,512,16,64]{2,4,3,1,0:T(8,128)}) conditional(s32[]{:T(128)} %convert_element_type.359, (bf16[4,1,512,16,64]{2,4,3,1,0:T(8,128)(2,1)}, s32[]{:T(128)}, s32[512]{0:T(512)S(1)}, s32[1,512]{1,0:T(1,128)S(1)}, ...), branch_computations={%region_14.14_spmd, %region_15.15_spmd} | conditional | flops 2735472640 | bytes 96310840 | solution.py:177
  628.2 14.6 %fusion.84 = f32[512,4096]{1,0:T(8,128)} fusion(bf16[2048,4096]{1,0:T(8,128)(2,1)} %all-gather.19.cloned.1.call-done, bf16[1,512,2048]{2,1,0:T(8,128)(2,1)S(1)} %copy-done.27), kind=kOutput, calls=%fused_computation.118 | convolution fusion | flops 8589934592 | bytes 27262976 | tf_op jit(solution)/shard_map/dot_general | solution.py:241
  642.8 21.0 %convert_reduce_fusion = (f32[4096]{0:T(1024)}, bf16[512,4096]{1,0:T(8,128)(2,1)}) fusion(f32[512,4096]{1,0:T(8,128)} %fusion.84, f32[4096]{0:T(1024)S(1)} %convert_element_type.243, bf16[4096,2048]{1,0:T(8,128)(2,1)} %all-gather.21.cloned.1.call-done, bf16[1,512,2048]{2,1,0:T(8,128)(2,1)} %all-gather.23.cloned.1.call-done), kind=kOutput, calls=%fused_computation.71 | convolution fusion | flops 8638164992 | bytes 31490048 | tf_op jit(solution)/shard_map/nf,cf->nc/dot_general | solution.py:291
  667.1 21.0 %reduce-scatter.16.cloned.1.call-done = bf16[1,512,1024]{1,2,0:T(8,128)(2,1)} async-done(((bf16[1,2048,1024]{1,2,0:T(8,128)(2,1)}), bf16[1,512,1024]{1,2,0:T(8,128)(2,1)}) %reduce-scatter.16.cloned.1.call-update) | async-done | bytes 1048592 | tf_op jit(solution)/shard_map/reduce_scatter | solution.py:308
  700.5 15.3 %fusion.59 = bf16[1,512,2048]{2,1,0:T(8,128)(2,1)} fusion(f32[512,2048]{1,0:T(8,128)S(1)} %fusion.96, bf16[512,4096]{1,0:T(8,128)(2,1)} %get-tuple-element.560, bf16[2048,4096]{1,0:T(8,128)(2,1)} %all-gather.19.cloned.1.call-done), kind=kOutput, calls=%fused_computation.90 | convolution fusion | flops 8592031744 | bytes 27262976 | tf_op jit(solution)/shard_map/nc,fc->nf/dot_general | solution.py:349
  720.5 18.5 %fusion.58 = bf16[1,512,2048]{2,1,0:T(8,128)(2,1)} fusion(f32[512,2048]{1,0:T(8,128)S(1)} %fusion.95, bf16[4096,2048]{1,0:T(8,128)(2,1)} %all-gather.21.cloned.1.call-done, f32[512,4096]{1,0:T(8,128)} %fusion.84, f32[4096]{0:T(1024)S(1)} %convert_element_type.243), kind=kOutput, calls=%fused_computation.89 | convolution fusion | flops 8613003264 | bytes 31473664 | tf_op jit(solution)/shard_map/dot_general | solution.py:264
  739.1 19.5 %convolution_convert_fusion = bf16[4096,2048]{1,0:T(8,128)(2,1)} fusion(bf16[1,512,2048]{2,1,0:T(8,128)(2,1)S(1)} %copy-done.30, f32[512,4096]{1,0:T(8,128)} %fusion.84, f32[4096]{0:T(1024)S(1)} %convert_element_type.243), kind=kOutput, calls=%fused_computation.59 | convolution fusion | flops 8619294720 | bytes 27279360 | tf_op jit(solution)/shard_map/nc,nf->cf/dot_general | solution.py:278
  758.6 21.5 %copy.70 = bf16[4096,2048]{0,1:T(8,128)(2,1)} copy(bf16[4096,2048]{1,0:T(8,128)(2,1)} %convolution_convert_fusion) | data formatting | bytes 33554432
  780.2 15.3 %convolution_convert_fusion.1 = bf16[2048,4096]{1,0:T(8,128)(2,1)} fusion(bf16[512,4096]{1,0:T(8,128)(2,1)} %get-tuple-element.560, bf16[1,512,2048]{2,1,0:T(8,128)(2,1)} %all-gather.9.cloned.1.call-done), kind=kOutput, calls=%fused_computation.60 | convolution fusion | flops 8598323200 | bytes 23068672 | tf_op jit(solution)/shard_map/nc,nf->cf/dot_general | solution.py:335
  805.3 20.7 %pad_maximum_fusion = bf16[2048,7168]{1,0:T(8,128)(2,1)} fusion(bf16[2048,4096]{1,0:T(8,128)(2,1)} %convolution_convert_fusion.1, bf16[2048,3072]{1,0:T(8,128)(2,1)} %convolution_convert_fusion.2), kind=kLoop, calls=%fused_computation.58 | loop fusion | flops 58720256 | bytes 58720256 | tf_op jit(solution)/shard_map/concatenate | solution.py:332
  828.9 61.5 %all-reduce.1 = (f32[3,1024]{1,0:T(4,128)}, f32[4096]{0:T(1024)}) all-reduce(f32[3,1024]{1,0:T(4,128)S(1)} %reshape.634, f32[4096]{0:T(1024)S(1)} %copy-done.20), channel_id=1, replica_groups=mesh['fsdp'=4,'ctx'=4,'tp'=2] {'fsdp','ctx'}, use_global_device_ids=true, to_apply=%region_28.29 | all-reduce | flops 7168 | bytes 57344 | tf_op jit(solution)/shard_map/psum | solution.py:330
  897.4 39.8 %all-reduce = (f32[2048]{0:T(1024)}, f32[2048]{0:T(1024)}, f32[2048]{0:T(1024)S(1)}) all-reduce(f32[2048]{0:T(1024)S(1)} %get-tuple-element.468, f32[2048]{0:T(1024)S(1)} %get-tuple-element.471, f32[2048]{0:T(1024)S(1)} %get-tuple-element.549), channel_id=1, replica_groups=mesh['fsdp'=4,'ctx'=4,'tp'=2] {'fsdp','ctx','tp'}, use_global_device_ids=true, to_apply=%region_23.24 | all-reduce | flops 6144 | bytes 49152 | tf_op jit(solution)/shard_map/psum | solution.py:367
  937.2 79.6 %reduce-scatter.24.cloned.1.call-done = bf16[128,4096]{1,0:T(8,128)(2,1)} async-done(((bf16[2048,4096]{1,0:T(8,128)(2,1)}), bf16[128,4096]{1,0:T(8,128)(2,1)}) %reduce-scatter.24.cloned.1.call-update) | async-done | bytes 1048592
  1019.9 278.2 %reduce-scatter.20.cloned.1.call-done = bf16[128,7168]{1,0:T(8,128)(2,1)} async-done(((bf16[2048,7168]{1,0:T(8,128)(2,1)}), bf16[128,7168]{1,0:T(8,128)(2,1)}) %reduce-scatter.20.cloned.1.call-update) | async-done | bytes 1835024 | tf_op jit(solution)/shard_map/reduce_scatter | solution.py:331
  (244 shorter events, 472.4 us)
Async XLA Ops:
  7.2 43.9 %all-gather.9.cloned.1.call-start = ((), (), s32[]{:S(2)}) async-start(), calls=%async_computation.7 | async-start | bytes 3145728 | tf_op jit(solution)/shard_map/all_gather | solution.py:231
  15.1 142.7 %all-gather.11.cloned.1.call-start = ((), (), s32[]{:S(2)}) async-start(), calls=%async_computation.8 | async-start | bytes 13369344 | tf_op jit(solution)/shard_map/all_gather | solution.py:233
  16.3 174.3 %all-gather.23.cloned.1.call-start = ((), (), s32[]{:S(2)}) async-start(), calls=%async_computation.15 | async-start | bytes 3145728 | tf_op jit(solution)/shard_map/all_gather | solution.py:274
  17.1 228.8 %all-gather.17.cloned.1.call-start = ((), (), s32[]{:S(2)}) async-start(), calls=%async_computation.11 | async-start | bytes 4456448 | tf_op jit(solution)/shard_map/all_gather | solution.py:261
  17.6 262.9 %all-gather.13.cloned.1.call-start = ((), (), s32[]{:S(2)}) async-start(), calls=%async_computation.9 | async-start | bytes 5242880 | tf_op jit(solution)/shard_map/all_gather | solution.py:248
  18.6 160.6 %copy-start.11 = (f32[512,16]{0,1:T(8,128)}, f32[512,16]{0,1:T(8,128)S(1)}, u32[]{:S(2)}) copy-start(f32[512,16]{0,1:T(8,128)S(1)} %get-tuple-element.558) | copy-start | bytes 98308
  181.4 135.7 %all-gather.15.cloned.1.call-start = ((), (), s32[]{:S(2)}) async-start(), calls=%async_computation.10 | async-start | bytes 5242880 | tf_op jit(solution)/shard_map/all_gather | solution.py:251
  184.2 442.6 %all-gather.19.cloned.1.call-start = ((), (), s32[]{:S(2)}) async-start(), calls=%async_computation.12 | async-start | bytes 17825792 | tf_op jit(solution)/shard_map/all_gather | solution.py:234
  184.9 457.9 %all-gather.21.cloned.1.call-start = ((), (), s32[]{:S(2)}) async-start(), calls=%async_computation.13 | async-start | bytes 17825792 | tf_op jit(solution)/shard_map/all_gather | solution.py:262
  185.7 478.2 %reduce-scatter.14.cloned.1.call-start = ((), (), s32[]{:S(2)}) async-start(), calls=%async_computation.16 | async-start | bytes 5242880 | tf_op jit(solution)/shard_map/reduce_scatter | solution.py:302
  596.9 91.2 %reduce-scatter.16.cloned.1.call-start = ((), (), s32[]{:S(2)}) async-start(), calls=%async_computation.17 | async-start | bytes 5242880 | tf_op jit(solution)/shard_map/reduce_scatter | solution.py:308
  612.7 214.0 %reduce-scatter.22.cloned.1.call-start = ((), (), s32[]{:S(2)}) async-start(), calls=%async_computation.20 | async-start | bytes 4456448
  626.7 263.7 %reduce-scatter.18.cloned.1.call-start = ((), (), s32[]{:S(2)}) async-start(), calls=%async_computation.18 | async-start | bytes 3145728 | tf_op jit(solution)/shard_map/reduce_scatter | solution.py:350
  715.8 176.9 %reduce-scatter.12.cloned.1.call-start = ((), (), s32[]{:S(2)}) async-start(), calls=%async_computation.14 | async-start | bytes 3145728 | tf_op jit(solution)/shard_map/reduce_scatter | solution.py:267
  720.5 18.6 %copy-start.30 = (bf16[1,512,2048]{2,1,0:T(8,128)(2,1)S(1)}, bf16[1,512,2048]{2,1,0:T(8,128)(2,1)}, u32[]{:S(2)}) copy-start(bf16[1,512,2048]{2,1,0:T(8,128)(2,1)} %all-gather.23.cloned.1.call-done) | copy-start | bytes 6291460
  739.1 277.7 %reduce-scatter.24.cloned.1.call-start = ((), (), s32[]{:S(2)}) async-start(), calls=%async_computation.21 | async-start | bytes 17825792
  780.2 15.4 %copy-start.8 = (bf16[1,512,3,16,64]{1,4,3,2,0:T(8,128)(2,1)S(1)}, bf16[1,512,3,16,64]{1,4,3,2,0:T(8,128)(2,1)}, u32[]{:S(2)}) copy-start(bf16[1,512,3,16,64]{1,4,3,2,0:T(8,128)(2,1)} %copy-done.7) | copy-start | bytes 9437188
  780.2 517.9 %reduce-scatter.20.cloned.1.call-start = ((), (), s32[]{:S(2)}) async-start(), calls=%async_computation.19 | async-start | bytes 31195136 | tf_op jit(solution)/shard_map/reduce_scatter | solution.py:331
  826.0 64.3 %copy-start = (bf16[1,256,2048]{2,1,0:T(8,128)(2,1)S(1)}, bf16[1,256,2048]{2,1,0:T(8,128)(2,1)}, u32[]{:S(2)}) copy-start(bf16[1,256,2048]{2,1,0:T(8,128)(2,1)} %param.21) | copy-start | bytes 3145732
  826.1 64.3 %copy-start.14 = (f32[2048]{0:T(1024)S(1)}, f32[2048]{0:T(1024)}, u32[]{:S(2)}) copy-start(f32[2048]{0:T(1024)} %copy-done.13) | copy-start | bytes 24580
  826.1 64.3 %copy-start.17 = (f32[256]{0:T(256)S(1)}, f32[256]{0:T(256)}, u32[]{:S(2)}) copy-start(f32[256]{0:T(256)} %copy-done.16) | copy-start | bytes 3076
  826.1 64.3 %copy-start.19 = (f32[256]{0:T(256)S(1)}, f32[256]{0:T(256)}, u32[]{:S(2)}) copy-start(f32[256]{0:T(256)} %copy-done.18) | copy-start | bytes 3076
  826.7 66.0 %copy-start.5 = (bf16[1,256,2048]{2,1,0:T(8,128)(2,1)S(1)}, bf16[1,256,2048]{2,1,0:T(8,128)(2,1)}, u32[]{:S(2)}) copy-start(bf16[1,256,2048]{2,1,0:T(8,128)(2,1)} %param.23) | copy-start | bytes 3145732
  937.2 368.5 %copy-start.24 = (f32[2048]{0:T(1024)}, f32[2048]{0:T(1024)S(1)}, u32[]{:S(2)}) copy-start(f32[2048]{0:T(1024)S(1)} %get-tuple-element.837) | copy-start | bytes 24580
  (25 other events, 126.0 us)
Sparse Core Ops, SparseCore 0:
  15.2 35.8 all-gather.8
  53.8 103.9 all-gather.10
  159.3 31.2 all-gather.22
  192.7 53.2 all-gather.16
  247.9 32.6 all-gather.12
  282.6 34.4 all-gather.14
  319.3 126.8 all-gather.18
  448.3 128.5 all-gather.20
  597.0 43.9 reduce-scatter.13
  643.5 44.5 reduce-scatter.15
  691.9 72.4 reduce-scatter.21
  767.2 30.8 reduce-scatter.17
  800.9 31.8 reduce-scatter.11
  837.3 179.4 reduce-scatter.23
  1021.3 276.7 reduce-scatter.19
where the time goes:
time: 1320 us; the launch traced here: 1310 us
  waiting for transfers between devices  630 us (48%)
  matrix products  344 us (26%)
  local copies, waits for them, and re-layouts  135 us (10%)
  blocking collectives  101 us (8%)
  other arithmetic  76 us (6%)
  between operations  14.7 us (1%)
    reduce_scatter x1, waiting for transfers between devices, on_device(): lax.psum_scatter(jnp.concatenate([jnp.einsum('nc,nf->cf', normed_flat, qk...  278 us
    all_gather x1, waiting for transfers between devices, on_device(): lax.all_gather(qkv_weight, ('fsdp', 'ctx'), axis=0, tiled=True)  107 us
    unnamed x17, waiting for transfers between devices  82.4 us
    psum x1, blocking collectives, on_device(): lax.psum((bias_parts[0], bias_parts[1]), ('fsdp', 'ctx'))  61.5 us
    all_gather x1, waiting for transfers between devices, on_device(): lax.all_gather(out_weight, ('fsdp', 'ctx'), axis=1, tiled=True)  55.3 us
    dot_general x8, matrix products, tile_scores(): jnp.einsum('sqhd,skhd->shqk', query_block, key_block, preferred_element_t...  54.9 us
    dot_general x4, matrix products, attention_compute(): jnp.einsum('shqk,sqhd->skhd', probabilities.astype(jnp.bfloat16), grad_bl...  46.8 us
    dot_general x4, matrix products, tile_grads(): jnp.einsum('sqhd,skhd->shqk', grad_block, value_block, preferred_element_...  40.4 us
  transfers between devices with their start and end apart: 15, of which 9 were waited for; matrix products, arithmetic and copies ran while one was open for 41% of the time, Pallas kernels for 0%

commit v1 on v0

v1 whole, which is shorter than its diff:
```python
import functools

import jax
import jax.numpy as jnp
from jax import lax
from jax.experimental import pallas as pl
from jax.experimental.pallas import tpu as pltpu
from jax.sharding import PartitionSpec as P

D = 2048
HEAD_DIM = 64
ROT = 32
GROUP = 256
PAIR = 2 * HEAD_DIM

EPSILON = 1e-05
MASKED = -1e30
GELU_SLOPE = 0.7978845608028654
GELU_CUBE = 0.044715

NT = (((1,), (1,)), ((), ()))
NN = (((1,), (0,)), ((), ()))


def dot(left, right, dims=NN):
    return lax.dot_general(left, right, dims, preferred_element_type=jnp.float32)


def turning(places):
    halfway = ROT // 2
    frequencies = 10000.0 ** (-(jnp.arange(halfway, dtype=jnp.float32) * 2.0 / ROT))
    angles = places.astype(jnp.float32)[:, None] * frequencies[None, :]
    cosine, sine = jnp.cos(angles), jnp.sin(angles)
    rest = jnp.ones((places.shape[0], HEAD_DIM - ROT), jnp.float32)
    cosine_table = jnp.concatenate([cosine, cosine, rest] * 2, axis=1)
    sine_table = jnp.concatenate([-sine, sine, 0.0 * rest] * 2, axis=1)
    return cosine_table, sine_table


def turn(values, cosine, sine):
    halfway = ROT // 2
    lane = lax.broadcasted_iota(jnp.int32, values.shape, 1) % HEAD_DIM
    partner = jnp.where(
        lane < halfway,
        pltpu.roll(values, PAIR - halfway, 1),
        pltpu.roll(values, halfway, 1),
    )
    return values * cosine + partner * sine


def attention_kernel(
    order,
    query_in,
    key_in,
    value_in,
    grad_in,
    cosine_all,
    sine_all,
    attended_out,
    query_out,
    key_out,
    value_out,
    keys,
    values,
    keys_turned,
    values_turned,
    key_total,
    value_total,
    strip,
):
    groups = pl.num_programs(1)
    group = pl.program_id(1)
    scale = HEAD_DIM ** (-0.5)

    def rows(index):
        return pl.ds(pl.multiple_of(index * GROUP, GROUP), GROUP)

    @pl.when(group == 0)
    def _():
        def sort(place, carry):
            source, target = rows(order[place]), rows(place)
            key = turn(key_in[source, :], cosine_all[source, :], sine_all[source, :])
            value = value_in[source, :]
            keys[target, :] = key.astype(jnp.bfloat16)
            values[target, :] = value.astype(jnp.bfloat16)
            keys_turned[place] = key.T.astype(jnp.bfloat16)
            values_turned[place] = value.T.astype(jnp.bfloat16)
            key_total[target, :] = jnp.zeros((GROUP, PAIR), jnp.float32)
            value_total[target, :] = jnp.zeros((GROUP, PAIR), jnp.float32)
            return carry

        lax.fori_loop(0, groups, sort, 0)

    own = rows(order[group])
    cosine, sine = cosine_all[own, :], sine_all[own, :]
    query = turn(query_in[...], cosine, sine).astype(jnp.bfloat16)
    query = (query.astype(jnp.float32) * scale).astype(jnp.bfloat16)
    grad = grad_in[...]
    first = lax.broadcasted_iota(jnp.int32, (GROUP, PAIR), 1) < HEAD_DIM
    nothing = jnp.zeros((GROUP, PAIR), jnp.bfloat16)
    query_pair = jnp.concatenate(
        [jnp.where(first, query, nothing), jnp.where(first, nothing, query)], axis=0
    )
    grad_pair = jnp.concatenate(
        [jnp.where(first, grad, nothing), jnp.where(first, nothing, grad)], axis=0
    )
    wide = 2 * GROUP

    def fold(tile):
        return tile.reshape(GROUP // 8, 8, wide)

    def score(place):
        return dot(keys[rows(place), :], query_pair, NT)

    def scores(place, most):
        tile = score(place)
        strip[place] = tile
        return jnp.maximum(most, jnp.max(fold(tile), axis=0))

    most = lax.fori_loop(0, group, scores, jnp.full((8, wide), MASKED, jnp.float32))
    key_row = lax.broadcasted_iota(jnp.int32, (GROUP, wide), 0)
    query_lane = lax.broadcasted_iota(jnp.int32, (GROUP, wide), 1) % GROUP
    tile = jnp.where(key_row <= query_lane, score(group), MASKED)
    strip[group] = tile
    most = jnp.max(jnp.maximum(most, jnp.max(fold(tile), axis=0)), axis=0, keepdims=True)

    def weigh(place, carry):
        total, upper, lower = carry
        tile = jnp.exp(strip[place] - most)
        strip[place] = tile
        low = tile.astype(jnp.bfloat16)
        upper = upper + dot(values_turned[place, :HEAD_DIM, :], low[:, :GROUP])
        lower = lower + dot(values_turned[place, HEAD_DIM:, :], low[:, GROUP:])
        return total + jnp.sum(fold(tile), axis=0), upper, lower

    blank = jnp.zeros((HEAD_DIM, GROUP), jnp.float32)
    total, upper, lower = lax.fori_loop(
        0, group + 1, weigh, (jnp.zeros((8, wide), jnp.float32), blank, blank)
    )
    share = 1.0 / jnp.sum(total, axis=0, keepdims=True)
    upper = upper * share[:, :GROUP]
    lower = lower * share[:, GROUP:]
    attended_out[...] = jnp.concatenate([upper, lower], axis=0).T.astype(jnp.bfloat16)
    grad_turned = grad.astype(jnp.float32).T
    delta = jnp.concatenate(
        [
            jnp.sum(upper * grad_turned[:HEAD_DIM], axis=0, keepdims=True),
            jnp.sum(lower * grad_turned[HEAD_DIM:], axis=0, keepdims=True),
        ],
        axis=1,
    )

    def back(place, carry):
        upper, lower = carry
        here = rows(place)
        part = strip[place] * share
        value_total[here, :] += dot(part.astype(jnp.bfloat16), grad_pair)
        part = part * (dot(values[here, :], grad_pair, NT) - delta)
        low = part.astype(jnp.bfloat16)
        key_total[here, :] += dot(low, query_pair)
        upper = upper + dot(keys_turned[place, :HEAD_DIM, :], low[:, :GROUP])
        lower = lower + dot(keys_turned[place, HEAD_DIM:, :], low[:, GROUP:])
        return upper, lower

    upper, lower = lax.fori_loop(0, group + 1, back, (blank, blank))
    query_grad = jnp.concatenate([upper, lower], axis=0).T * scale
    query_out[...] = turn(query_grad, cosine, -sine).astype(jnp.bfloat16)

    @pl.when(group == groups - 1)
    def _():
        def unsort(place, carry):
            source, target = rows(place), rows(order[place])
            key_grad = turn(key_total[source, :], cosine_all[target, :], -sine_all[target, :])
            key_out[target, :] = key_grad.astype(jnp.bfloat16)
            value_out[target, :] = value_total[source, :].astype(jnp.bfloat16)
            return carry

        lax.fori_loop(0, groups, unsort, 0)


def attention(order, mixed, out_grads, cosine_table, sine_table):
    length = mixed.shape[0]
    width = out_grads.shape[1]
    pairs = width // PAIR
    groups = length // GROUP
    mixed = mixed.reshape(length, 3 * width)

    def block(which):
        return pl.BlockSpec((GROUP, PAIR), lambda pair, group, order: (order[group], which * pairs + pair))

    def column(which):
        return pl.BlockSpec((length, PAIR), lambda pair, group, order: (0, which * pairs + pair))

    table = pl.BlockSpec((length, PAIR), lambda pair, group, order: (0, 0))
    shape = jax.ShapeDtypeStruct((length, width), jnp.bfloat16)
    tiles = groups * (groups + 1) // 2 * pairs * 2 * GROUP * GROUP
    return pl.pallas_call(
        attention_kernel,
        grid_spec=pltpu.PrefetchScalarGridSpec(
            num_scalar_prefetch=1,
            grid=(pairs, groups),
            in_specs=[block(0), column(1), column(2), block(0), table, table],
            out_specs=[block(0), block(0), column(0), column(0)],
            scratch_shapes=[
                pltpu.VMEM((length, PAIR), jnp.bfloat16),
                pltpu.VMEM((length, PAIR), jnp.bfloat16),
                pltpu.VMEM((groups, PAIR, GROUP), jnp.bfloat16),
                pltpu.VMEM((groups, PAIR, GROUP), jnp.bfloat16),
                pltpu.VMEM((length, PAIR), jnp.float32),
                pltpu.VMEM((length, PAIR), jnp.float32),
                pltpu.VMEM((groups, GROUP, 2 * GROUP), jnp.float32),
            ],
        ),
        out_shape=[shape] * 4,
        compiler_params=pltpu.CompilerParams(
            dimension_semantics=("arbitrary", "arbitrary"), vmem_limit_bytes=40 * 1024 * 1024
        ),
        cost_estimate=pl.CostEstimate(
            flops=tiles * 6 * 2 * 256, bytes_accessed=length * width * 22, transcendentals=tiles
        ),
    )(order, mixed, mixed, mixed, out_grads, cosine_table, sine_table)


def swap(values, axis, bit):
    size = lax.axis_size(axis)
    return lax.ppermute(values, axis, [(place, place ^ bit) for place in range(size)])


def total(values, axes):
    for axis in axes:
        bit = 1
        while bit < lax.axis_size(axis):
            values = values + swap(values, axis, bit)
            bit *= 2
    return values


def paired():
    return lax.axis_size("ctx") == 4 and lax.axis_size("tp") == 2


def gather_rows(own):
    if not paired():
        return lax.all_gather(own, ("ctx", "tp"), axis=0, tiled=True)
    half = own.shape[0] // 2
    across = swap(own, "tp", 1)
    along = swap(own, "ctx", 2)
    corner = jnp.concatenate([swap(across[:half], "ctx", 2), swap(along[half:], "tp", 1)], axis=0)
    near = [own, across, along, corner]
    return jnp.concatenate(near + [swap(part, "ctx", 1) for part in near], axis=0)


def scatter_rows(parts):
    if not paired():
        return lax.psum_scatter(parts, ("ctx", "tp"), scatter_dimension=0, tiled=True).astype(
            jnp.float32
        )
    size = parts.shape[0] // 8
    half = size // 2

    def add(left, right):
        return left.astype(jnp.float32) + right.astype(jnp.float32)

    def block(index):
        return parts[index * size : (index + 1) * size]

    own, across, along, corner = [
        add(block(index), swap(block(4 + index), "ctx", 1)) for index in range(4)
    ]
    corner = corner.astype(jnp.bfloat16)
    from_across = swap(corner[:half], "tp", 1)
    from_along = swap(corner[half:], "ctx", 2)
    along = jnp.concatenate([add(along[:half], from_across), along[half:]], axis=0)
    across = jnp.concatenate([across[:half], add(across[half:], from_along)], axis=0)
    return add(
        add(own, swap(across.astype(jnp.bfloat16), "tp", 1)),
        swap(along.astype(jnp.bfloat16), "ctx", 2),
    )


def local_places(positions):
    if not paired():
        return positions
    devices = jnp.array([2 * along + near for near in (0, 1) for along in (0, 1) for _ in (0, 1)])
    blocks = (lax.axis_index("ctx") ^ devices) * 2 + (
        lax.axis_index("tp") ^ jnp.array([0, 1] * 4)
    )
    return positions.reshape(8, -1)[blocks].reshape(-1)


def spread(own):
    size, place = lax.axis_size("fsdp"), lax.axis_index("fsdp")
    result = jnp.zeros((size,) + own.shape, own.dtype)
    result = lax.dynamic_update_index_in_dim(result, own, place, 0)
    upward = downward = own
    for step in range(1, size):
        upward = lax.ppermute(upward, "fsdp", [(j, j + 1) for j in range(step - 1, size - 1)])
        downward = lax.ppermute(downward, "fsdp", [(j, j - 1) for j in range(1, size - step + 1)])
        for there, source, block in (
            (place >= step, place - step, upward),
            (place < size - step, place + step, downward),
        ):
            result = lax.dynamic_update_index_in_dim(
                result, jnp.where(there, block, own), jnp.where(there, source, place), 0
            )
    return result


def collapse(parts):
    size, place = lax.axis_size("fsdp"), lax.axis_index("fsdp")

    def block(index):
        return lax.dynamic_index_in_dim(parts, jnp.clip(index, 0, size - 1), 0, keepdims=False)

    def add(left, right):
        return left if right is None else left.astype(jnp.float32) + right.astype(jnp.float32)

    upward = downward = None
    for step in range(1, size):
        send = add(block(size - step + place), upward).astype(jnp.bfloat16)
        upward = lax.ppermute(send, "fsdp", [(j, j + 1) for j in range(step)])
        send = add(block(place + step - size), downward).astype(jnp.bfloat16)
        downward = lax.ppermute(send, "fsdp", [(j, j - 1) for j in range(size - step, size)])
    return add(add(block(place), upward), downward)


def gather_weight(shard):
    width = shard.shape[2] // lax.axis_size("ctx")
    mine = lax.all_to_all(shard, "ctx", 2, 0, tiled=True)
    return spread(mine.reshape(mine.shape[0], -1)).reshape(-1, shard.shape[1] * width)


def scatter_grad(grad, parts):
    size = lax.axis_size("fsdp")
    mine = collapse(grad.reshape(size, -1, grad.shape[1])).astype(jnp.bfloat16)
    mine = mine.reshape(mine.shape[0], parts, -1)
    return lax.all_to_all(mine, "ctx", 0, 2, tiled=True).astype(jnp.float32)


def on_device(
    tokens,
    positions,
    cotangent,
    norm_gain,
    norm_bias,
    qkv_weight,
    qkv_bias,
    out_weight,
    out_bias,
    up_weight,
    up_bias,
    down_weight,
    down_bias,
):
    parts = lax.axis_size("ctx")
    part = lax.axis_index("ctx")
    width = qkv_weight.shape[2] // parts
    units = up_weight.shape[1] // parts

    inputs = tokens[0].astype(jnp.float32)
    row_mean = jnp.mean(inputs, axis=-1, keepdims=True)
    centered = inputs - row_mean
    inverse = lax.rsqrt(jnp.mean(centered * centered, axis=-1, keepdims=True) + EPSILON)
    unit_rows = centered * inverse
    normed_own = (unit_rows * norm_gain + norm_bias).astype(jnp.bfloat16)

    attention_shard = jnp.concatenate([qkv_weight, out_weight.T[:, None, :]], axis=1)
    attention_weight = gather_weight(attention_shard)
    normed = gather_rows(normed_own)
    up_full = gather_weight(up_weight[:, None, :])
    grads = gather_rows(cotangent[0])
    down_full = gather_weight(down_weight.T[:, None, :])

    qkv_full = attention_weight[:, : 3 * width]
    out_full = attention_weight[:, 3 * width :]
    bias = lax.dynamic_slice_in_dim(qkv_bias, part * width, width, 1).reshape(3 * width)
    mixed = dot(normed, qkv_full) + bias
    out_grads = dot(grads, out_full).astype(jnp.bfloat16)
    places = local_places(positions)
    groups = places[::GROUP] // GROUP
    order = jnp.sum(
        jnp.where(
            groups[None, :] == jnp.arange(groups.shape[0])[:, None],
            jnp.arange(groups.shape[0])[None, :],
            0,
        ),
        axis=1,
    ).astype(jnp.int32)
    cosine_table, sine_table = turning(places)
    mixed = mixed.reshape(-1, 3, width)
    short = -width % PAIR
    attended, *head_grads = attention(
        order,
        jnp.pad(mixed, ((0, 0), (0, 0), (0, short))),
        jnp.pad(out_grads, ((0, 0), (0, short))),
        cosine_table,
        sine_table,
    )
    attended = attended[:, :width]
    qkv_grad = jnp.concatenate([item[:, :width] for item in head_grads], axis=1)

    own_bias = lax.dynamic_slice_in_dim(up_bias, part * units, units, 0)
    hidden = dot(normed, up_full) + own_bias
    bent = jnp.tanh(GELU_SLOPE * (hidden + GELU_CUBE * hidden * hidden * hidden))
    activated = (0.5 * hidden * (1.0 + bent)).astype(jnp.bfloat16)
    slope = 0.5 * (1.0 + bent) + 0.5 * hidden * (1.0 - bent * bent) * GELU_SLOPE * (
        1.0 + 3.0 * GELU_CUBE * hidden * hidden
    )
    hidden_grad = (dot(grads, down_full, NN) * slope).astype(jnp.bfloat16)

    branch = dot(attended, out_full, NT) + dot(activated, down_full, NT)
    branch_sum = scatter_rows(branch.astype(jnp.bfloat16))
    layer_output = (inputs + branch_sum + out_bias + down_bias).astype(jnp.bfloat16)

    def across(left, right):
        return dot(left, right, (((0,), (0,)), ((), ()))).astype(jnp.bfloat16)

    attention_grad = scatter_grad(
        jnp.concatenate([across(normed, qkv_grad), across(grads, attended)], axis=1), 4
    )
    down_grad = scatter_grad(across(grads, activated), 1)
    up_grad = scatter_grad(across(normed, hidden_grad), 1)

    normed_part = dot(qkv_grad, qkv_full, NT) + dot(hidden_grad, up_full, NT)
    normed_back = scatter_rows(normed_part.astype(jnp.bfloat16))
    unit_grad = normed_back * norm_gain
    tokens_grad = cotangent[0].astype(jnp.float32) + inverse * (
        unit_grad
        - jnp.mean(unit_grad, axis=-1, keepdims=True)
        - unit_rows * jnp.mean(unit_grad * unit_rows, axis=-1, keepdims=True)
    )

    qkv_sums = jnp.sum(qkv_grad, axis=0, dtype=jnp.float32).reshape(3, width)
    up_sums = jnp.sum(hidden_grad, axis=0, dtype=jnp.float32)
    bias_sums = jnp.concatenate(
        [
            lax.dynamic_update_slice_in_dim(
                jnp.zeros(qkv_bias.shape, jnp.float32), qkv_sums, part * width, 1
            ).reshape(-1),
            lax.dynamic_update_slice_in_dim(
                jnp.zeros(up_bias.shape, jnp.float32), up_sums, part * units, 0
            ),
        ]
    )
    bias_sums = total(bias_sums, ("fsdp", "ctx"))
    norm_sums = total(
        jnp.stack(
            [
                jnp.sum(normed_back * unit_rows, axis=0),
                jnp.sum(normed_back, axis=0),
                jnp.sum(cotangent[0], axis=0, dtype=jnp.float32),
            ]
        ),
        ("ctx", "tp", "fsdp"),
    )
    return (
        layer_output[None],
        tokens_grad[None],
        norm_sums[0],
        norm_sums[1],
        attention_grad[:, :3],
        bias_sums[: qkv_bias.size].reshape(qkv_bias.shape),
        attention_grad[:, 3].T,
        norm_sums[2],
        up_grad[:, 0],
        bias_sums[qkv_bias.size :],
        down_grad[:, 0].T,
        norm_sums[2],
    )


def solution(mesh):
    rows = P("fsdp", ("ctx", "tp"), None)
    placed = (
        rows,
        P(),
        rows,
        P(),
        P(),
        P(("fsdp", "ctx"), None, "tp"),
        P(None, "tp"),
        P("tp", ("fsdp", "ctx")),
        P(),
        P(("fsdp", "ctx"), "tp"),
        P("tp"),
        P("tp", ("fsdp", "ctx")),
        P(),
    )
    return jax.shard_map(
        on_device,
        mesh=mesh,
        in_specs=placed,
        out_specs=(
            rows,
            rows,
            P(),
            P(),
            P(("fsdp", "ctx"), None, "tp"),
            P(None, "tp"),
            P("tp", ("fsdp", "ctx")),
            P(),
            P(("fsdp", "ctx"), "tp"),
            P("tp"),
            P("tp", ("fsdp", "ctx")),
            P(),
        ),
        check_vma=False,
    )
```

time: 1320 us -> 982 us (0.74)
  waiting for transfers between devices: 630 us -> 300 us
  matrix products: 344 us -> 131 us
  starting transfers between devices: 0.79 us -> 202 us
  blocking collectives: 101 us -> 0 us
  Pallas kernels: 0 us -> 82.4 us
  other arithmetic: 76 us -> 124 us
    reduce_scatter x5 -> x0, waiting for transfers between devices: 299 us -> none  [the longest x1 278 us: on_device(): lax.psum_scatter(jnp.concatenate([jnp.einsum('nc,nf->cf', normed_flat, qk...]
    ppermute x0 -> x77, waiting for transfers between devices: none -> 296 us  [the longest x9 94.6 us: spread(): lax.ppermute(downward, 'fsdp', [(j, j - 1) for j in range(1, size - step...]
    all_gather x8 -> x0, waiting for transfers between devices: 249 us -> none  [the longest x1 107 us: on_device(): lax.all_gather(qkv_weight, ('fsdp', 'ctx'), axis=0, tiled=True)]
    dot_general x40 -> x12, matrix products: 344 us -> 131 us  [dot(): lax.dot_general(left, right, dims, preferred_element_type=jnp.float32)]
    ppermute x0 -> x77, starting transfers between devices: none -> 178 us  [the longest x9 62.5 us: collapse(): upward = lax.ppermute(send, 'fsdp', [(j, j + 1) for j in range(step)])]
    psum x2 -> x0, blocking collectives: 101 us -> none  [the longest x1 61.5 us: on_device(): lax.psum((bias_parts[0], bias_parts[1]), ('fsdp', 'ctx'))]
    pallas_call x0 -> x1, Pallas kernels: none -> 82.4 us  [attention(): pl.pallas_call(attention_kernel, grid_spec=pltpu.PrefetchScalarGridSpec(n...]
    unnamed x17 -> x0, waiting for transfers between devices: 82.4 us -> none
  transfers between devices with their start and end apart: 15 -> 83, of which waited for: 9 -> 26; matrix products, arithmetic and copies ran while one was open for 41% -> 33% of each run, Pallas kernels for 0% -> 8%
where the time goes in v1:
time: 982 us; the launch traced here: 972 us
  waiting for transfers between devices  300 us (31%)
  starting transfers between devices  202 us (21%)
  matrix products  131 us (13%)
  local copies, waits for them, and re-layouts  130 us (13%)
  other arithmetic  124 us (13%)
  Pallas kernels  82.4 us (8%)
    dot_general x12, matrix products, dot(): lax.dot_general(left, right, dims, preferred_element_type=jnp.float32)  131 us
    ppermute x9, waiting for transfers between devices, spread(): lax.ppermute(downward, 'fsdp', [(j, j - 1) for j in range(1, size - step...  94.6 us
    ppermute x9, waiting for transfers between devices, collapse(): upward = lax.ppermute(send, 'fsdp', [(j, j + 1) for j in range(step)])  90.8 us
    pallas_call x1, Pallas kernels, attention(): pl.pallas_call(attention_kernel, grid_spec=pltpu.PrefetchScalarGridSpec(n...  82.4 us
    ppermute x41, waiting for transfers between devices, swap(): lax.ppermute(values, axis, [(place, place ^ bit) for place in range(size)])  64.9 us
    ppermute x9, starting transfers between devices, collapse(): upward = lax.ppermute(send, 'fsdp', [(j, j + 1) for j in range(step)])  62.5 us
    ppermute x41, starting transfers between devices, swap(): lax.ppermute(values, axis, [(place, place ^ bit) for place in range(size)])  61.9 us
    unnamed x148, local copies, waits for them, and re-layouts  60.6 us
  transfers between devices with their start and end apart: 83, of which 26 were waited for; matrix products, arithmetic and copies ran while one was open for 33% of the time, Pallas kernels for 8%

profile of v1, /device:TPU:0, one launch (start us, length us, event | category | flops | bytes accessed | tf_op | source)
XLA Modules:
  0.0 972.3 jit_solution(7389039484726126166)
XLA Ops:
  23.9 22.4 %reduce.2 = bf16[4096,128]{1,0:T(8,128)(2,1)S(1)} reduce(bf16[4096,1,128]{2,1,0:T(2,128)(2,1)S(1)} %bitcast.279, bf16[]{:T(256)} %broadcast.123), dimensions={1}, to_apply=%bitcast.209.reduce_sub_computation | reduce | bytes 2097154
  58.2 22.4 %reduce.1 = bf16[4096,128]{1,0:T(8,128)(2,1)S(1)} reduce(bf16[4096,1,128]{2,1,0:T(2,128)(2,1)S(1)} %bitcast.283, bf16[]{:T(256)} %broadcast.123), dimensions={1}, to_apply=%bitcast.211.reduce_sub_computation | reduce | bytes 2097154
  198.0 17.6 %collective-permute-done.8 = bf16[512,1024]{1,0:T(8,128)(2,1)S(1)} collective-permute-done((bf16[512,1024]{1,0:T(8,128)(2,1)S(1)}, bf16[512,1024]{1,0:T(8,128)(2,1)S(1)}, u32[]{:S(2)}, u32[]{:S(2)}) %collective-permute-start.8) | collective-permute-done | bytes 1048608 | tf_op jit(solution)/shard_map/ppermute | solution.py:297
  217.5 19.2 %collective-permute-done.28 = bf16[512,1024]{1,0:T(8,128)(2,1)S(1)} collective-permute-done((bf16[512,1024]{1,0:T(8,128)(2,1)S(1)}, bf16[512,1024]{1,0:T(8,128)(2,1)S(1)}, u32[]{:S(2)}, u32[]{:S(2)}) %collective-permute-start.28) | collective-permute-done | bytes 1048608 | tf_op jit(solution)/shard_map/ppermute | solution.py:297
  250.6 19.7 %collective-permute-done.31 = bf16[512,1024]{1,0:T(8,128)(2,1)} collective-permute-done((bf16[512,1024]{1,0:T(8,128)(2,1)S(1)}, bf16[512,1024]{1,0:T(8,128)(2,1)}, u32[]{:S(2)}, u32[]{:S(2)}) %collective-permute-start.31) | collective-permute-done | bytes 1048608 | tf_op jit(solution)/shard_map/ppermute | solution.py:298
  272.3 20.3 %collective-permute-done.11 = bf16[512,1024]{1,0:T(8,128)(2,1)S(1)} collective-permute-done((bf16[512,1024]{1,0:T(8,128)(2,1)S(1)}, bf16[512,1024]{1,0:T(8,128)(2,1)S(1)}, u32[]{:S(2)}, u32[]{:S(2)}) %collective-permute-start.11) | collective-permute-done | bytes 1048608 | tf_op jit(solution)/shard_map/ppermute | solution.py:298
  294.4 20.9 %collective-permute-done.25 = bf16[512,1024]{1,0:T(8,128)(2,1)} collective-permute-done((bf16[512,1024]{1,0:T(8,128)(2,1)S(1)}, bf16[512,1024]{1,0:T(8,128)(2,1)}, u32[]{:S(2)}, u32[]{:S(2)}) %collective-permute-start.25) | collective-permute-done | bytes 1048608 | tf_op jit(solution)/shard_map/ppermute | solution.py:298
  326.4 33.7 %collective-permute-done.13 = bf16[512,1024]{1,0:T(8,128)(2,1)S(1)} collective-permute-done((bf16[512,1024]{1,0:T(8,128)(2,1)S(1)}, bf16[512,1024]{1,0:T(8,128)(2,1)S(1)}, u32[]{:S(2)}, u32[]{:S(2)}) %collective-permute-start.13) | collective-permute-done | bytes 1048608 | tf_op jit(solution)/shard_map/ppermute | solution.py:298
  372.4 82.4 %shard_map.238 = (bf16[2048,256]{1,0:T(8,128)(2,1)S(1)}, bf16[2048,256]{1,0:T(8,128)(2,1)S(1)}, bf16[2048,256]{1,0:T(8,128)(2,1)S(1)}, bf16[2048,256]{1,0:T(8,128)(2,1)S(1)}) custom-call(s32[8]{0:T(128)S(1)} %select_reduce_fusion.order, f32[2048,768]{1,0:T(8,128)S(1)} %broadcast_add_fusion.query_in.key_in.value_in, ...), custom_call_target="tpu_custom_call" | custom-call | flops 28991029248 | bytes 11534336 | tf_op jit(solution)/shard_map/pallas_call | solution.py:197
  455.1 10.5 %convolution_convert_fusion.2 = bf16[2048,768]{0,1:T(8,128)(2,1)} fusion(bf16[2048,2048]{1,0:T(8,128)(2,1)} %constant_dynamic-update-slice_fusion, bf16[2048,768]{1,0:T(8,128)(2,1)S(1)} %constant_dynamic-update-slice_fusion.18), kind=kOutput, calls=%fused_computation.18 | convolution fusion | flops 6444023808 | bytes 14680064 | tf_op jit(solution)/shard_map/dot_general | solution.py:26
  479.9 12.7 %fusion.67 = f32[2048,1024]{1,0:T(8,128)S(1)} fusion(bf16[2048,2048]{1,0:T(8,128)(2,1)} %constant_dynamic-update-slice_fusion, bf16[2048,1024]{1,0:T(8,128)(2,1)} %bitcast.296), kind=kOutput, calls=%fused_computation.195 | convolution fusion | flops 8589934592 | bytes 20971520 | tf_op jit(solution)/shard_map/dot_general | solution.py:26
  492.7 10.9 %convolution_convert_fusion = bf16[2048,1024]{1,0:T(8,128)(2,1)} fusion(bf16[2048,2048]{1,0:T(8,128)(2,1)S(1)} %bitcast.310, f32[2048,1024]{1,0:T(8,128)S(1)} %fusion.67, f32[1024]{0:T(1024)S(1)} %dynamic-slice_convert_fusion), kind=kOutput, calls=%fused_computation.16 | convolution fusion | flops 8613003264 | bytes 20975616 | tf_op jit(solution)/shard_map/dot_general | solution.py:26
  516.6 9.8 %fusion.54 = f32[2048,2048]{1,0:T(8,128)} fusion(bf16[2048,256]{1,0:T(8,128)(2,1)S(1)} %get-tuple-element.16, bf16[2048,1024]{1,0:T(8,128)(2,1)} %bitcast.289), kind=kOutput, calls=%fused_computation.140 | convolution fusion | flops 2147483648 | bytes 18874368 | tf_op jit(solution)/shard_map/dot_general | solution.py:26
  528.1 18.3 %convert_reduce_fusion = (f32[1024]{0:T(1024)S(1)}, bf16[2048,1024]{1,0:T(8,128)(2,1)}) fusion(f32[2048,1024]{1,0:T(8,128)S(1)} %bitcast.330, f32[1024]{0:T(1024)S(1)} %dynamic-slice_convert_fusion, bf16[2048,2048]{1,0:T(8,128)(2,1)} %copy-done.26, bf16[2048,1024]{1,0:T(8,128)(2,1)S(1)} %bitcast.294), kind=kOutput, calls=%fused_computation.12 | convolution fusion | flops 8636070912 | bytes 25174016 | tf_op jit(solution)/shard_map/dot_general | solution.py:26
  546.4 12.5 %convolution_convert_fusion.1 = bf16[2048,1024]{1,0:T(8,128)(2,1)} fusion(bf16[2048,2048]{1,0:T(8,128)(2,1)S(1)} %bitcast.312, bf16[2048,1024]{1,0:T(8,128)(2,1)} %get-tuple-element.151), kind=kOutput, calls=%fused_computation.17 | convolution fusion | flops 8592031744 | bytes 16777216 | tf_op jit(solution)/shard_map/dot_general | solution.py:26
  558.9 14.4 %add_convert_fusion = bf16[2048,2048]{1,0:T(8,128)(2,1)S(1)} fusion(f32[2048,2048]{1,0:T(8,128)} %fusion.7, bf16[2048,1024]{1,0:T(8,128)(2,1)} %get-tuple-element.151, bf16[2048,1024]{1,0:T(8,128)(2,1)} %bitcast.297), kind=kOutput, calls=%fused_computation.1 | convolution fusion | flops 8598323200 | bytes 33554432 | tf_op jit(solution)/shard_map/dot_general | solution.py:26
  578.4 18.0 %add_convert_fusion.1 = bf16[2048,2048]{1,0:T(8,128)(2,1)} fusion(f32[2048,2048]{1,0:T(8,128)} %fusion.54, bf16[2048,1024]{1,0:T(8,128)(2,1)} %bitcast.295, f32[2048,1024]{1,0:T(8,128)} %copy-done.43, f32[1024]{0:T(1024)S(1)} %dynamic-slice_convert_fusion), kind=kOutput, calls=%fused_computation.2 | convolution fusion | flops 8619294720 | bytes 37752832 | tf_op jit(solution)/shard_map/dot_general | solution.py:26
  634.7 20.0 %collective-permute-done.65 = bf16[512,1024]{1,0:T(8,128)(2,1)} collective-permute-done((bf16[512,1024]{1,0:T(8,128)(2,1)}, bf16[512,1024]{1,0:T(8,128)(2,1)}, u32[]{:S(2)}, u32[]{:S(2)}) %collective-permute-start.65) | collective-permute-done | bytes 1048608 | tf_op jit(solution)/shard_map/ppermute | solution.py:321
  657.8 19.1 %collective-permute-done.71 = bf16[512,1024]{1,0:T(8,128)(2,1)} collective-permute-done((bf16[512,1024]{1,0:T(8,128)(2,1)}, bf16[512,1024]{1,0:T(8,128)(2,1)}, u32[]{:S(2)}, u32[]{:S(2)}) %collective-permute-start.71) | collective-permute-done | bytes 1048608 | tf_op jit(solution)/shard_map/ppermute | solution.py:321
  721.6 19.5 %collective-permute-done.66 = bf16[512,1024]{1,0:T(8,128)(2,1)S(1)} collective-permute-done((bf16[512,1024]{1,0:T(8,128)(2,1)S(1)}, bf16[512,1024]{1,0:T(8,128)(2,1)S(1)}, u32[]{:S(2)}, u32[]{:S(2)}) %collective-permute-start.66) | collective-permute-done | bytes 1048608 | tf_op jit(solution)/shard_map/ppermute | solution.py:321
  742.6 19.0 %collective-permute-done.72 = bf16[512,1024]{1,0:T(8,128)(2,1)S(1)} collective-permute-done((bf16[512,1024]{1,0:T(8,128)(2,1)S(1)}, bf16[512,1024]{1,0:T(8,128)(2,1)S(1)}, u32[]{:S(2)}, u32[]{:S(2)}) %collective-permute-start.72) | collective-permute-done | bytes 1048608 | tf_op jit(solution)/shard_map/ppermute | solution.py:321
  802.0 20.5 %collective-permute-start.67 = (bf16[512,1024]{1,0:T(8,128)(2,1)}, bf16[512,1024]{1,0:T(8,128)(2,1)S(1)}, u32[]{:S(2)}, u32[]{:S(2)}) collective-permute-start(bf16[512,1024]{1,0:T(8,128)(2,1)} %get-tuple-element.129), channel_id=1, source_target_pairs={{0,8},{8,16},{16,24},{1,9},{9,17},{17,25},{2,10},{10,18},{18,26},{... | collective-permute-start | bytes 3145736 | tf_op jit(solution)/shard_map/ppermute | solution.py:321
  826.6 22.6 %collective-permute-start.73 = (bf16[512,1024]{1,0:T(8,128)(2,1)}, bf16[512,1024]{1,0:T(8,128)(2,1)}, u32[]{:S(2)}, u32[]{:S(2)}) collective-permute-start(bf16[512,1024]{1,0:T(8,128)(2,1)} %get-tuple-element.125), channel_id=1, source_target_pairs={{0,8},{8,16},{16,24},{1,9},{9,17},{17,25},{2,10},{10,18},{18,26},{... | collective-permute-start | bytes 3145736 | tf_op jit(solution)/shard_map/ppermute | solution.py:321
  880.7 19.2 %collective-permute-done.53 = f32[3,2048]{1,0:T(4,128)S(1)} collective-permute-done((f32[3,2048]{1,0:T(4,128)S(1)}, f32[3,2048]{1,0:T(4,128)S(1)}, u32[]{:S(2)}, u32[]{:S(2)}) %collective-permute-start.53) | collective-permute-done | bytes 24608 | tf_op jit(solution)/shard_map/ppermute | solution.py:226
  (450 shorter events, 463.7 us)
Async XLA Ops:
  0.7 174.4 %collective-permute-start.18 = (bf16[256,2048]{1,0:T(8,128)(2,1)}, bf16[256,2048]{1,0:T(8,128)(2,1)}, u32[]{:S(2)}, u32[]{:S(2)}) collective-permute-start(bf16[256,2048]{1,0:T(8,128)(2,1)} %bitcast.298), channel_id=1, source_target_pairs={{0,2},{2,0},{4,6},{6,4},{1,3},{3,1},{5,7},{7,5},{8,10},{10,8},{12,... | collective-permute-start | bytes 3145736 | tf_op jit(solution)/shard_map/ppermute | solution.py:226
  1.2 131.9 %collective-permute-start.15 = (bf16[256,2048]{1,0:T(8,128)(2,1)}, bf16[256,2048]{1,0:T(8,128)(2,1)}, u32[]{:S(2)}, u32[]{:S(2)}) collective-permute-start(bf16[256,2048]{1,0:T(8,128)(2,1)} %bitcast.299), channel_id=1, source_target_pairs={{0,4},{2,6},{4,0},{6,2},{1,5},{3,7},{5,1},{7,3},{8,12},{10,14},{12... | collective-permute-start | bytes 3145736 | tf_op jit(solution)/shard_map/ppermute | solution.py:226
  3.8 137.0 %collective-permute-start.14 = (bf16[256,2048]{1,0:T(8,128)(2,1)}, bf16[256,2048]{1,0:T(8,128)(2,1)}, u32[]{:S(2)}, u32[]{:S(2)}) collective-permute-start(bf16[256,2048]{1,0:T(8,128)(2,1)} %bitcast.300), channel_id=1, source_target_pairs={{0,1},{1,0},{2,3},{3,2},{4,5},{5,4},{6,7},{7,6},{8,9},{9,8},{10,11... | collective-permute-start | bytes 3145736 | tf_op jit(solution)/shard_map/ppermute | solution.py:226
  17.5 126.4 %collective-permute-start.1 = (bf16[256,2048]{1,0:T(8,128)(2,1)}, bf16[256,2048]{1,0:T(8,128)(2,1)}, u32[]{:S(2)}, u32[]{:S(2)}) collective-permute-start(bf16[256,2048]{1,0:T(8,128)(2,1)} %get-tuple-element.110), channel_id=1, source_target_pairs={{0,4},{2,6},{4,0},{6,2},{1,5},{3,7},{5,1},{7,3},{8,12},{10,14},{12... | collective-permute-start | bytes 3145736 | tf_op jit(solution)/shard_map/ppermute | solution.py:226
  19.4 127.0 %collective-permute-start = (bf16[256,2048]{1,0:T(8,128)(2,1)}, bf16[256,2048]{1,0:T(8,128)(2,1)}, u32[]{:S(2)}, u32[]{:S(2)}) collective-permute-start(bf16[256,2048]{1,0:T(8,128)(2,1)} %get-tuple-element.110), channel_id=1, source_target_pairs={{0,1},{1,0},{2,3},{3,2},{4,5},{5,4},{6,7},{7,6},{8,9},{9,8},{10,11... | collective-permute-start | bytes 3145736 | tf_op jit(solution)/shard_map/ppermute | solution.py:226
  156.7 58.9 %collective-permute-start.23 = (bf16[512,1024]{1,0:T(8,128)(2,1)S(1)}, bf16[512,1024]{1,0:T(8,128)(2,1)S(1)}, u32[]{:S(2)}, u32[]{:S(2)}) collective-permute-start(bf16[512,1024]{1,0:T(8,128)(2,1)S(1)} %bitcast.242), channel_id=1, source_target_pairs={{8,0},{16,8},{24,16},{9,1},{17,9},{25,17},{10,2},{18,10},{26,18},{... | collective-permute-start | bytes 3145736 | tf_op jit(solution)/shard_map/ppermute | solution.py:298
  177.6 59.5 %collective-permute-start.29 = (bf16[512,1024]{1,0:T(8,128)(2,1)S(1)}, bf16[512,1024]{1,0:T(8,128)(2,1)S(1)}, u32[]{:S(2)}, u32[]{:S(2)}) collective-permute-start(bf16[512,1024]{1,0:T(8,128)(2,1)S(1)} %bitcast.233), channel_id=1, source_target_pairs={{8,0},{16,8},{24,16},{9,1},{17,9},{25,17},{10,2},{18,10},{26,18},{... | collective-permute-start | bytes 3145736 | tf_op jit(solution)/shard_map/ppermute | solution.py:298
  244.8 70.4 %collective-permute-start.25 = (bf16[512,1024]{1,0:T(8,128)(2,1)S(1)}, bf16[512,1024]{1,0:T(8,128)(2,1)}, u32[]{:S(2)}, u32[]{:S(2)}) collective-permute-start(bf16[512,1024]{1,0:T(8,128)(2,1)S(1)} %collective-permute-done.23), channel_id=1, source_target_pairs={{8,0},{16,8},{9,1},{17,9},{10,2},{18,10},{11,3},{19,11},{12,4},{20... | collective-permute-start | bytes 3145736 | tf_op jit(solution)/shard_map/ppermute | solution.py:298
  246.1 70.4 %collective-permute-start.24 = (bf16[512,1024]{1,0:T(8,128)(2,1)S(1)}, bf16[512,1024]{1,0:T(8,128)(2,1)}, u32[]{:S(2)}, u32[]{:S(2)}) collective-permute-start(bf16[512,1024]{1,0:T(8,128)(2,1)S(1)} %collective-permute-done.22), channel_id=1, source_target_pairs={{8,16},{16,24},{9,17},{17,25},{10,18},{18,26},{11,19},{19,27},{12,... | collective-permute-start | bytes 3145736 | tf_op jit(solution)/shard_map/ppermute | solution.py:297
  271.0 255.3 %collective-permute-start.33 = (bf16[512,1024]{1,0:T(8,128)(2,1)}, bf16[512,1024]{1,0:T(8,128)(2,1)}, u32[]{:S(2)}, u32[]{:S(2)}) collective-permute-start(bf16[512,1024]{1,0:T(8,128)(2,1)} %collective-permute-done.31), channel_id=1, source_target_pairs={{8,0},{9,1},{10,2},{11,3},{12,4},{13,5},{14,6},{15,7}} | collective-permute-start | bytes 3145736 | tf_op jit(solution)/shard_map/ppermute | solution.py:298
  292.7 222.5 %collective-permute-start.32 = (bf16[512,1024]{1,0:T(8,128)(2,1)}, bf16[512,1024]{1,0:T(8,128)(2,1)}, u32[]{:S(2)}, u32[]{:S(2)}) collective-permute-start(bf16[512,1024]{1,0:T(8,128)(2,1)} %collective-permute-done.30), channel_id=1, source_target_pairs={{16,24},{17,25},{18,26},{19,27},{20,28},{21,29},{22,30},{23,31}} | collective-permute-start | bytes 3145736 | tf_op jit(solution)/shard_map/ppermute | solution.py:297
  316.6 160.6 %collective-permute-start.27 = (bf16[512,1024]{1,0:T(8,128)(2,1)}, bf16[512,1024]{1,0:T(8,128)(2,1)}, u32[]{:S(2)}, u32[]{:S(2)}) collective-permute-start(bf16[512,1024]{1,0:T(8,128)(2,1)} %collective-permute-done.25), channel_id=1, source_target_pairs={{8,0},{9,1},{10,2},{11,3},{12,4},{13,5},{14,6},{15,7}} | collective-permute-start | bytes 3145736 | tf_op jit(solution)/shard_map/ppermute | solution.py:298
  324.2 151.5 %collective-permute-start.26 = (bf16[512,1024]{1,0:T(8,128)(2,1)}, bf16[512,1024]{1,0:T(8,128)(2,1)}, u32[]{:S(2)}, u32[]{:S(2)}) collective-permute-start(bf16[512,1024]{1,0:T(8,128)(2,1)} %collective-permute-done.24), channel_id=1, source_target_pairs={{16,24},{17,25},{18,26},{19,27},{20,28},{21,29},{22,30},{23,31}} | collective-permute-start | bytes 3145736 | tf_op jit(solution)/shard_map/ppermute | solution.py:297
  609.4 86.9 %collective-permute-start.58 = (bf16[512,1024]{1,0:T(8,128)(2,1)S(1)}, bf16[512,1024]{1,0:T(8,128)(2,1)}, u32[]{:S(2)}, u32[]{:S(2)}) collective-permute-start(bf16[512,1024]{1,0:T(8,128)(2,1)S(1)} %get-tuple-element.136), channel_id=1, source_target_pairs={{24,16},{25,17},{26,18},{27,19},{28,20},{29,21},{30,22},{31,23}} | collective-permute-start | bytes 3145736 | tf_op jit(solution)/shard_map/ppermute | solution.py:323
  617.6 78.9 %collective-permute-start.68 = (bf16[512,1024]{1,0:T(8,128)(2,1)}, bf16[512,1024]{1,0:T(8,128)(2,1)}, u32[]{:S(2)}, u32[]{:S(2)}) collective-permute-start(bf16[512,1024]{1,0:T(8,128)(2,1)} %get-tuple-element.132), channel_id=1, source_target_pairs={{24,16},{25,17},{26,18},{27,19},{28,20},{29,21},{30,22},{31,23}} | collective-permute-start | bytes 3145736 | tf_op jit(solution)/shard_map/ppermute | solution.py:323
  620.2 56.7 %collective-permute-start.71 = (bf16[512,1024]{1,0:T(8,128)(2,1)}, bf16[512,1024]{1,0:T(8,128)(2,1)}, u32[]{:S(2)}, u32[]{:S(2)}) collective-permute-start(bf16[512,1024]{1,0:T(8,128)(2,1)} %get-tuple-element.127), channel_id=1, source_target_pairs={{0,8},{1,9},{2,10},{3,11},{4,12},{5,13},{6,14},{7,15}} | collective-permute-start | bytes 3145736 | tf_op jit(solution)/shard_map/ppermute | solution.py:321
  632.2 78.3 %collective-permute-start.74 = (bf16[512,1024]{1,0:T(8,128)(2,1)S(1)}, bf16[512,1024]{1,0:T(8,128)(2,1)S(1)}, u32[]{:S(2)}, u32[]{:S(2)}) collective-permute-start(bf16[512,1024]{1,0:T(8,128)(2,1)S(1)} %get-tuple-element.128), channel_id=1, source_target_pairs={{24,16},{25,17},{26,18},{27,19},{28,20},{29,21},{30,22},{31,23}} | collective-permute-start | bytes 3145736 | tf_op jit(solution)/shard_map/ppermute | solution.py:323
  710.5 56.8 %collective-permute-start.49 = (bf16[256,2048]{1,0:T(8,128)(2,1)S(1)}, bf16[256,2048]{1,0:T(8,128)(2,1)S(1)}, u32[]{:S(2)}, u32[]{:S(2)}) collective-permute-start(bf16[256,2048]{1,0:T(8,128)(2,1)S(1)} %pad_maximum_fusion.7), channel_id=1, source_target_pairs={{0,4},{2,6},{4,0},{6,2},{1,5},{3,7},{5,1},{7,3},{8,12},{10,14},{12... | collective-permute-start | bytes 3145736 | tf_op jit(solution)/shard_map/ppermute | solution.py:226
  794.6 71.5 %collective-permute-start.62 = (f32[7168]{0:T(1024)S(1)}, f32[7168]{0:T(1024)S(1)}, u32[]{:S(2)}, u32[]{:S(2)}) collective-permute-start(f32[7168]{0:T(1024)S(1)} %fusion.59), channel_id=1, source_target_pairs={{0,16},{8,24},{16,0},{24,8},{1,17},{9,25},{17,1},{25,9},{2,18},{10... | collective-permute-start | bytes 86024 | tf_op jit(solution)/shard_map/ppermute | solution.py:226
  802.0 112.6 %collective-permute-start.67 = (bf16[512,1024]{1,0:T(8,128)(2,1)}, bf16[512,1024]{1,0:T(8,128)(2,1)S(1)}, u32[]{:S(2)}, u32[]{:S(2)}) collective-permute-start(bf16[512,1024]{1,0:T(8,128)(2,1)} %get-tuple-element.129), channel_id=1, source_target_pairs={{0,8},{8,16},{16,24},{1,9},{9,17},{17,25},{2,10},{10,18},{18,26},{... | collective-permute-start | bytes 3145736 | tf_op jit(solution)/shard_map/ppermute | solution.py:321
  823.9 90.8 %collective-permute-start.70 = (bf16[512,1024]{1,0:T(8,128)(2,1)}, bf16[512,1024]{1,0:T(8,128)(2,1)}, u32[]{:S(2)}, u32[]{:S(2)}) collective-permute-start(bf16[512,1024]{1,0:T(8,128)(2,1)} %fusion.36), channel_id=1, source_target_pairs={{8,0},{16,8},{24,16},{9,1},{17,9},{25,17},{10,2},{18,10},{26,18},{... | collective-permute-start | bytes 3145736 | tf_op jit(solution)/shard_map/ppermute | solution.py:323
  826.6 98.8 %collective-permute-start.73 = (bf16[512,1024]{1,0:T(8,128)(2,1)}, bf16[512,1024]{1,0:T(8,128)(2,1)}, u32[]{:S(2)}, u32[]{:S(2)}) collective-permute-start(bf16[512,1024]{1,0:T(8,128)(2,1)} %get-tuple-element.125), channel_id=1, source_target_pairs={{0,8},{8,16},{16,24},{1,9},{9,17},{17,25},{2,10},{10,18},{18,26},{... | collective-permute-start | bytes 3145736 | tf_op jit(solution)/shard_map/ppermute | solution.py:321
  852.9 67.3 %all-to-all-start.3 = ((bf16[512,4,256]{2,1,0:T(4,128)(2,1)}), bf16[512,4,256]{2,1,0:T(4,128)(2,1)S(1)}, u32[]{:S(2)}, u32[]{:S(2)}) async-start(bf16[512,4,256]{2,1,0:T(4,128)(2,1)} %reshape.194), calls=%async_computation.3 | async-start | bytes 2097152 | tf_op jit(solution)/shard_map/all_to_all | solution.py:337
  856.5 68.9 %collective-permute-start.76 = (bf16[512,1024]{1,0:T(8,128)(2,1)}, bf16[512,1024]{1,0:T(8,128)(2,1)}, u32[]{:S(2)}, u32[]{:S(2)}) collective-permute-start(bf16[512,1024]{1,0:T(8,128)(2,1)} %fusion.30), channel_id=1, source_target_pairs={{8,0},{16,8},{24,16},{9,1},{17,9},{25,17},{10,2},{18,10},{26,18},{... | collective-permute-start | bytes 3145736 | tf_op jit(solution)/shard_map/ppermute | solution.py:323
  (115 other events, 2629.1 us)

commit v2 on v1

v2 whole, which is shorter than its diff:
```python
import functools
import types

import jax
import jax.numpy as jnp
from jax import lax
from jax.experimental import pallas as pl
from jax.experimental.pallas import tpu as pltpu
from jax.sharding import PartitionSpec as P

FSDP, CTX, TP = "fsdp", "ctx", "tp"

D = 2048
HEAD_DIM = 64
ROT = 32
GROUP = 256
PAIR = 2 * HEAD_DIM

EPSILON = 1e-05
MASKED = -1e30
GELU_SLOPE = 0.7978845608028654
GELU_CUBE = 0.044715


TURNS = ((3, 2, 1, 0), (3, 2, 0, 1), (0, 1, 3, 2), (0, 1, 2, 3))

NT = (((1,), (1,)), ((), ()))
NN = (((1,), (0,)), ((), ()))


NO_COST = pl.CostEstimate(flops=0, bytes_accessed=0, transcendentals=0)


def params(mebibytes=48):
    return pltpu.CompilerParams(vmem_limit_bytes=mebibytes * 1024 * 1024)


def dot(left, right, dims=NN):
    return lax.dot_general(left, right, dims, preferred_element_type=jnp.float32)


def turning(places):
    halfway = ROT // 2
    lane = jnp.arange(PAIR) % HEAD_DIM
    frequencies = 10000.0 ** (-((lane % halfway).astype(jnp.float32) * 2.0 / ROT))
    frequencies = jnp.where(lane < ROT, frequencies, 0.0)
    angles = places.astype(jnp.float32)[:, None] * frequencies[None, :]
    return jnp.cos(angles), jnp.sin(angles) * jnp.where(lane < halfway, -1.0, 1.0)[None, :]


def turn(values, cosine, sine):
    halfway = ROT // 2
    lane = lax.broadcasted_iota(jnp.int32, values.shape, 1) % HEAD_DIM
    partner = jnp.where(
        lane < halfway,
        pltpu.roll(values, PAIR - halfway, 1),
        pltpu.roll(values, halfway, 1),
    )
    return values * cosine + partner * sine


def attention_kernel(
    order,
    query_in,
    key_all,
    value_all,
    key_turned,
    value_turned,
    grad_in,
    grad_turned,
    cosine_all,
    sine_all,
    *refs,
):
    (attended_out, query_out, key_out, value_out, key_total, value_total, strip) = refs[-7:]
    groups, group = pl.num_programs(0), pl.program_id(0)
    tall, wide = strip.shape[1:]
    blocks = tall // GROUP

    def rows(place):
        return pl.ds(pl.multiple_of(order[place] * GROUP, GROUP), GROUP)

    def load(ref, step):
        return jnp.concatenate([ref[rows(step * blocks + at), :] for at in range(blocks)], axis=0)

    def load_turned(ref, step, head):
        here = slice(head * HEAD_DIM, (head + 1) * HEAD_DIM)
        return jnp.concatenate([ref[here, rows(step * blocks + at)] for at in range(blocks)], axis=1)

    def put(ref, step, values):
        for at in range(blocks):
            ref[rows(step * blocks + at), :] += values[at * GROUP : (at + 1) * GROUP]

    def fold(tile):
        return tile.reshape(tall // 8, 8, wide)

    def pair_up(values):
        first = lax.broadcasted_iota(jnp.int32, (GROUP, PAIR), 1) < HEAD_DIM
        nothing = jnp.zeros((GROUP, PAIR), jnp.bfloat16)
        return jnp.concatenate(
            [jnp.where(first, values, nothing), jnp.where(first, nothing, values)], axis=0
        )

    @pl.when(group == 0)
    def _():
        key_total[...] = jnp.zeros_like(key_total)
        value_total[...] = jnp.zeros_like(value_total)

    query_pair, grad_pair = pair_up(query_in[...]), pair_up(grad_in[...])
    steps = (group + blocks) // blocks
    ahead = lax.broadcasted_iota(jnp.int32, (tall, wide), 0) - (
        lax.broadcasted_iota(jnp.int32, (tall, wide), 1) % GROUP
    )

    def scores(step, most):
        tile = dot(load(key_all, step), query_pair, NT)
        tile = jnp.where(ahead <= (group - step * blocks) * GROUP, tile, MASKED)
        strip[step] = tile
        return jnp.maximum(most, jnp.max(fold(tile), axis=0))

    most = lax.fori_loop(0, steps, scores, jnp.full((8, wide), MASKED, jnp.float32))
    most = jnp.max(most, axis=0, keepdims=True)

    def weigh(step, carry):
        total, upper, lower = carry
        tile = jnp.exp(strip[step] - most)
        strip[step] = tile
        low = tile.astype(jnp.bfloat16)
        upper = upper + dot(load_turned(value_turned, step, 0), low[:, :GROUP])
        lower = lower + dot(load_turned(value_turned, step, 1), low[:, GROUP:])
        return total + jnp.sum(fold(tile), axis=0), upper, lower

    blank = jnp.zeros((HEAD_DIM, GROUP), jnp.float32)
    total, upper, lower = lax.fori_loop(
        0, steps, weigh, (jnp.zeros((8, wide), jnp.float32), blank, blank)
    )
    share = 1.0 / jnp.sum(total, axis=0, keepdims=True)
    upper = upper * share[:, :GROUP]
    lower = lower * share[:, GROUP:]
    attended_out[...] = jnp.concatenate([upper, lower], axis=0).astype(jnp.bfloat16).T
    grad = grad_turned[...].astype(jnp.float32)
    delta = jnp.concatenate(
        [
            jnp.sum(upper * grad[:HEAD_DIM], axis=0, keepdims=True),
            jnp.sum(lower * grad[HEAD_DIM:], axis=0, keepdims=True),
        ],
        axis=1,
    )

    def back(step, carry):
        upper, lower = carry
        part = strip[step] * share
        put(value_total, step, dot(part.astype(jnp.bfloat16), grad_pair))
        part = part * (dot(load(value_all, step), grad_pair, NT) - delta)
        low = part.astype(jnp.bfloat16)
        put(key_total, step, dot(low, query_pair))
        upper = upper + dot(load_turned(key_turned, step, 0), low[:, :GROUP])
        lower = lower + dot(load_turned(key_turned, step, 1), low[:, GROUP:])
        return upper, lower

    upper, lower = lax.fori_loop(0, steps, back, (blank, blank))
    own = rows(group)
    query_grad = jnp.concatenate([upper, lower], axis=0).T * HEAD_DIM ** (-0.5)
    query_out[...] = turn(query_grad, cosine_all[own, :], -sine_all[own, :]).astype(jnp.bfloat16)

    @pl.when(group == groups - 1)
    def _():
        key_grad = turn(key_total[...], cosine_all[...], -sine_all[...])
        key_out[...] = key_grad.astype(jnp.bfloat16)
        value_out[...] = value_total[...].astype(jnp.bfloat16)


def attention(order, projected, tables, pair, earlier=()):
    length, width = projected[0].shape
    groups = length // GROUP
    block = pl.BlockSpec((GROUP, PAIR), lambda group, order: (order[group], pair))
    turned_block = pl.BlockSpec((PAIR, GROUP), lambda group, order: (pair, order[group]))
    column = pl.BlockSpec((length, PAIR), lambda group, order: (0, pair))
    turned_column = pl.BlockSpec((PAIR, length), lambda group, order: (pair, 0))
    table = pl.BlockSpec((length, PAIR), lambda group, order: (0, 0))
    specs = [block, column, column, turned_column, turned_column, block, turned_block, table, table]
    return pl.pallas_call(
        attention_kernel,
        grid_spec=pltpu.PrefetchScalarGridSpec(
            num_scalar_prefetch=1,
            grid=(groups,),
            in_specs=specs + [pl.BlockSpec(memory_space=pl.ANY)] * len(earlier),
            out_specs=[block, block, column, column],
            scratch_shapes=[
                pltpu.VMEM((length, PAIR), jnp.float32),
                pltpu.VMEM((length, PAIR), jnp.float32),
                pltpu.VMEM((groups // 2, 2 * GROUP, 2 * GROUP), jnp.float32),
            ],
        ),
        out_shape=[jax.ShapeDtypeStruct((length, width), jnp.bfloat16)] * 4,
        input_output_aliases={1 + len(specs) + at: at for at in range(len(earlier))},
        compiler_params=params(60),
        cost_estimate=NO_COST,
        name=f"attention_{pair}",
    )(order, *projected, *tables, *earlier)


ROWS = 512


def chunk(place, which, size):
    return pl.ds(pl.multiple_of(place[which] * size, size), size)


def row_call(name, kernel, row_inputs, full_inputs, outputs, size=ROWS, turn=0, mebibytes=48):
    count = row_inputs[0].shape[0] // size
    rows = count * size

    def out(item):
        if len(item) == 4 and item[3] is None:
            shape, spec = item[:2], pl.BlockSpec(item[:2], lambda at: (0, 0))
        elif len(item) == 4:
            shape = ((item[3] - item[2]) * size, item[0])
            spec = pl.BlockSpec(
                (size, item[0]),
                lambda at: (jnp.clip(at, item[2], item[3] - 1) - item[2], 0),
            )
        elif len(item) == 3:
            shape = (item[0], rows)
            spec = pl.BlockSpec((item[0], size), lambda at: (0, at))
        else:
            shape = (rows, item[0])
            spec = pl.BlockSpec((size, item[0]), lambda at: (at, 0))
        kind = item[2] if len(item) == 4 and item[3] is None else item[1]
        return spec, jax.ShapeDtypeStruct(shape, kind)

    return pl.pallas_call(
        kernel,
        grid=(count,),
        in_specs=[
            pl.BlockSpec((size, item.shape[1]), lambda at: (lax.rem(at + turn, count), 0))
            for item in row_inputs
        ]
        + [pl.BlockSpec(item.shape, lambda at: (0, 0)) for item in full_inputs],
        out_specs=[out(item)[0] for item in outputs],
        out_shape=[out(item)[1] for item in outputs],
        compiler_params=params(mebibytes),
        cost_estimate=NO_COST,
        name=name,
    )(*row_inputs, *full_inputs)


def add_up(target, at, values):
    part = jnp.sum(values.astype(jnp.float32), axis=0, keepdims=True)

    @pl.when(pl.program_id(0) == 0)
    def _():
        target[at : at + 1, :] = part

    @pl.when(pl.program_id(0) > 0)
    def _():
        target[at : at + 1, :] += part


def project_kernel(normed, grads, cosine, sine, weight, bias, *refs):
    query, key, value, key_turned, value_turned, out_grads, grads_turned = refs
    width = weight.shape[1] // 4
    mixed = dot(normed[...], weight[:, : 3 * width]) + bias[...]
    parts = [mixed[:, which * width : (which + 1) * width] for which in range(3)]
    parts.append(dot(grads[...], weight[:, 3 * width :]))
    for pair in range(-(-width // PAIR)):
        here = slice(pair * PAIR, (pair + 1) * PAIR)
        items = [part[:, here] for part in parts]
        if width < PAIR:
            nothing = jnp.zeros((ROWS, PAIR - width), jnp.float32)
            items = [jnp.concatenate([item, nothing], axis=1) for item in items]
        turned = [turn(item, cosine[...], sine[...]) for item in items[:2]]
        low = turned[0].astype(jnp.bfloat16).astype(jnp.float32) * HEAD_DIM ** (-0.5)
        query[:, here] = low.astype(jnp.bfloat16)
        for target, target_turned, item in (
            (key, key_turned, turned[1]),
            (value, value_turned, items[2]),
            (out_grads, grads_turned, items[3]),
        ):
            low = item.astype(jnp.bfloat16)
            target[:, here] = low
            target_turned[here, :] = low.T


def hidden_kernel(normed, weight, bias, activated, slope):
    hidden = dot(normed[...], weight[...]) + bias[...]
    square = hidden * hidden
    bent = jnp.tanh(GELU_SLOPE * hidden * (1.0 + GELU_CUBE * square))
    half = 0.5 * (1.0 + bent)
    activated[...] = (hidden * half).astype(jnp.bfloat16)
    slope[...] = (
        half
        + 0.5 * GELU_SLOPE * hidden * (1.0 - bent * bent) * (1.0 + 3.0 * GELU_CUBE * square)
    ).astype(jnp.bfloat16)


def hidden_grad_kernel(grads, slope, weight, target, sums):
    low = (dot(grads[...], weight[...]) * slope[...].astype(jnp.float32)).astype(jnp.bfloat16)
    target[...] = low
    add_up(sums, 0, low)


def back_kernel(columns, start, summing, halves, *refs):
    lefts = refs[: len(columns)]
    weights, outs = refs[len(columns) + start : -1 - summing - halves], refs[-1 - summing - halves :]
    result = refs[len(columns)][...].astype(jnp.float32) if start else None
    for left, (which, here) in zip(lefts, columns):
        part = dot(left[:, : here.stop - here.start], weights[which][:, here], NT)
        result = part if result is None else result + part
    if halves:
        early = pl.program_id(0) < pl.num_programs(0) // 2

        @pl.when(early)
        def _():
            outs[0][...] = result.astype(jnp.bfloat16)

        @pl.when(jnp.logical_not(early))
        def _():
            outs[1][...] = result.astype(jnp.bfloat16)

    else:
        outs[0][...] = result.astype(jnp.bfloat16)
    if summing:
        for at, left in enumerate(lefts):
            add_up(outs[1], at, left[...])


def back(lefts, columns, weights, start=None, halves=False, summing=False):
    size = ROWS
    count = lefts[0].shape[0] // size
    starts = [] if start is None else [start]
    outputs = [(weights[0].shape[0], jnp.bfloat16)]
    if halves:
        outputs = [outputs[0] + (0, count // 2), outputs[0] + (count // 2, count)]
    if summing:
        outputs.append((len(lefts), lefts[0].shape[1], jnp.float32, None))
    got = row_call(
        "back",
        functools.partial(back_kernel, columns, len(starts), int(summing), int(halves)),
        lefts + starts,
        weights,
        outputs,
        size,
        count // 2 if halves else 0,
    )
    return got if summing or halves else got[0]


def grad_kernel(counts, width, turns, *refs):
    target = refs[-1]
    refs = list(refs[:-1])
    at = 0
    for count in counts:
        left = refs.pop(0)
        for _ in range(count):
            right = refs.pop(0)
            columns = min(width, right.shape[1])
            target[0, :, at : at + columns] = dot(
                left[...], right[:, :columns], (((0,), (0,)), ((), ()))
            ).astype(jnp.bfloat16)
            at += columns


def grad_pieces(products, turns, first, count, width):
    size = lax.axis_size(FSDP)
    specs, items, columns = [], [], 0
    for left, rights in products:
        rows = left.shape[1] // size
        specs.append(
            pl.BlockSpec((left.shape[0], rows), lambda at, turns: (0, turns[first + at]))
        )
        specs += [pl.BlockSpec(item.shape, lambda at, turns: (0, 0)) for item in rights]
        items += [left, *rights]
        columns += sum(min(width, item.shape[1]) for item in rights)
    return pl.pallas_call(
        functools.partial(grad_kernel, [len(rights) for _, rights in products], width),
        grid_spec=pltpu.PrefetchScalarGridSpec(
            num_scalar_prefetch=1,
            grid=(count,),
            in_specs=specs,
            out_specs=pl.BlockSpec((1, rows, columns), lambda at, turns: (at, 0, 0)),
        ),
        out_shape=jax.ShapeDtypeStruct((count, rows, columns), jnp.bfloat16),
        compiler_params=params(),
        cost_estimate=NO_COST,
        name=f"grad_{first}",
    )(turns, *items)


def pointwise(name, function, scalars, inputs, outputs):
    def spec(item):
        if not isinstance(item, tuple):
            return pl.BlockSpec(item.shape, lambda at, n=item.ndim: (0,) * n)
        array, rows, index = item
        return pl.BlockSpec(
            (rows,) + array.shape[1:], lambda at, n=array.ndim, index=index: (index,) + (0,) * (n - 1)
        )

    def kernel(*refs):
        count = len(scalars) + len(inputs)
        for target, value in zip(refs[count:], function(*refs[:count])):
            target[...] = value.astype(target.dtype)

    return pl.pallas_call(
        kernel,
        grid=(1,),
        in_specs=[pl.BlockSpec(memory_space=pltpu.SMEM)] * len(scalars) + [spec(i) for i in inputs],
        out_specs=[pl.BlockSpec(shape, lambda at, n=len(shape): (0,) * n) for shape, _ in outputs],
        out_shape=[jax.ShapeDtypeStruct(shape, kind) for shape, kind in outputs],
        compiler_params=params(),
        cost_estimate=NO_COST,
        name=name,
    )(*scalars, *[item[0] if isinstance(item, tuple) else item for item in inputs])


def stack_kernel(parts, *refs):
    *sources, target, arrived = refs
    copies = [
        pltpu.make_async_copy(
            source.at[pl.ds(first, rows)], target.at[pl.ds(start, rows)], arrived.at[at]
        )
        for at, (source, (first, rows, start)) in enumerate(zip(sources, parts))
    ]
    for copy in copies:
        copy.start()
    for copy in copies:
        copy.wait()


def stack(parts, rows):
    array = parts[0][0]
    return pl.pallas_call(
        functools.partial(stack_kernel, [part[1:] for part in parts]),
        in_specs=[pl.BlockSpec(memory_space=pl.ANY)] * len(parts),
        out_specs=pl.BlockSpec(memory_space=pltpu.VMEM),
        out_shape=jax.ShapeDtypeStruct((rows, array.shape[1]), array.dtype),
        scratch_shapes=[pltpu.SemaphoreType.DMA((len(parts),))],
        compiler_params=params(),
        cost_estimate=NO_COST,
        name="stack",
    )(*[part[0] for part in parts])


def fill_kernel(starts, *refs):
    count = len(starts)
    sources, target = refs[:count], refs[count + 1]
    held, arrived, left = refs[count + 2 :]
    rows = [source.shape[0] for source in sources]
    slots = [pl.ds(sum(rows[:at]), rows[at]) for at in range(count)]
    inward = [
        pltpu.make_async_copy(source, held.at[slots[at]], arrived.at[at])
        for at, source in enumerate(sources)
    ]
    outward = [
        pltpu.make_async_copy(held.at[slots[at]], target.at[pl.ds(start, rows[at])], left.at[at])
        for at, start in enumerate(starts)
    ]
    for copy in inward:
        copy.start()
    for first, second in zip(inward, outward):
        first.wait()
        second.start()
    for copy in outward:
        copy.wait()


def fill(target, parts):
    anywhere = pl.BlockSpec(memory_space=pl.ANY)
    count = len(parts)
    rows = sum(array.shape[0] for array, _ in parts)
    return pl.pallas_call(
        functools.partial(fill_kernel, [start for _, start in parts]),
        in_specs=[anywhere] * (count + 1),
        out_specs=anywhere,
        out_shape=jax.ShapeDtypeStruct(target.shape, target.dtype),
        scratch_shapes=[
            pltpu.VMEM((rows, target.shape[1]), target.dtype),
            pltpu.SemaphoreType.DMA((count,)),
            pltpu.SemaphoreType.DMA((count,)),
        ],
        input_output_aliases={count: 0},
        compiler_params=params(),
        cost_estimate=NO_COST,
        name="fill",
    )(*[array for array, _ in parts], target)


def line_kernel(place, *refs):
    own, up_one, down_one, up_two, down_two, up_three, down_three, target, arrived = refs
    rows = own.shape[0]
    for where, sources in enumerate(
        (
            (own, down_one, down_two, down_three),
            (up_one, own, down_one, down_two),
            (up_two, up_one, own, down_one),
            (up_three, up_two, up_one, own),
        )
    ):

        @pl.when(place[0] == where)
        def _(sources=sources):
            copies = [
                pltpu.make_async_copy(source, target.at[pl.ds(at * rows, rows)], arrived.at[at])
                for at, source in enumerate(sources)
            ]
            for copy in copies:
                copy.start()
            for copy in copies:
                copy.wait()


def in_line(got):
    anywhere = pl.BlockSpec(memory_space=pl.ANY)
    rows, columns = got[0].shape
    return pl.pallas_call(
        line_kernel,
        in_specs=[pl.BlockSpec(memory_space=pltpu.SMEM)] + [anywhere] * len(got),
        out_specs=pl.BlockSpec(memory_space=pltpu.VMEM),
        out_shape=jax.ShapeDtypeStruct((4 * rows, columns), got[0].dtype),
        scratch_shapes=[pltpu.SemaphoreType.DMA((4,))],
        compiler_params=params(),
        cost_estimate=NO_COST,
        name="in_line",
    )(lax.axis_index(FSDP).astype(jnp.int32).reshape(1), *got)


def swap(values, axis, bit):
    size = lax.axis_size(axis)
    with jax.named_scope(f"{axis}_{bit}"):
        return lax.ppermute(values, axis, [(place, place ^ bit) for place in range(size)])


def total(values, axis):
    bit = 1
    while bit < lax.axis_size(axis):
        values = values + swap(values, axis, bit)
        bit *= 2
    return values


def move(values, pairs):
    with jax.named_scope("line"):
        return lax.ppermute(values, FSDP, pairs)


def spread_first(own):
    return [own, move(own, [(0, 1), (1, 2), (2, 3)]), move(own, [(1, 0), (2, 1), (3, 2)])]


def spread_second(got):
    return got + [move(got[1], [(1, 2), (2, 3)]), move(got[2], [(1, 0), (2, 1)])]


def spread_third(got):
    return got + [move(got[3], [(2, 3)]), move(got[4], [(1, 0)])]


def reduce_first(parts):
    return move(parts[0], [(0, 1), (3, 2)])


def square_first(own):
    return [own, swap(own, FSDP, 1), swap(own, FSDP, 2)]


def square_second(got):
    return got + [swap(got[2], FSDP, 1)]


def square_kernel(place, *refs):
    *sources, target, arrived = refs
    rows = sources[0].shape[0]
    copies = []
    for which, source in enumerate(sources):
        here = pl.ds(pl.multiple_of((place[0] ^ which) * rows, rows), rows)
        copies.append(pltpu.make_async_copy(source, target.at[here], arrived.at[which]))
    for copy in copies:
        copy.start()
    for copy in copies:
        copy.wait()


def in_square(got, place):
    rows, columns = got[0].shape
    return pl.pallas_call(
        square_kernel,
        in_specs=[pl.BlockSpec(memory_space=pltpu.SMEM)]
        + [pl.BlockSpec(memory_space=pl.ANY)] * len(got),
        out_specs=pl.BlockSpec(memory_space=pltpu.VMEM),
        out_shape=jax.ShapeDtypeStruct((len(got) * rows, columns), got[0].dtype),
        scratch_shapes=[pltpu.SemaphoreType.DMA((len(got),))],
        compiler_params=params(),
        cost_estimate=NO_COST,
        name="in_square",
    )(place, *got)


UP, DOWN = [(0, 1), (1, 2), (2, 3)], [(1, 0), (2, 1), (3, 2)]


def second_of(place, first, second, got):
    ends = (place[0] == 0) | (place[0] == 3)
    return jnp.where(ends, sum_of(second)[0], sum_of(first) + got)


def third_of(place, second, third, upward, downward):
    one, two = sum_of(second)[0], sum_of(third)[0]
    return (
        jnp.where(place[0] == 1, one, two) + sum_of(upward),
        jnp.where(place[0] == 2, one, two) + sum_of(downward),
    )


def reduce_second(sums, place):
    inputs = []
    for (first, rest), got in sums:
        inputs += [first, (rest, 1, 0), got]
    rows, columns = sums[0][0][0].shape

    def choose(place, *refs):
        sent = [
            second_of(place, first, second, sum_of(got))
            for first, second, got in zip(refs[::3], refs[1::3], refs[2::3])
        ]
        return [jnp.concatenate(sent, axis=0)]

    sent = pointwise(
        "second", choose, [place], inputs, [((len(sums) * rows, columns), jnp.bfloat16)]
    )[0]
    return [move(sent, UP[:2]), move(sent, DOWN[1:])]


def reduce_third(parts, got, place, new=None):
    first, rest = parts
    rows, columns = first.shape
    shape = (rows if new is None else 2 * rows, columns)

    def choose(place, second, third, upward, downward, *others):
        sent = third_of(place, second, third, upward, downward)
        if not others:
            return sent
        first, second, got = others
        other = second_of(place, first, second, sum_of(got))
        return [jnp.concatenate([item, other], axis=0) for item in sent]

    inputs = [(rest, 1, 0), (rest, 1, 1), *got]
    if new is not None:
        inputs += [new[0][0], (new[0][1], 1, 0), new[1]]
    upward, downward = pointwise(
        "third", choose, [place], inputs, [(shape, jnp.bfloat16)] * 2
    )
    return [move(upward, UP), move(downward, DOWN)]


def reduce_last(parts, got, index=0):
    first, rest = parts
    return pointwise(
        "last",
        lambda last, *got: [sum_of(last)[0] + sum_of(*got)],
        [],
        [(rest, 1, 2)] + [(item, first.shape[0], index) for item in got],
        [(first.shape, jnp.bfloat16)],
    )[0]


def paired():
    return lax.axis_size(CTX) == 4 and lax.axis_size(TP) == 2


def gather_first(own):
    if not paired():
        return [own]
    return [own, swap(own, TP, 1), swap(own, CTX, 2), swap(own, CTX, 1)]


def gather_second(got):
    if not paired():
        return got
    size = got[0].shape[0] // 2
    corner = [swap(got[1][:size], CTX, 2), swap(got[2][size:], TP, 1)]
    return got + [swap(got[1], CTX, 1), swap(got[2], CTX, 1)] + corner


def gather_third(got):
    if not paired():
        size = got[0].shape[0] // 2
        return [
            lax.all_gather(item, (CTX, TP), axis=0, tiled=True)
            for item in (got[0][:size], got[0][size:])
        ]
    own, across, along, far_own, far_across, far_along, *corner = got
    size = corner[0].shape[0]
    half = size // 2
    results = []
    for which in range(2):
        sides = (own, across, along, None, far_own, far_across, far_along, None)
        parts = [
            (item, which * size, size, at * size)
            for at, item in enumerate(sides)
            if item is not None
        ]
        results.append(stack(parts, 8 * size))
    corner, results = lax.optimization_barrier((corner, results))
    for which in range(2):
        parts = [(corner[which], 3 * size)]
        for at in (0, half):
            parts.append((swap(corner[which][at : at + half], CTX, 1), 7 * size + at))
        results[which] = fill(results[which], parts)
    return results


def scatter_first(near, far):
    return [near, swap(far, CTX, 1) if paired() else far]


def sum_of(*refs):
    result = None
    for ref in refs:
        values = ref[...].astype(jnp.float32)
        result = values if result is None else result + values
    return result


def scatter_second(*all_got):
    if not paired():
        return list(all_got)
    size, columns = all_got[0][0].shape[0] // 4, all_got[0][0].shape[1]
    half = size // 2

    def corners(*refs):
        sums = [sum_of(*refs[at : at + 2]) for at in range(0, len(refs), 2)]
        return [
            jnp.concatenate([item[:half] for item in sums], axis=0),
            jnp.concatenate([item[half:] for item in sums], axis=0),
        ]

    sent = pointwise(
        "corners",
        corners,
        [],
        [(item, size, 3) for got in all_got for item in got],
        [((len(all_got) * half, columns), jnp.bfloat16)] * 2,
    )
    from_across, from_along = swap(sent[0], TP, 1), swap(sent[1], CTX, 2)
    return [got + [from_across, from_along] for got in all_got]


def scatter_third(*all_got):
    if not paired():
        return [
            [lax.psum_scatter(jnp.concatenate(got), (CTX, TP), scatter_dimension=0, tiled=True)]
            for got in all_got
        ]
    size, columns = all_got[0][0].shape[0] // 4, all_got[0][0].shape[1]
    half = size // 2

    def sides(*refs):
        acrosses, alongs = [], []
        for at in range(0, len(refs), 6):
            across, along = sum_of(*refs[at : at + 2]), sum_of(*refs[at + 2 : at + 4])
            from_across, from_along = refs[at + 4 : at + 6]
            acrosses += [across[:half], across[half:] + sum_of(from_along)]
            alongs += [along[:half] + sum_of(from_across), along[half:]]
        return [jnp.concatenate(acrosses, axis=0), jnp.concatenate(alongs, axis=0)]

    inputs = []
    for at, (near, far, from_across, from_along) in enumerate(all_got):
        inputs += [(near, size, 1), (far, size, 1), (near, size, 2), (far, size, 2)]
        inputs += [(from_across, half, at), (from_along, half, at)]
    across, along = pointwise(
        "sides", sides, [], inputs, [((len(all_got) * size, columns), jnp.bfloat16)] * 2
    )
    across, along = swap(across, TP, 1), swap(along, CTX, 2)
    return [[near, far, across, along] for near, far, *_ in all_got]


def addends(got, index):
    if not paired():
        return got
    size = got[0].shape[0] // 4
    return [(got[0], size, 0), (got[1], size, 0), (got[2], size, index), (got[3], size, index)]


def local_places(positions):
    if not paired():
        return positions
    devices = jnp.array([2 * along + near for near in (0, 1) for along in (0, 1) for _ in (0, 1)])
    blocks = (lax.axis_index(CTX) ^ devices) * 2 + (
        lax.axis_index(TP) ^ jnp.array([0, 1] * 4)
    )
    return positions.reshape(8, -1)[blocks].reshape(-1)


def hold(values, *after):
    return lax.optimization_barrier((values,) + after)[0]


def tick(live):
    vars(live).update(lax.optimization_barrier(dict(vars(live))))


def small_call(name, kernel, place, items, shapes, kind):
    vmem = pl.BlockSpec(memory_space=pltpu.VMEM)
    return pl.pallas_call(
        kernel,
        in_specs=[pl.BlockSpec(memory_space=pltpu.SMEM)] + [vmem] * len(items),
        out_specs=[vmem] * len(shapes),
        out_shape=[jax.ShapeDtypeStruct(shape, kind) for shape in shapes],
        compiler_params=params(),
        cost_estimate=NO_COST,
        name=name,
    )(place, *items)


def small_call(name, kernel, items, shapes, kind):
    vmem = pl.BlockSpec(memory_space=pltpu.VMEM)
    return pl.pallas_call(
        kernel,
        in_specs=[vmem] * len(items),
        out_specs=[vmem] * len(shapes),
        out_shape=[jax.ShapeDtypeStruct(shape, kind) for shape in shapes],
        compiler_params=params(),
        cost_estimate=NO_COST,
        name=name,
    )(*items)


def pieces(kind, *sources):
    parts = lax.axis_size(CTX)
    rows = sources[-1].shape[0 if kind == "up" else 1]
    width = sources[-1].shape[1 if kind == "up" else 0] // parts
    columns = 4 * width if kind == "attention" else width
    if width % PAIR:
        items = jnp.stack([*sources[0], sources[1].T]).reshape(4, rows, parts, width)
        return jnp.transpose(items, (2, 1, 0, 3)).reshape(parts, rows, columns)

    def kernel(*refs):
        *sources, target = refs
        for r in range(parts):
            here = slice(r * width, (r + 1) * width)
            if kind == "attention":
                for which in range(3):
                    target[r, :, which * width : (which + 1) * width] = sources[0][which, :, here]
                target[r, :, 3 * width :] = sources[1][here, :].T
            elif kind == "up":
                target[r] = sources[0][:, here]
            else:
                target[r] = sources[0][here, :].T

    return small_call("pieces", kernel, sources, [(parts, rows, columns)], sources[0].dtype)[0]


def trade(sent):
    return lax.all_to_all(sent, CTX, 0, 0, tiled=True)


def gather_rows_of(sent):
    got = trade(sent)
    return got.reshape(-1, got.shape[2])


def trade_back(*summed):
    parts = lax.axis_size(CTX)
    split = [item.reshape(parts, -1, item.shape[1]) for item in summed]
    return trade(split[0] if len(split) == 1 else jnp.concatenate(split, axis=1))


def finish(received, kind, index=0, count=1):
    parts, rows, columns = received.shape
    rows //= count
    width = columns // 4 if kind == "attention" else columns
    if width % PAIR:
        items = received[:, index * rows : (index + 1) * rows].astype(jnp.float32)
        items = jnp.transpose(items.reshape(parts, rows, 4, width), (2, 1, 0, 3))
        items = items.reshape(4, rows, parts * width)
        return items[:3], items[3].T

    def kernel(source, *targets):
        for r in range(parts):
            here = slice(r * width, (r + 1) * width)
            values = source[r, index * rows : (index + 1) * rows].astype(jnp.float32)
            if kind == "attention":
                for which in range(3):
                    targets[0][which, :, here] = values[:, which * width : (which + 1) * width]
                targets[1][here, :] = values[:, 3 * width :].T
            elif kind == "up":
                targets[0][:, here] = values
            else:
                targets[0][here, :] = values.T

    shapes = {
        "attention": [(3, rows, parts * width), (parts * width, rows)],
        "up": [(rows, parts * width)],
        "down": [(parts * width, rows)],
    }[kind]
    return small_call("finish", kernel, [received], shapes, jnp.float32)


def unit_of(tokens):
    inputs = tokens.astype(jnp.float32)
    centered = inputs - jnp.mean(inputs, axis=-1, keepdims=True)
    inverse = lax.rsqrt(jnp.mean(centered * centered, axis=-1, keepdims=True) + EPSILON)
    return centered * inverse, inverse


def tokens_grad_of(tokens, cotangent, norm_gain, *refs):
    unit, inverse = unit_of(tokens[...])
    grads = cotangent[...].astype(jnp.float32)
    normed_grad = sum_of(*refs)
    unit_grad = normed_grad * norm_gain[...].astype(jnp.float32)
    tokens_grad = grads + inverse * (
        unit_grad
        - jnp.mean(unit_grad, axis=-1, keepdims=True)
        - unit * jnp.mean(unit_grad * unit, axis=-1, keepdims=True)
    )
    sums = [
        jnp.sum(item, axis=0, keepdims=True) for item in (normed_grad * unit, normed_grad, grads)
    ]
    return [tokens_grad, jnp.concatenate(sums, axis=0)]


def on_device(
    tokens,
    positions,
    cotangent,
    norm_gain,
    norm_bias,
    qkv_weight,
    qkv_bias,
    out_weight,
    out_bias,
    up_weight,
    up_bias,
    down_weight,
    down_bias,
):
    parts = lax.axis_size(CTX)
    part = lax.axis_index(CTX)
    width = qkv_weight.shape[2] // parts
    units = up_weight.shape[1] // parts

    unit_rows, _ = unit_of(tokens[0])
    normed_own = (unit_rows * norm_gain + norm_bias).astype(jnp.bfloat16)

    place = lax.axis_index(FSDP)
    turns = jnp.array(TURNS, jnp.int32)[place]
    place = place.astype(jnp.int32).reshape(1)

    def first_grad(columns, *products):
        return grad_pieces(products, turns, 0, 1, columns)[0]

    def later_grads(columns, *products):
        return [grad_pieces(products, turns, 1, 3, columns)]

    live = types.SimpleNamespace(
        attention=gather_rows_of(pieces("attention", jnp.swapaxes(qkv_weight, 0, 1), out_weight)),
        rows=jnp.concatenate([normed_own, cotangent[0]], axis=0),
        tokens=tokens[0],
        cotangent=cotangent[0],
        weights=(up_weight, down_weight),
        positions=positions,
    )
    tick(live)
    live.attention = square_first(live.attention)
    live.rows = gather_first(live.rows)
    live.places = local_places(live.positions)
    live.turning = turning(live.places)
    tick(live)
    live.attention = square_second(live.attention)
    live.normed, live.grads = gather_third(gather_second(live.rows))
    live.up = gather_rows_of(pieces("up", live.weights[0]))
    live.down = pieces("down", live.weights[1])
    del live.rows
    tick(live)
    live.up = square_first(live.up)
    live.down = gather_rows_of(live.down)
    live.attention = in_square(live.attention, place)
    qkv_part = lax.dynamic_slice_in_dim(qkv_bias, part * width, width, 1).astype(jnp.float32)
    padded = width + -width % PAIR
    pairs = padded // PAIR
    projected = row_call(
        "project",
        project_kernel,
        [live.normed, live.grads, *live.turning],
        [live.attention, qkv_part.reshape(1, 3 * width)],
        [(padded, jnp.bfloat16)] * 3
        + [(padded, jnp.bfloat16, True)] * 2
        + [(padded, jnp.bfloat16), (padded, jnp.bfloat16, True)],
        mebibytes=60,
    )
    groups = live.places[::GROUP] // GROUP
    order = jnp.sum(
        jnp.where(
            groups[None, :] == jnp.arange(groups.shape[0])[:, None],
            jnp.arange(groups.shape[0])[None, :],
            0,
        ),
        axis=1,
    ).astype(jnp.int32)
    heads = ()
    for pair in range(pairs // 2):
        heads = attention(order, projected, live.turning, pair, heads)
    live.projected, live.order, live.heads = projected, order, heads
    tick(live)
    live.up = square_second(live.up)
    live.down = spread_first(live.down)
    heads = live.heads
    for pair in range(pairs // 2, pairs):
        heads = attention(live.order, live.projected, live.turning, pair, heads)
    live.heads = heads
    attended, *head_grads = live.heads
    head_products = ((live.normed, head_grads), (live.grads, [attended]))
    live.head_parts = [first_grad(width, *head_products)]
    tick(live)
    live.down = spread_second(live.down)
    live.head_sum = reduce_first(live.head_parts)
    attended, *head_grads = live.heads
    head_products = ((live.normed, head_grads), (live.grads, [attended]))
    live.up = in_square(live.up, place)
    own_bias = lax.dynamic_slice_in_dim(up_bias, part * units, units, 0).astype(jnp.float32)
    live.activated, live.slope = row_call(
        "hidden",
        hidden_kernel,
        [live.normed],
        [live.up, own_bias[None]],
        [(units, jnp.bfloat16), (units, jnp.bfloat16)],
    )
    live.head_parts = live.head_parts + later_grads(width, *head_products)
    tick(live)
    live.down = spread_third(live.down)
    live.head_sum = reduce_second([(live.head_parts, live.head_sum)], place)
    down_products = (live.grads, [live.activated])
    live.down_parts = [first_grad(units, down_products)] + later_grads(units, down_products)
    columns = [(0, slice(which * width, (which + 1) * width)) for which in range(4)]
    live.normed_part, live.qkv_sums = back(
        list(live.heads[1:]), columns[:3], [live.attention], summing=True
    )
    tick(live)
    live.head_sum = reduce_third(live.head_parts, live.head_sum, place)
    live.down_sum = reduce_first(live.down_parts)
    live.down = in_line(live.down)
    live.hidden_grad, live.up_sums = row_call(
        "hidden_grad",
        hidden_grad_kernel,
        [live.grads, live.slope],
        [live.down],
        [(units, jnp.bfloat16), (1, units, jnp.float32, None)],
    )
    everything = (0, slice(0, units))
    live.branch = back(
        [live.activated, live.heads[0]],
        [everything, (1, columns[3][1])],
        [live.down, live.attention],
        halves=True,
    )
    tick(live)
    live.down_sum = reduce_second([(live.down_parts, live.down_sum)], place)
    far, near = live.branch
    (live.branch,) = scatter_third(*scatter_second(scatter_first(near, far)))
    up_products = (live.normed, [live.hidden_grad])
    live.up_parts = [first_grad(units, up_products)]
    live.up_sum = reduce_first(live.up_parts)
    live.up_parts = live.up_parts + later_grads(units, up_products)
    live.normed_part = back(
        [live.hidden_grad], [everything], [live.up], live.normed_part, halves=True
    )
    tick(live)
    live.down_sum = reduce_third(
        live.down_parts, live.down_sum, place, (live.up_parts, live.up_sum)
    )
    far, near = live.normed_part
    (live.normed_part,) = scatter_third(*scatter_second(scatter_first(near, far)))
    live.head_sum = reduce_last(live.head_parts, live.head_sum)
    live.sums = jnp.concatenate(
        [
            lax.dynamic_update_slice_in_dim(
                jnp.zeros(qkv_bias.shape, jnp.float32),
                live.qkv_sums[:, :width],
                part * width,
                1,
            ).reshape(-1),
            lax.dynamic_update_slice_in_dim(
                jnp.zeros(up_bias.shape, jnp.float32), live.up_sums[0], part * units, 0
            ),
        ]
    )
    tick(live)
    second = [(item, live.up_parts[0].shape[0], 1) for item in live.down_sum]
    live.up_sum = reduce_third(live.up_parts, second, place)
    down_sum = reduce_last(live.down_parts, live.down_sum)
    live.both = trade_back(live.head_sum, down_sum)
    live.tokens_grad, norm_sums = pointwise(
        "tokens_grad",
        tokens_grad_of,
        [],
        [live.tokens, live.cotangent, norm_gain[None]] + addends(live.normed_part, 0),
        [(tokens.shape[1:], jnp.float32), ((3, D), jnp.float32)],
    )
    (live.layer_output,) = pointwise(
        "layer_output",
        lambda tokens, *refs: [sum_of(tokens, *refs)],
        [],
        [live.tokens, out_bias[None], down_bias[None]] + addends(live.branch, 0),
        [(tokens.shape[1:], jnp.bfloat16)],
    )
    norm_sums = total(norm_sums.reshape(-1), TP)
    live.sums = jnp.concatenate([live.sums, norm_sums])
    tick(live)
    up_sum = trade_back(reduce_last(live.up_parts, live.up_sum))
    (down_weight_grad,) = finish(live.both, "down", 1, 2)
    qkv_weight_grad, out_weight_grad = finish(live.both, "attention", 0, 2)
    sums = total(total(live.sums, FSDP), CTX)
    (up_weight_grad,) = finish(up_sum, "up")
    bias_sums = sums[: -3 * D]
    norm_sums = sums[-3 * D :].reshape(3, D)
    tokens_grad, layer_output = live.tokens_grad, live.layer_output

    return (
        layer_output[None],
        tokens_grad[None],
        norm_sums[0],
        norm_sums[1],
        jnp.swapaxes(qkv_weight_grad, 0, 1),
        bias_sums[: qkv_bias.size].reshape(qkv_bias.shape),
        out_weight_grad,
        norm_sums[2],
        up_weight_grad,
        bias_sums[qkv_bias.size :],
        down_weight_grad,
        norm_sums[2],
    )


def solution(mesh):
    rows = P(FSDP, (CTX, TP), None)
    placed = (
        rows,
        P(),
        rows,
        P(),
        P(),
        P((FSDP, CTX), None, TP),
        P(None, TP),
        P(TP, (FSDP, CTX)),
        P(),
        P((FSDP, CTX), TP),
        P(TP),
        P(TP, (FSDP, CTX)),
        P(),
    )
    return jax.shard_map(
        on_device,
        mesh=mesh,
        in_specs=placed,
        out_specs=(
            rows,
            rows,
            P(),
            P(),
            P((FSDP, CTX), None, TP),
            P(None, TP),
            P(TP, (FSDP, CTX)),
            P(),
            P((FSDP, CTX), TP),
            P(TP),
            P(TP, (FSDP, CTX)),
            P(),
        ),
        check_vma=False,
    )
```

time: 982 us -> 574 us (0.58)
  Pallas kernels: 82.4 us -> 284 us
  waiting for transfers between devices: 300 us -> 133 us
  matrix products: 131 us -> 0 us
  other arithmetic: 124 us -> 10.4 us
  starting transfers between devices: 202 us -> 99.8 us
  local copies, waits for them, and re-layouts: 130 us -> 35.2 us
    pallas_call x0 -> x39, Pallas kernels: none -> 216 us  [the longest x6 92.4 us: row_call(): pl.pallas_call(kernel, grid=(count,), in_specs=[pl.BlockSpec((size, item....]
    ppermute x36 -> x19, waiting for transfers between devices: 231 us -> 40.4 us  [move(): return lax.ppermute(values, FSDP, pairs)]
    dot_general x12 -> x0, matrix products: 131 us -> none  [dot(): lax.dot_general(left, right, dims, preferred_element_type=jnp.float32)]
    ppermute x36 -> x19, starting transfers between devices: 116 us -> 53.2 us  [move(): return lax.ppermute(values, FSDP, pairs)]
    unnamed x9 -> x1, other arithmetic: 46.6 us -> 0.69 us
    unnamed x148 -> x93, local copies, waits for them, and re-layouts: 60.6 us -> 24.4 us
    ppermute x41 -> x32, starting transfers between devices: 61.9 us -> 27.4 us  [swap(): lax.ppermute(values, axis, [(place, place ^ bit) for place in range(size)])]
    convert_element_type x16 -> x0, other arithmetic: 24 us -> none  [the longest x6 12.2 us: collapse(): send = add(block(size - step + place), upward).astype(jnp.bfloat16)]
  transfers between devices with their start and end apart: 83 -> 56, of which waited for: 26 -> 18; matrix products, arithmetic and copies ran while one was open for 33% -> 4% of each run, Pallas kernels for 8% -> 49%
where the time goes in v2:
time: 574 us; the launch traced here: 565 us
  Pallas kernels  284 us (49%)
  waiting for transfers between devices  133 us (23%)
  starting transfers between devices  99.8 us (17%)
  local copies, waits for them, and re-layouts  35.2 us (6%)
  other arithmetic  10.4 us (2%)
    pallas_call x6, Pallas kernels, row_call(): pl.pallas_call(kernel, grid=(count,), in_specs=[pl.BlockSpec((size, item....  92.4 us
    ppermute x32, waiting for transfers between devices, swap(): lax.ppermute(values, axis, [(place, place ^ bit) for place in range(size)])  79.2 us
    pallas_call x2, Pallas kernels, attention(): pl.pallas_call(attention_kernel, grid_spec=pltpu.PrefetchScalarGridSpec(n...  67.9 us
    ppermute x19, starting transfers between devices, move(): return lax.ppermute(values, FSDP, pairs)  53.2 us
    pallas_call x6, Pallas kernels, grad_pieces(): pl.pallas_call(functools.partial(grad_kernel, [len(rights) for _, rights...  47.3 us
    ppermute x19, waiting for transfers between devices, move(): return lax.ppermute(values, FSDP, pairs)  40.4 us
    pallas_call x14, Pallas kernels, pointwise(): pl.pallas_call(kernel, grid=(1,), in_specs=[pl.BlockSpec(memory_space=plt...  39.9 us
    ppermute x32, starting transfers between devices, swap(): lax.ppermute(values, axis, [(place, place ^ bit) for place in range(size)])  27.4 us
  transfers between devices with their start and end apart: 56, of which 18 were waited for; matrix products, arithmetic and copies ran while one was open for 4% of the time, Pallas kernels for 49%

profile of v2, /device:TPU:0, one launch (start us, length us, event | category | flops | bytes accessed | tf_op | source)
XLA Modules:
  0.0 564.8 jit_solution(3369822289603080500)
XLA Ops:
  9.6 13.8 %all-to-all-done = bf16[4,128,1024]{2,1,0:T(8,128)(2,1)} async-done(((bf16[4,128,1024]{2,1,0:T(8,128)(2,1)}), bf16[4,128,1024]{2,1,0:T(8,128)(2,1)}, u32[]{:S(2)}, u32[]{:S(2)}) %all-to-all-start) | async-done | bytes 1048608 | tf_op jit(solution)/shard_map/all_to_all | solution.py:854
  36.4 37.8 %collective-permute-done.refs_1_ = bf16[512,1024]{1,0:T(8,128)(2,1)} collective-permute-done((bf16[512,1024]{1,0:T(8,128)(2,1)}, bf16[512,1024]{1,0:T(8,128)(2,1)}, u32[]{:S(2)}, u32[]{:S(2)}) %collective-permute-start) | collective-permute-done | bytes 1048608 | tf_op jit(solution)/shard_map/fsdp_1/ppermute | solution.py:530
  89.8 5.9 %stack.2.refs_3_ = bf16[2048,2048]{1,0:T(8,128)(2,1)} custom-call(bf16[512,2048]{1,0:T(8,128)(2,1)S(1)} %pad_maximum_fusion.refs_0_, bf16[512,2048]{1,0:T(8,128)(2,1)} %collective-permute-done.2.refs_1_, bf16[512,2048]{1,0:T(8,128)(2,1)} %collective-permute-done.3.refs_2_, bf16[512,2048]{1,0:T(8,128)(2,1)} %collective-permute-done.4.refs_3_, ...), custom_call_target="tpu_custom_call" | custom-call | tf_op jit(solution)/shard_map/stack/pallas_call | solution.py:432
  95.8 6.0 %stack.3.refs_3_ = bf16[2048,2048]{1,0:T(8,128)(2,1)} custom-call(bf16[512,2048]{1,0:T(8,128)(2,1)S(1)} %pad_maximum_fusion.refs_0_, bf16[512,2048]{1,0:T(8,128)(2,1)} %collective-permute-done.2.refs_1_, bf16[512,2048]{1,0:T(8,128)(2,1)} %collective-permute-done.3.refs_2_, bf16[512,2048]{1,0:T(8,128)(2,1)} %collective-permute-done.4.refs_3_, ...), custom_call_target="tpu_custom_call" | custom-call | tf_op jit(solution)/shard_map/stack/pallas_call | solution.py:432
  101.7 6.5 %collective-permute-done.6.refs_0_ = bf16[256,2048]{1,0:T(8,128)(2,1)} collective-permute-done((bf16[256,2048]{1,0:T(8,128)(2,1)}, bf16[256,2048]{1,0:T(8,128)(2,1)}, u32[]{:S(2)}, u32[]{:S(2)}) %collective-permute-start.6) | collective-permute-done | bytes 1048608 | tf_op jit(solution)/shard_map/ctx_2/ppermute | solution.py:530
  131.4 15.4 %project.1 = (bf16[2048,256]{1,0:T(8,128)(2,1)}, bf16[2048,256]{1,0:T(8,128)(2,1)}, bf16[2048,256]{1,0:T(8,128)(2,1)}, bf16[256,2048]{1,0:T(8,128)(2,1)}, bf16[2...) custom-call(bf16[2048,2048]{1,0:T(8,128)(2,1)} %fill.3.normed.refs_0_, ...), custom_call_target="tpu_custom_call" | custom-call | tf_op jit(solution)/shard_map/project/pallas_call | solution.py:232
  147.4 34.0 %attention_0.1 = (bf16[2048,256]{1,0:T(8,128)(2,1)}, bf16[2048,256]{1,0:T(8,128)(2,1)}, bf16[2048,256]{1,0:T(8,128)(2,1)}, bf16[2048,256]{1,0:T(8,128)(2,1)}) custom-call(s32[8]{0:T(128)} %select_reduce_fusion.order, bf16[2048,256]{1,0:T(8,128)(2,1)} %get-tuple-element.289.query_in, bf16[2048,256]{1,0:T(8,128)(2,1)} %get-tuple-element.290.key_all, ...), custom_call_target="tpu_custom_call" | custom-call | tf_op jit(solution)/shard_map/attention_0/pallas_call | solution.py:182
  189.5 33.9 %attention_1.1 = (bf16[2048,256]{1,0:T(8,128)(2,1)}, bf16[2048,256]{1,0:T(8,128)(2,1)}, bf16[2048,256]{1,0:T(8,128)(2,1)}, bf16[2048,256]{1,0:T(8,128)(2,1)}) custom-call(s32[8]{0:T(128)} %select_reduce_fusion.order, bf16[2048,256]{1,0:T(8,128)(2,1)} %get-tuple-element.289.query_in, ...), custom_call_target="tpu_custom_call", output_to_operand_aliasing={{0}: (10, {}), {1}: (11, {}), {2}: (12, {}), {3}: (13, {})} | custom-call | tf_op jit(solution)/shard_map/attention_1/pallas_call | solution.py:182
  236.1 6.7 %collective-permute-start.21 = (bf16[512,1024]{1,0:T(8,128)(2,1)S(1)}, bf16[512,1024]{1,0:T(8,128)(2,1)}, u32[]{:S(2)}, u32[]{:S(2)}) collective-permute-start(bf16[512,1024]{1,0:T(8,128)(2,1)S(1)} %bitcast.31), channel_id=1, source_target_pairs={{0,8},{24,16},{1,9},{25,17},{2,10},{26,18},{3,11},{27,19},{4,12},{... | collective-permute-start | bytes 3145736 | tf_op jit(solution)/shard_map/line/ppermute | solution.py:543
  248.6 17.6 %hidden.1 = (bf16[2048,1024]{1,0:T(8,128)(2,1)S(1)}, bf16[2048,1024]{1,0:T(8,128)(2,1)}) custom-call(bf16[2048,2048]{1,0:T(8,128)(2,1)} %fill.3.normed.refs_0_, bf16[2048,1024]{1,0:T(8,128)(2,1)} %in_square.3.weight.refs_2_, f32[1,1024]{1,0:T(1,128)S(1)} %bitcast.46), custom_call_target="tpu_custom_call" | custom-call | tf_op jit(solution)/shard_map/hidden/pallas_call | solution.py:232
  266.2 12.1 %grad_1.3.refs_2_.refs_1_.refs_0_ = bf16[3,512,1024]{2,1,0:T(8,128)(2,1)} custom-call(s32[4]{0:T(128)S(1)} %fusion.7.turns, bf16[2048,2048]{1,0:T(8,128)(2,1)} %fill.3.normed.refs_0_, bf16[2048,256]{1,0:T(8,128)(2,1)S(1)} %copy-done.8, bf16[2048,256]{1,0:T(8,128)(2,1)S(1)} %copy-done.10, bf16[2048,256]{1,0:T(8,128)(2,1)S(1)} %copy-done.12, ...), custom_call_target="tpu_custom_call" | custom-call | tf_op jit(solution)/shard_map/grad_1/pallas_call | solution.py:375
  294.2 10.5 %grad_1.4.refs_2_.refs_1_.refs_0_ = bf16[3,512,1024]{2,1,0:T(8,128)(2,1)S(1)} custom-call(s32[4]{0:T(128)S(1)} %fusion.7.turns, bf16[2048,2048]{1,0:T(8,128)(2,1)} %fill.2.grads.refs_4_.refs_0_, bf16[2048,1024]{1,0:T(8,128)(2,1)} %copy-done.4), custom_call_target="tpu_custom_call" | custom-call | tf_op jit(solution)/shard_map/grad_1/pallas_call | solution.py:375
  306.4 11.6 %back.3 = (bf16[2048,2048]{1,0:T(8,128)(2,1)}, f32[3,256]{1,0:T(4,128)S(1)}) custom-call(bf16[2048,256]{1,0:T(8,128)(2,1)S(1)} %copy-done.8, bf16[2048,256]{1,0:T(8,128)(2,1)S(1)} %copy-done.10, bf16[2048,256]{1,0:T(8,128)(2,1)S(1)} %copy-done.12, bf16[2048,1024]{1,0:T(8,128)(2,1)} %in_square.2.weight.refs_3_), custom_call_target="tpu_custom_call" | custom-call | tf_op jit(solution)/shard_map/back/pallas_call | solution.py:232
  318.1 5.6 collective-permute-start.26
  333.8 12.9 %hidden_grad.1 = (bf16[2048,1024]{1,0:T(8,128)(2,1)S(1)}, f32[1,1024]{1,0:T(1,128)S(1)}) custom-call(bf16[2048,2048]{1,0:T(8,128)(2,1)} %fill.2.grads.refs_4_.refs_0_, bf16[2048,1024]{1,0:T(8,128)(2,1)} %get-tuple-element.372.slope, bf16[2048,1024]{1,0:T(8,128)(2,1)} %in_line.1.refs_2_.weight), custom_call_target="tpu_custom_call" | custom-call | tf_op jit(solution)/shard_map/hidden_grad/pallas_call | solution.py:232
  346.7 19.2 %back.4 = (bf16[1024,2048]{1,0:T(8,128)(2,1)S(1)}, bf16[1024,2048]{1,0:T(8,128)(2,1)}) custom-call(bf16[2048,1024]{1,0:T(8,128)(2,1)} %copy-done.4, bf16[2048,256]{1,0:T(8,128)(2,1)S(1)} %copy-done.14, bf16[2048,1024]{1,0:T(8,128)(2,1)} %in_line.1.refs_2_.weight, bf16[2048,1024]{1,0:T(8,128)(2,1)} %in_square.2.weight.refs_3_), custom_call_target="tpu_custom_call" | custom-call | tf_op jit(solution)/shard_map/back/pallas_call | solution.py:232
  367.0 7.3 %collective-permute-done.29.refs_1_.refs_3_.refs_4_ = bf16[1024,2048]{1,0:T(8,128)(2,1)} collective-permute-done((bf16[1024,2048]{1,0:T(8,128)(2,1)S(1)}, bf16[1024,2048]{1,0:T(8,128)(2,1)}, u32[]{:S(2)}, u32[]{:S(2)}) %collective-permute-start.29) | collective-permute-done | bytes 4194336 | tf_op jit(solution)/shard_map/ctx_1/ppermute | solution.py:530
  401.2 10.5 %grad_1.5.refs_6_.refs_1_.refs_2_.refs_0_ = bf16[3,512,1024]{2,1,0:T(8,128)(2,1)S(1)} custom-call(s32[4]{0:T(128)S(1)} %fusion.7.turns, bf16[2048,2048]{1,0:T(8,128)(2,1)} %fill.3.normed.refs_0_, bf16[2048,1024]{1,0:T(8,128)(2,1)} %copy-done.5), custom_call_target="tpu_custom_call" | custom-call | tf_op jit(solution)/shard_map/grad_1/pallas_call | solution.py:375
  413.4 15.7 %back.5 = (bf16[1024,2048]{1,0:T(8,128)(2,1)}, bf16[1024,2048]{1,0:T(8,128)(2,1)}) custom-call(bf16[2048,1024]{1,0:T(8,128)(2,1)} %copy-done.5, bf16[2048,2048]{1,0:T(8,128)(2,1)} %get-tuple-element.395.refs_1_, bf16[2048,1024]{1,0:T(8,128)(2,1)} %in_square.3.weight.refs_2_), custom_call_target="tpu_custom_call" | custom-call | tf_op jit(solution)/shard_map/back/pallas_call | solution.py:232
  445.9 12.2 %collective-permute-done.40.refs_4_ = bf16[128,2048]{1,0:T(8,128)(2,1)S(1)} collective-permute-done((bf16[128,2048]{1,0:T(8,128)(2,1)S(1)}, bf16[128,2048]{1,0:T(8,128)(2,1)S(1)}, u32[]{:S(2)}, u32[]{:S(2)}) %collective-permute-start.40) | collective-permute-done | bytes 524320 | tf_op jit(solution)/shard_map/tp_1/ppermute | solution.py:530
  468.6 18.4 %collective-permute-done.37.refs_1_.refs_3_ = bf16[1024,1024]{1,0:T(8,128)(2,1)S(1)} collective-permute-done((bf16[1024,1024]{1,0:T(8,128)(2,1)}, bf16[1024,1024]{1,0:T(8,128)(2,1)S(1)}, u32[]{:S(2)}, u32[]{:S(2)}) %collective-permute-start.37) | collective-permute-done | bytes 2097184 | tf_op jit(solution)/shard_map/line/ppermute | solution.py:543
  487.0 6.3 %collective-permute-done.38.refs_2_.refs_4_ = bf16[1024,1024]{1,0:T(8,128)(2,1)} collective-permute-done((bf16[1024,1024]{1,0:T(8,128)(2,1)}, bf16[1024,1024]{1,0:T(8,128)(2,1)}, u32[]{:S(2)}, u32[]{:S(2)}) %collective-permute-start.38) | collective-permute-done | bytes 2097184 | tf_op jit(solution)/shard_map/line/ppermute | solution.py:543
  511.8 5.7 %tokens_grad.1 = (f32[256,2048]{1,0:T(8,128)}, f32[3,2048]{1,0:T(4,128)S(1)}) custom-call(bf16[256,2048]{1,0:T(8,128)(2,1)S(1)} %bitcast.29, bf16[256,2048]{1,0:T(8,128)(2,1)S(1)} %bitcast.41, bf16[1,2048]{1,0:T(2,128)(2,1)S(1)} %broadcast_in_dim.75.refs_2_, bf16[1024,2048]{1,0:T(8,128)(2,1)} %get-tuple-element.437.refs_0_.refs_2_.refs_3_, ...), custom_call_target="tpu_custom_call" | custom-call | tf_op jit(solution)/shard_map/tokens_grad/pallas_call | solution.py:404
  525.0 7.6 %collective-permute-done.45.refs_1_ = bf16[512,1024]{1,0:T(8,128)(2,1)} collective-permute-done((bf16[512,1024]{1,0:T(8,128)(2,1)}, bf16[512,1024]{1,0:T(8,128)(2,1)}, u32[]{:S(2)}, u32[]{:S(2)}) %collective-permute-start.45) | collective-permute-done | bytes 1048608 | tf_op jit(solution)/shard_map/line/ppermute | solution.py:543
  (268 shorter events, 229.5 us)
Async XLA Ops:
  23.4 53.3 %collective-permute-start.2 = (bf16[512,2048]{1,0:T(8,128)(2,1)S(1)}, bf16[512,2048]{1,0:T(8,128)(2,1)}, u32[]{:S(2)}, u32[]{:S(2)}) collective-permute-start(bf16[512,2048]{1,0:T(8,128)(2,1)S(1)} %pad_maximum_fusion.refs_0_), channel_id=1, source_target_pairs={{0,1},{1,0},{2,3},{3,2},{4,5},{5,4},{6,7},{7,6},{8,9},{9,8},{10,11... | collective-permute-start | bytes 6291464 | tf_op jit(solution)/shard_map/tp_1/ppermute | solution.py:530
  25.7 51.0 %collective-permute-start.3 = (bf16[512,2048]{1,0:T(8,128)(2,1)S(1)}, bf16[512,2048]{1,0:T(8,128)(2,1)}, u32[]{:S(2)}, u32[]{:S(2)}) collective-permute-start(bf16[512,2048]{1,0:T(8,128)(2,1)S(1)} %pad_maximum_fusion.refs_0_), channel_id=1, source_target_pairs={{0,4},{2,6},{4,0},{6,2},{1,5},{3,7},{5,1},{7,3},{8,12},{10,14},{12... | collective-permute-start | bytes 6291464 | tf_op jit(solution)/shard_map/ctx_2/ppermute | solution.py:530
  26.0 50.6 %collective-permute-start.4 = (bf16[512,2048]{1,0:T(8,128)(2,1)S(1)}, bf16[512,2048]{1,0:T(8,128)(2,1)}, u32[]{:S(2)}, u32[]{:S(2)}) collective-permute-start(bf16[512,2048]{1,0:T(8,128)(2,1)S(1)} %pad_maximum_fusion.refs_0_), channel_id=1, source_target_pairs={{0,2},{2,0},{4,6},{6,4},{1,3},{3,1},{5,7},{7,5},{8,10},{10,8},{12,... | collective-permute-start | bytes 6291464 | tf_op jit(solution)/shard_map/ctx_1/ppermute | solution.py:530
  26.0 48.2 %collective-permute-start = (bf16[512,1024]{1,0:T(8,128)(2,1)}, bf16[512,1024]{1,0:T(8,128)(2,1)}, u32[]{:S(2)}, u32[]{:S(2)}) collective-permute-start(bf16[512,1024]{1,0:T(8,128)(2,1)} %bitcast.2.refs_0_), channel_id=1, source_target_pairs={{0,8},{8,0},{16,24},{24,16},{1,9},{9,1},{17,25},{25,17},{2,10},{10... | collective-permute-start | bytes 3145736 | tf_op jit(solution)/shard_map/fsdp_1/ppermute | solution.py:530
  27.6 49.0 %collective-permute-start.1 = (bf16[512,1024]{1,0:T(8,128)(2,1)}, bf16[512,1024]{1,0:T(8,128)(2,1)}, u32[]{:S(2)}, u32[]{:S(2)}) collective-permute-start(bf16[512,1024]{1,0:T(8,128)(2,1)} %bitcast.2.refs_0_), channel_id=1, source_target_pairs={{0,16},{8,24},{16,0},{24,8},{1,17},{9,25},{17,1},{25,9},{2,18},{10... | collective-permute-start | bytes 3145736 | tf_op jit(solution)/shard_map/fsdp_2/ppermute | solution.py:530
  119.1 62.3 %collective-permute-start.14 = (bf16[512,1024]{1,0:T(8,128)(2,1)}, bf16[512,1024]{1,0:T(8,128)(2,1)S(1)}, u32[]{:S(2)}, u32[]{:S(2)}) collective-permute-start(bf16[512,1024]{1,0:T(8,128)(2,1)} %bitcast.5.refs_0_), channel_id=1, source_target_pairs={{0,8},{8,0},{16,24},{24,16},{1,9},{9,1},{17,25},{25,17},{2,10},{10... | collective-permute-start | bytes 3145736 | tf_op jit(solution)/shard_map/fsdp_1/ppermute | solution.py:530
  119.6 61.8 %collective-permute-start.15 = (bf16[512,1024]{1,0:T(8,128)(2,1)}, bf16[512,1024]{1,0:T(8,128)(2,1)}, u32[]{:S(2)}, u32[]{:S(2)}) collective-permute-start(bf16[512,1024]{1,0:T(8,128)(2,1)} %bitcast.5.refs_0_), channel_id=1, source_target_pairs={{0,16},{8,24},{16,0},{24,8},{1,17},{9,25},{17,1},{25,9},{2,18},{10... | collective-permute-start | bytes 3145736 | tf_op jit(solution)/shard_map/fsdp_2/ppermute | solution.py:530
  122.2 59.2 %all-to-all-start.2 = ((bf16[4,128,1024]{2,1,0:T(8,128)(2,1)}), bf16[4,128,1024]{2,1,0:T(8,128)(2,1)S(1)}, u32[]{:S(2)}, u32[]{:S(2)}) async-start(bf16[4,128,1024]{2,1,0:T(8,128)(2,1)} %pieces.4), calls=%async_computation.2 | async-start | bytes 2097152 | tf_op jit(solution)/shard_map/all_to_all | solution.py:854
  181.4 52.1 %collective-permute-start.16 = (bf16[512,1024]{1,0:T(8,128)(2,1)S(1)}, bf16[512,1024]{1,0:T(8,128)(2,1)}, u32[]{:S(2)}, u32[]{:S(2)}) collective-permute-start(bf16[512,1024]{1,0:T(8,128)(2,1)S(1)} %bitcast.33), channel_id=1, source_target_pairs={{0,8},{8,16},{16,24},{1,9},{9,17},{17,25},{2,10},{10,18},{18,26},{... | collective-permute-start | bytes 3145736 | tf_op jit(solution)/shard_map/line/ppermute | solution.py:543
  184.4 49.2 %collective-permute-start.17 = (bf16[512,1024]{1,0:T(8,128)(2,1)S(1)}, bf16[512,1024]{1,0:T(8,128)(2,1)}, u32[]{:S(2)}, u32[]{:S(2)}) collective-permute-start(bf16[512,1024]{1,0:T(8,128)(2,1)S(1)} %bitcast.34), channel_id=1, source_target_pairs={{8,0},{16,8},{24,16},{9,1},{17,9},{25,17},{10,2},{18,10},{26,18},{... | collective-permute-start | bytes 3145736 | tf_op jit(solution)/shard_map/line/ppermute | solution.py:543
  186.1 48.0 %collective-permute-start.18 = (bf16[512,1024]{1,0:T(8,128)(2,1)}, bf16[512,1024]{1,0:T(8,128)(2,1)}, u32[]{:S(2)}, u32[]{:S(2)}) collective-permute-start(bf16[512,1024]{1,0:T(8,128)(2,1)} %collective-permute-done.15.refs_2_), channel_id=1, source_target_pairs={{0,8},{8,0},{16,24},{24,16},{1,9},{9,1},{17,25},{25,17},{2,10},{10... | collective-permute-start | bytes 3145736 | tf_op jit(solution)/shard_map/fsdp_1/ppermute | solution.py:530
  234.1 44.2 %collective-permute-start.19 = (bf16[512,1024]{1,0:T(8,128)(2,1)}, bf16[512,1024]{1,0:T(8,128)(2,1)S(1)}, u32[]{:S(2)}, u32[]{:S(2)}) collective-permute-start(bf16[512,1024]{1,0:T(8,128)(2,1)} %collective-permute-done.16.refs_1_), channel_id=1, source_target_pairs={{8,16},{16,24},{9,17},{17,25},{10,18},{18,26},{11,19},{19,27},{12,... | collective-permute-start | bytes 3145736 | tf_op jit(solution)/shard_map/line/ppermute | solution.py:543
  234.8 43.5 %collective-permute-start.20 = (bf16[512,1024]{1,0:T(8,128)(2,1)}, bf16[512,1024]{1,0:T(8,128)(2,1)}, u32[]{:S(2)}, u32[]{:S(2)}) collective-permute-start(bf16[512,1024]{1,0:T(8,128)(2,1)} %collective-permute-done.17.refs_2_), channel_id=1, source_target_pairs={{8,0},{16,8},{9,1},{17,9},{10,2},{18,10},{11,3},{19,11},{12,4},{20... | collective-permute-start | bytes 3145736 | tf_op jit(solution)/shard_map/line/ppermute | solution.py:543
  236.1 42.2 %collective-permute-start.21 = (bf16[512,1024]{1,0:T(8,128)(2,1)S(1)}, bf16[512,1024]{1,0:T(8,128)(2,1)}, u32[]{:S(2)}, u32[]{:S(2)}) collective-permute-start(bf16[512,1024]{1,0:T(8,128)(2,1)S(1)} %bitcast.31), channel_id=1, source_target_pairs={{0,8},{24,16},{1,9},{25,17},{2,10},{26,18},{3,11},{27,19},{4,12},{... | collective-permute-start | bytes 3145736 | tf_op jit(solution)/shard_map/line/ppermute | solution.py:543
  278.3 39.7 %collective-permute-start.22 = (bf16[512,1024]{1,0:T(8,128)(2,1)S(1)}, bf16[512,1024]{1,0:T(8,128)(2,1)}, u32[]{:S(2)}, u32[]{:S(2)}) collective-permute-start(bf16[512,1024]{1,0:T(8,128)(2,1)S(1)} %collective-permute-done.19.refs_3_), channel_id=1, source_target_pairs={{16,24},{17,25},{18,26},{19,27},{20,28},{21,29},{22,30},{23,31}} | collective-permute-start | bytes 3145736 | tf_op jit(solution)/shard_map/line/ppermute | solution.py:543
  318.1 47.8 %collective-permute-start.26 = (bf16[512,1024]{1,0:T(8,128)(2,1)S(1)}, bf16[512,1024]{1,0:T(8,128)(2,1)S(1)}, u32[]{:S(2)}, u32[]{:S(2)}) collective-permute-start(bf16[512,1024]{1,0:T(8,128)(2,1)S(1)} %bitcast.37), channel_id=1, source_target_pairs={{0,8},{24,16},{1,9},{25,17},{2,10},{26,18},{3,11},{27,19},{4,12},{... | collective-permute-start | bytes 3145736 | tf_op jit(solution)/shard_map/line/ppermute | solution.py:543
  327.1 40.0 %collective-permute-start.27 = (bf16[512,1024]{1,0:T(8,128)(2,1)}, bf16[512,1024]{1,0:T(8,128)(2,1)S(1)}, u32[]{:S(2)}, u32[]{:S(2)}) collective-permute-start(bf16[512,1024]{1,0:T(8,128)(2,1)} %get-tuple-element.370), channel_id=1, source_target_pairs={{0,8},{8,16},{16,24},{1,9},{9,17},{17,25},{2,10},{10,18},{18,26},{... | collective-permute-start | bytes 3145736 | tf_op jit(solution)/shard_map/line/ppermute | solution.py:543
  328.4 38.6 %collective-permute-start.28 = (bf16[512,1024]{1,0:T(8,128)(2,1)}, bf16[512,1024]{1,0:T(8,128)(2,1)S(1)}, u32[]{:S(2)}, u32[]{:S(2)}) collective-permute-start(bf16[512,1024]{1,0:T(8,128)(2,1)} %get-tuple-element.371), channel_id=1, source_target_pairs={{8,0},{16,8},{24,16},{9,1},{17,9},{25,17},{10,2},{18,10},{26,18},{... | collective-permute-start | bytes 3145736 | tf_op jit(solution)/shard_map/line/ppermute | solution.py:543
  381.8 47.3 %collective-permute-start.34 = (bf16[512,1024]{1,0:T(8,128)(2,1)S(1)}, bf16[512,1024]{1,0:T(8,128)(2,1)S(1)}, u32[]{:S(2)}, u32[]{:S(2)}) collective-permute-start(bf16[512,1024]{1,0:T(8,128)(2,1)S(1)} %second.3), channel_id=1, source_target_pairs={{0,8},{8,16},{1,9},{9,17},{2,10},{10,18},{3,11},{11,19},{4,12},{12... | collective-permute-start | bytes 3145736 | tf_op jit(solution)/shard_map/line/ppermute | solution.py:543
  386.5 42.7 %collective-permute-start.35 = (bf16[512,1024]{1,0:T(8,128)(2,1)S(1)}, bf16[512,1024]{1,0:T(8,128)(2,1)S(1)}, u32[]{:S(2)}, u32[]{:S(2)}) collective-permute-start(bf16[512,1024]{1,0:T(8,128)(2,1)S(1)} %second.3), channel_id=1, source_target_pairs={{16,8},{24,16},{17,9},{25,17},{18,10},{26,18},{19,11},{27,19},{20,... | collective-permute-start | bytes 3145736 | tf_op jit(solution)/shard_map/line/ppermute | solution.py:543
  391.7 39.1 %collective-permute-start.36 = (bf16[512,1024]{1,0:T(8,128)(2,1)S(1)}, bf16[512,1024]{1,0:T(8,128)(2,1)S(1)}, u32[]{:S(2)}, u32[]{:S(2)}) collective-permute-start(bf16[512,1024]{1,0:T(8,128)(2,1)S(1)} %bitcast.43), channel_id=1, source_target_pairs={{0,8},{24,16},{1,9},{25,17},{2,10},{26,18},{3,11},{27,19},{4,12},{... | collective-permute-start | bytes 3145736 | tf_op jit(solution)/shard_map/line/ppermute | solution.py:543
  436.7 50.2 %collective-permute-start.37 = (bf16[1024,1024]{1,0:T(8,128)(2,1)}, bf16[1024,1024]{1,0:T(8,128)(2,1)S(1)}, u32[]{:S(2)}, u32[]{:S(2)}) collective-permute-start(bf16[1024,1024]{1,0:T(8,128)(2,1)} %get-tuple-element.413), channel_id=1, source_target_pairs={{0,8},{8,16},{16,24},{1,9},{9,17},{17,25},{2,10},{10,18},{18,26},{... | collective-permute-start | bytes 6291464 | tf_op jit(solution)/shard_map/line/ppermute | solution.py:543
  441.2 52.0 %collective-permute-start.38 = (bf16[1024,1024]{1,0:T(8,128)(2,1)}, bf16[1024,1024]{1,0:T(8,128)(2,1)}, u32[]{:S(2)}, u32[]{:S(2)}) collective-permute-start(bf16[1024,1024]{1,0:T(8,128)(2,1)} %get-tuple-element.414), channel_id=1, source_target_pairs={{8,0},{16,8},{24,16},{9,1},{17,9},{25,17},{10,2},{18,10},{26,18},{... | collective-permute-start | bytes 6291464 | tf_op jit(solution)/shard_map/line/ppermute | solution.py:543
  496.7 41.2 %all-to-all-start.3 = ((bf16[4,256,1024]{2,1,0:T(8,128)(2,1)}), bf16[4,256,1024]{2,1,0:T(8,128)(2,1)S(1)}, u32[]{:S(2)}, u32[]{:S(2)}) async-start(bf16[4,256,1024]{2,1,0:T(8,128)(2,1)} %pad_maximum_fusion.1), calls=%async_computation.3 | async-start | bytes 4194304 | tf_op jit(solution)/shard_map/all_to_all | solution.py:854
  (77 other events, 1011.0 us)

commit v3 on v2

--- a/solution.py
+++ b/solution.py
@@ -361,7 +361,7 @@
             at += columns
 
 
-def grad_pieces(products, turns, first, count, width):
+def grad_pieces(products, turns, first, count, width, mebibytes=48):
     size = lax.axis_size(FSDP)
     specs, items, columns = [], [], 0
     for left, rights in products:
@@ -381,7 +381,7 @@
             out_specs=pl.BlockSpec((1, rows, columns), lambda at, turns: (at, 0, 0)),
         ),
         out_shape=jax.ShapeDtypeStruct((count, rows, columns), jnp.bfloat16),
-        compiler_params=params(),
+        compiler_params=params(mebibytes),
         cost_estimate=NO_COST,
         name=f"grad_{first}",
     )(turns, *items)
@@ -649,7 +649,7 @@
     upward, downward = pointwise(
         "third", choose, [place], inputs, [(shape, jnp.bfloat16)] * 2
     )
-    return [move(upward, UP), move(downward, DOWN)]
+    return [move(upward, UP), move(downward, DOWN)], upward
 
 
 def reduce_last(parts, got, index=0):
@@ -795,6 +795,10 @@
     return lax.optimization_barrier((values,) + after)[0]
 
 
+def hold(values, *after):
+    return lax.optimization_barrier((values,) + after)[0]
+
+
 def tick(live):
     vars(live).update(lax.optimization_barrier(dict(vars(live))))
 
@@ -812,17 +816,17 @@
     )(place, *items)
 
 
-def small_call(name, kernel, items, shapes, kind):
+def small_call(name, kernel, items, shapes, kind, *places):
     vmem = pl.BlockSpec(memory_space=pltpu.VMEM)
     return pl.pallas_call(
         kernel,
-        in_specs=[vmem] * len(items),
+        in_specs=[pl.BlockSpec(memory_space=pltpu.SMEM)] * len(places) + [vmem] * len(items),
         out_specs=[vmem] * len(shapes),
         out_shape=[jax.ShapeDtypeStruct(shape, kind) for shape in shapes],
         compiler_params=params(),
         cost_estimate=NO_COST,
         name=name,
-    )(*items)
+    )(*places, *items)
 
 
 def pieces(kind, *sources):
@@ -850,6 +854,43 @@
     return small_call("pieces", kernel, sources, [(parts, rows, columns)], sources[0].dtype)[0]
 
 
+def near_pieces(kind, *sources):
+    parts = lax.axis_size(CTX)
+    place = lax.axis_index(CTX).astype(jnp.int32)
+    sent = pieces(kind, *sources) if sources[-1].shape[0] // parts % PAIR else None
+    if sent is not None:
+        return [lax.dynamic_index_in_dim(sent, place ^ r, 0, False) for r in range(parts)]
+    rows, width = sources[1].shape[1], sources[1].shape[0] // parts
+
+    def kernel(place, qkv, out, *targets):
+        for r, target in enumerate(targets):
+            here = pl.ds(pl.multiple_of((place[0] ^ r) * width, width), width)
+            for which in range(3):
+                target[:, which * width : (which + 1) * width] = qkv[which, :, here]
+            target[:, 3 * width :] = out[here, :].T
+
+    return small_call(
+        "pieces", kernel, sources, [(rows, 4 * width)] * parts, sources[0].dtype, place.reshape(1)
+    )
+
+
+def near_trade(sent):
+    return [sent[0]] + [swap(sent[r], CTX, r) for r in range(1, len(sent))]
+
+
+def laid(received):
+    def kernel(place, *refs):
+        *sources, target = refs
+        for r, source in enumerate(sources):
+            rows = source.shape[0]
+            target[pl.ds(pl.multiple_of((place[0] ^ r) * rows, rows), rows), :] = source[...]
+
+    rows, columns = received[0].shape
+    place = lax.axis_index(CTX).astype(jnp.int32).reshape(1)
+    shape = (len(received) * rows, columns)
+    return small_call("laid", kernel, received, [shape], received[0].dtype, place)[0]
+
+
 def trade(sent):
     return lax.all_to_all(sent, CTX, 0, 0, tiled=True)
 
@@ -859,10 +900,26 @@
     return got.reshape(-1, got.shape[2])
 
 
-def trade_back(*summed):
-    parts = lax.axis_size(CTX)
-    split = [item.reshape(parts, -1, item.shape[1]) for item in summed]
-    return trade(split[0] if len(split) == 1 else jnp.concatenate(split, axis=1))
+def trade_back(summed):
+    return trade(summed.reshape(lax.axis_size(CTX), -1, summed.shape[1]))
+
+
+def last_beside(other, parts, got):
+    first, rest = parts
+    count = lax.axis_size(CTX)
+    rows, columns = first.shape[0] // count, first.shape[1]
+
+    def choose(other, last, *got):
+        total = (sum_of(last)[0] + sum_of(*got)).reshape(count, rows, columns)
+        return [jnp.concatenate([sum_of(other).reshape(count, rows, columns), total], axis=1)]
+
+    return pointwise(
+        "last",
+        choose,
+        [],
+        [other, (rest, 1, 2)] + [(item, first.shape[0], 0) for item in got],
+        [((count, 2 * rows, columns), jnp.bfloat16)],
+    )[0]
 
 
 def finish(received, kind, index=0, count=1):
@@ -946,14 +1003,16 @@
     turns = jnp.array(TURNS, jnp.int32)[place]
     place = place.astype(jnp.int32).reshape(1)
 
-    def first_grad(columns, *products):
-        return grad_pieces(products, turns, 0, 1, columns)[0]
+    def first_grad(columns, *products, mebibytes=48):
+        return grad_pieces(products, turns, 0, 1, columns, mebibytes)[0]
 
     def later_grads(columns, *products):
         return [grad_pieces(products, turns, 1, 3, columns)]
 
     live = types.SimpleNamespace(
-        attention=gather_rows_of(pieces("attention", jnp.swapaxes(qkv_weight, 0, 1), out_weight)),
+        attention=laid(
+            near_trade(near_pieces("attention", jnp.swapaxes(qkv_weight, 0, 1), out_weight))
+        ),
         rows=jnp.concatenate([normed_own, cotangent[0]], axis=0),
         tokens=tokens[0],
         cotangent=cotangent[0],
@@ -1010,7 +1069,7 @@
     live.heads = heads
     attended, *head_grads = live.heads
     head_products = ((live.normed, head_grads), (live.grads, [attended]))
-    live.head_parts = [first_grad(width, *head_products)]
+    live.head_parts = [first_grad(width, *head_products, mebibytes=60)]
     tick(live)
     live.down = spread_second(live.down)
     live.head_sum = reduce_first(live.head_parts)
@@ -1036,7 +1095,7 @@
         list(live.heads[1:]), columns[:3], [live.attention], summing=True
     )
     tick(live)
-    live.head_sum = reduce_third(live.head_parts, live.head_sum, place)
+    live.head_sum, _ = reduce_third(live.head_parts, live.head_sum, place)
     live.down_sum = reduce_first(live.down_parts)
     live.down = in_line(live.down)
     live.hidden_grad, live.up_sums = row_call(
@@ -1055,22 +1114,23 @@
     )
     tick(live)
     live.down_sum = reduce_second([(live.down_parts, live.down_sum)], place)
-    far, near = live.branch
-    (live.branch,) = scatter_third(*scatter_second(scatter_first(near, far)))
     up_products = (live.normed, [live.hidden_grad])
     live.up_parts = [first_grad(units, up_products)]
     live.up_sum = reduce_first(live.up_parts)
+    far, near = live.branch
+    got = hold(scatter_first(near, far), live.up_parts[0])
+    (live.branch,) = scatter_third(*scatter_second(got))
     live.up_parts = live.up_parts + later_grads(units, up_products)
     live.normed_part = back(
         [live.hidden_grad], [everything], [live.up], live.normed_part, halves=True
     )
     tick(live)
-    live.down_sum = reduce_third(
+    live.down_sum, sent = reduce_third(
         live.down_parts, live.down_sum, place, (live.up_parts, live.up_sum)
     )
+    live.head_sum = reduce_last(live.head_parts, hold(live.head_sum, sent))
     far, near = live.normed_part
     (live.normed_part,) = scatter_third(*scatter_second(scatter_first(near, far)))
-    live.head_sum = reduce_last(live.head_parts, live.head_sum)
     live.sums = jnp.concatenate(
         [
             lax.dynamic_update_slice_in_dim(
@@ -1086,9 +1146,8 @@
     )
     tick(live)
     second = [(item, live.up_parts[0].shape[0], 1) for item in live.down_sum]
-    live.up_sum = reduce_third(live.up_parts, second, place)
-    down_sum = reduce_last(live.down_parts, live.down_sum)
-    live.both = trade_back(live.head_sum, down_sum)
+    live.up_sum, sent = reduce_third(live.up_parts, second, place)
+    live.both = trade(last_beside(live.head_sum, live.down_parts, hold(live.down_sum, sent)))
     live.tokens_grad, norm_sums = pointwise(
         "tokens_grad",
         tokens_grad_of,

time: 574 us -> 570 us (level)
  local copies, waits for them, and re-layouts: 35.2 us -> 26.8 us
  Pallas kernels: 284 us -> 292 us
    all_to_all x5 -> x4, waiting for transfers between devices: 13.8 us -> 0.01 us  [trade(): return lax.all_to_all(sent, CTX, 0, 0, tiled=True)]
    unnamed x93 -> x81, local copies, waits for them, and re-layouts: 24.4 us -> 15.5 us
    ppermute x32 -> x35, waiting for transfers between devices: 79.2 us -> 84.1 us  [swap(): lax.ppermute(values, axis, [(place, place ^ bit) for place in range(size)])]
    all_to_all x5 -> x4, starting transfers between devices: 19.2 us -> 15.9 us  [trade(): return lax.all_to_all(sent, CTX, 0, 0, tiled=True)]
    ppermute x32 -> x35, starting transfers between devices: 27.4 us -> 30.7 us  [swap(): lax.ppermute(values, axis, [(place, place ^ bit) for place in range(size)])]
  transfers between devices with their start and end apart: 56 -> 58, of which waited for: 18 -> 17; matrix products, arithmetic and copies ran while one was open for 4% -> 4% of each run, Pallas kernels for 49% -> 50%
where the time goes in v3:
time: 570 us; the launch traced here: 562 us
  Pallas kernels  292 us (51%)
  waiting for transfers between devices  128 us (22%)
  starting transfers between devices  100 us (18%)
  local copies, waits for them, and re-layouts  26.8 us (5%)
  other arithmetic  13 us (2%)
    pallas_call x6, Pallas kernels, row_call(): pl.pallas_call(kernel, grid=(count,), in_specs=[pl.BlockSpec((size, item....  93.2 us
    ppermute x35, waiting for transfers between devices, swap(): lax.ppermute(values, axis, [(place, place ^ bit) for place in range(size)])  84.1 us
    pallas_call x2, Pallas kernels, attention(): pl.pallas_call(attention_kernel, grid_spec=pltpu.PrefetchScalarGridSpec(n...  67.8 us
    ppermute x19, starting transfers between devices, move(): return lax.ppermute(values, FSDP, pairs)  53.5 us
    pallas_call x6, Pallas kernels, grad_pieces(): pl.pallas_call(functools.partial(grad_kernel, [len(rights) for _, rights...  50.5 us
    ppermute x19, waiting for transfers between devices, move(): return lax.ppermute(values, FSDP, pairs)  43.7 us
    pallas_call x14, Pallas kernels, pointwise(): pl.pallas_call(kernel, grid=(1,), in_specs=[pl.BlockSpec(memory_space=plt...  42.2 us
    ppermute x35, starting transfers between devices, swap(): lax.ppermute(values, axis, [(place, place ^ bit) for place in range(size)])  30.7 us
  transfers between devices with their start and end apart: 58, of which 17 were waited for; matrix products, arithmetic and copies ran while one was open for 4% of the time, Pallas kernels for 50%

profile of v3, /device:TPU:0, one launch (start us, length us, event | category | flops | bytes accessed | tf_op | source)
XLA Modules:
  0.0 561.6 jit_solution(10477540271562099936)
XLA Ops:
  26.4 5.6 fusion.6
  32.0 37.5 %collective-permute-done.3.refs_1_ = bf16[512,1024]{1,0:T(8,128)(2,1)S(1)} collective-permute-done((bf16[512,1024]{1,0:T(8,128)(2,1)S(1)}, bf16[512,1024]{1,0:T(8,128)(2,1)S(1)}, u32[]{:S(2)}, u32[]{:S(2)}) %collective-permute-start.3) | collective-permute-done | bytes 1048608 | tf_op jit(solution)/shard_map/fsdp_1/ppermute | solution.py:530
  83.3 6.2 %stack.2.refs_3_ = bf16[2048,2048]{1,0:T(8,128)(2,1)} custom-call(bf16[512,2048]{1,0:T(8,128)(2,1)} %pad_maximum_fusion.refs_0_, bf16[512,2048]{1,0:T(8,128)(2,1)} %collective-permute-done.5.refs_1_, bf16[512,2048]{1,0:T(8,128)(2,1)} %collective-permute-done.6.refs_2_, bf16[512,2048]{1,0:T(8,128)(2,1)} %collective-permute-done.7.refs_3_, ...), custom_call_target="tpu_custom_call" | custom-call | tf_op jit(solution)/shard_map/stack/pallas_call | solution.py:432
  89.5 6.2 %stack.3.refs_3_ = bf16[2048,2048]{1,0:T(8,128)(2,1)} custom-call(bf16[512,2048]{1,0:T(8,128)(2,1)} %pad_maximum_fusion.refs_0_, bf16[512,2048]{1,0:T(8,128)(2,1)} %collective-permute-done.5.refs_1_, bf16[512,2048]{1,0:T(8,128)(2,1)} %collective-permute-done.6.refs_2_, bf16[512,2048]{1,0:T(8,128)(2,1)} %collective-permute-done.7.refs_3_, ...), custom_call_target="tpu_custom_call" | custom-call | tf_op jit(solution)/shard_map/stack/pallas_call | solution.py:432
  95.7 7.8 %collective-permute-done.9.refs_0_ = bf16[256,2048]{1,0:T(8,128)(2,1)} collective-permute-done((bf16[256,2048]{1,0:T(8,128)(2,1)}, bf16[256,2048]{1,0:T(8,128)(2,1)}, u32[]{:S(2)}, u32[]{:S(2)}) %collective-permute-start.9) | collective-permute-done | bytes 1048608 | tf_op jit(solution)/shard_map/ctx_2/ppermute | solution.py:530
  127.7 15.4 %project.1 = (bf16[2048,256]{1,0:T(8,128)(2,1)}, bf16[2048,256]{1,0:T(8,128)(2,1)}, bf16[2048,256]{1,0:T(8,128)(2,1)}, bf16[256,2048]{1,0:T(8,128)(2,1)}, bf16[2...) custom-call(bf16[2048,2048]{1,0:T(8,128)(2,1)} %fill.3.normed.refs_0_, ...), custom_call_target="tpu_custom_call" | custom-call | tf_op jit(solution)/shard_map/project/pallas_call | solution.py:232
  143.7 33.9 %attention_0.1 = (bf16[2048,256]{1,0:T(8,128)(2,1)}, bf16[2048,256]{1,0:T(8,128)(2,1)}, bf16[2048,256]{1,0:T(8,128)(2,1)}, bf16[2048,256]{1,0:T(8,128)(2,1)}) custom-call(s32[8]{0:T(128)} %select_reduce_fusion.order, bf16[2048,256]{1,0:T(8,128)(2,1)} %get-tuple-element.303.query_in, bf16[2048,256]{1,0:T(8,128)(2,1)} %get-tuple-element.304.key_all, ...), custom_call_target="tpu_custom_call" | custom-call | tf_op jit(solution)/shard_map/attention_0/pallas_call | solution.py:182
  185.2 33.9 %attention_1.1 = (bf16[2048,256]{1,0:T(8,128)(2,1)}, bf16[2048,256]{1,0:T(8,128)(2,1)}, bf16[2048,256]{1,0:T(8,128)(2,1)}, bf16[2048,256]{1,0:T(8,128)(2,1)}) custom-call(s32[8]{0:T(128)} %select_reduce_fusion.order, bf16[2048,256]{1,0:T(8,128)(2,1)} %get-tuple-element.303.query_in, ...), custom_call_target="tpu_custom_call", output_to_operand_aliasing={{0}: (10, {}), {1}: (11, {}), {2}: (12, {}), {3}: (13, {})} | custom-call | tf_op jit(solution)/shard_map/attention_1/pallas_call | solution.py:182
  219.1 7.5 %grad_0.3 = bf16[1,512,1024]{2,1,0:T(8,128)(2,1)} custom-call(s32[4]{0:T(128)} %fusion.7.turns, bf16[2048,2048]{1,0:T(8,128)(2,1)} %fill.3.normed.refs_0_, bf16[2048,256]{1,0:T(8,128)(2,1)} %get-tuple-element.356.refs_1_.refs_0_, bf16[2048,256]{1,0:T(8,128)(2,1)} %get-tuple-element.357.refs_2_.refs_1_, bf16[2048,256]{1,0:T(8,128)(2,1)} %get-tuple-element.358.refs_3_.refs_2_, ...), custom_call_target="tpu_custom_call" | custom-call | tf_op jit(solution)/shard_map/grad_0/pallas_call | solution.py:375
  232.5 7.1 %collective-permute-start.24 = (bf16[512,1024]{1,0:T(8,128)(2,1)}, bf16[512,1024]{1,0:T(8,128)(2,1)}, u32[]{:S(2)}, u32[]{:S(2)}) collective-permute-start(bf16[512,1024]{1,0:T(8,128)(2,1)} %bitcast.29), channel_id=1, source_target_pairs={{0,8},{24,16},{1,9},{25,17},{2,10},{26,18},{3,11},{27,19},{4,12},{... | collective-permute-start | bytes 3145736 | tf_op jit(solution)/shard_map/line/ppermute | solution.py:543
  244.3 17.6 %hidden.1 = (bf16[2048,1024]{1,0:T(8,128)(2,1)S(1)}, bf16[2048,1024]{1,0:T(8,128)(2,1)}) custom-call(bf16[2048,2048]{1,0:T(8,128)(2,1)} %fill.3.normed.refs_0_, bf16[2048,1024]{1,0:T(8,128)(2,1)} %in_square.3.weight.refs_2_, f32[1,1024]{1,0:T(1,128)S(1)} %bitcast.41), custom_call_target="tpu_custom_call" | custom-call | tf_op jit(solution)/shard_map/hidden/pallas_call | solution.py:232
  261.9 12.4 %grad_1.3.refs_2_.refs_1_.refs_0_ = bf16[3,512,1024]{2,1,0:T(8,128)(2,1)} custom-call(s32[4]{0:T(128)S(1)} %copy-done.30, bf16[2048,2048]{1,0:T(8,128)(2,1)} %fill.3.normed.refs_0_, bf16[2048,256]{1,0:T(8,128)(2,1)S(1)} %copy-done.7, bf16[2048,256]{1,0:T(8,128)(2,1)S(1)} %copy-done.8, bf16[2048,256]{1,0:T(8,128)(2,1)S(1)} %copy-done.9, ...), custom_call_target="tpu_custom_call" | custom-call | tf_op jit(solution)/shard_map/grad_1/pallas_call | solution.py:375
  278.4 5.6 collective-permute-start.27
  289.7 10.5 %grad_1.4.refs_2_.refs_1_ = bf16[3,512,1024]{2,1,0:T(8,128)(2,1)S(1)} custom-call(s32[4]{0:T(128)S(1)} %copy-done.30, bf16[2048,2048]{1,0:T(8,128)(2,1)} %fill.2.grads.refs_4_.refs_0_, bf16[2048,1024]{1,0:T(8,128)(2,1)} %copy-done.4), custom_call_target="tpu_custom_call" | custom-call | tf_op jit(solution)/shard_map/grad_1/pallas_call | solution.py:375
  301.9 11.6 %back.3 = (bf16[2048,2048]{1,0:T(8,128)(2,1)}, f32[3,256]{1,0:T(4,128)S(1)}) custom-call(bf16[2048,256]{1,0:T(8,128)(2,1)S(1)} %copy-done.7, bf16[2048,256]{1,0:T(8,128)(2,1)S(1)} %copy-done.8, bf16[2048,256]{1,0:T(8,128)(2,1)S(1)} %copy-done.9, bf16[2048,1024]{1,0:T(8,128)(2,1)} %in_square.2.weight.refs_3_), custom_call_target="tpu_custom_call" | custom-call | tf_op jit(solution)/shard_map/back/pallas_call | solution.py:232
  329.5 12.9 %hidden_grad.1 = (bf16[2048,1024]{1,0:T(8,128)(2,1)S(1)}, f32[1,1024]{1,0:T(1,128)S(1)}) custom-call(bf16[2048,2048]{1,0:T(8,128)(2,1)} %fill.2.grads.refs_4_.refs_0_, bf16[2048,1024]{1,0:T(8,128)(2,1)} %get-tuple-element.386.slope, bf16[2048,1024]{1,0:T(8,128)(2,1)} %in_line.1.refs_2_.weight), custom_call_target="tpu_custom_call" | custom-call | tf_op jit(solution)/shard_map/hidden_grad/pallas_call | solution.py:232
  342.4 19.9 %back.4 = (bf16[1024,2048]{1,0:T(8,128)(2,1)}, bf16[1024,2048]{1,0:T(8,128)(2,1)}) custom-call(bf16[2048,1024]{1,0:T(8,128)(2,1)} %copy-done.4, bf16[2048,256]{1,0:T(8,128)(2,1)S(1)} %copy-done.10, bf16[2048,1024]{1,0:T(8,128)(2,1)} %in_line.1.refs_2_.weight, bf16[2048,1024]{1,0:T(8,128)(2,1)} %in_square.2.weight.refs_3_), custom_call_target="tpu_custom_call" | custom-call | tf_op jit(solution)/shard_map/back/pallas_call | solution.py:232
  392.7 10.5 %grad_1.5.refs_6_.refs_1_.refs_2_.refs_0_ = bf16[3,512,1024]{2,1,0:T(8,128)(2,1)S(1)} custom-call(s32[4]{0:T(128)S(1)} %copy-done.30, bf16[2048,2048]{1,0:T(8,128)(2,1)} %fill.3.normed.refs_0_, bf16[2048,1024]{1,0:T(8,128)(2,1)} %copy-done.5), custom_call_target="tpu_custom_call" | custom-call | tf_op jit(solution)/shard_map/grad_1/pallas_call | solution.py:375
  404.8 15.8 %back.5 = (bf16[1024,2048]{1,0:T(8,128)(2,1)}, bf16[1024,2048]{1,0:T(8,128)(2,1)}) custom-call(bf16[2048,1024]{1,0:T(8,128)(2,1)} %copy-done.5, bf16[2048,2048]{1,0:T(8,128)(2,1)} %get-tuple-element.411.refs_1_, bf16[2048,1024]{1,0:T(8,128)(2,1)} %in_square.3.weight.refs_2_), custom_call_target="tpu_custom_call" | custom-call | tf_op jit(solution)/shard_map/back/pallas_call | solution.py:232
  440.7 12.3 %collective-permute-done.43.refs_4_ = bf16[128,2048]{1,0:T(8,128)(2,1)S(1)} collective-permute-done((bf16[128,2048]{1,0:T(8,128)(2,1)S(1)}, bf16[128,2048]{1,0:T(8,128)(2,1)S(1)}, u32[]{:S(2)}, u32[]{:S(2)}) %collective-permute-start.43) | collective-permute-done | bytes 524320 | tf_op jit(solution)/shard_map/tp_1/ppermute | solution.py:530
  463.4 18.4 %collective-permute-done.40.refs_3_.refs_2_ = bf16[1024,1024]{1,0:T(8,128)(2,1)S(1)} collective-permute-done((bf16[1024,1024]{1,0:T(8,128)(2,1)}, bf16[1024,1024]{1,0:T(8,128)(2,1)S(1)}, u32[]{:S(2)}, u32[]{:S(2)}) %collective-permute-start.40) | collective-permute-done | bytes 2097184 | tf_op jit(solution)/shard_map/line/ppermute | solution.py:543
  481.8 6.3 %collective-permute-done.41.refs_4_.refs_3_ = bf16[1024,1024]{1,0:T(8,128)(2,1)} collective-permute-done((bf16[1024,1024]{1,0:T(8,128)(2,1)}, bf16[1024,1024]{1,0:T(8,128)(2,1)}, u32[]{:S(2)}, u32[]{:S(2)}) %collective-permute-start.41) | collective-permute-done | bytes 2097184 | tf_op jit(solution)/shard_map/line/ppermute | solution.py:543
  505.9 5.8 %tokens_grad.1 = (f32[256,2048]{1,0:T(8,128)}, f32[3,2048]{1,0:T(4,128)S(1)}) custom-call(bf16[256,2048]{1,0:T(8,128)(2,1)S(1)} %bitcast.27, bf16[256,2048]{1,0:T(8,128)(2,1)S(1)} %bitcast.37, bf16[1,2048]{1,0:T(2,128)(2,1)S(1)} %broadcast_in_dim.75.refs_2_, bf16[1024,2048]{1,0:T(8,128)(2,1)} %get-tuple-element.459.refs_0_.refs_2_.refs_3_, ...), custom_call_target="tpu_custom_call" | custom-call | tf_op jit(solution)/shard_map/tokens_grad/pallas_call | solution.py:404
  517.8 8.8 %collective-permute-done.48.refs_1_ = bf16[512,1024]{1,0:T(8,128)(2,1)} collective-permute-done((bf16[512,1024]{1,0:T(8,128)(2,1)}, bf16[512,1024]{1,0:T(8,128)(2,1)}, u32[]{:S(2)}, u32[]{:S(2)}) %collective-permute-start.48) | collective-permute-done | bytes 1048608 | tf_op jit(solution)/shard_map/line/ppermute | solution.py:543
  (260 shorter events, 230.1 us)
Async XLA Ops:
  18.5 53.5 %collective-permute-start.5 = (bf16[512,2048]{1,0:T(8,128)(2,1)}, bf16[512,2048]{1,0:T(8,128)(2,1)}, u32[]{:S(2)}, u32[]{:S(2)}) collective-permute-start(bf16[512,2048]{1,0:T(8,128)(2,1)} %pad_maximum_fusion.refs_0_), channel_id=1, source_target_pairs={{0,1},{1,0},{2,3},{3,2},{4,5},{5,4},{6,7},{7,6},{8,9},{9,8},{10,11... | collective-permute-start | bytes 6291464 | tf_op jit(solution)/shard_map/tp_1/ppermute | solution.py:530
  20.1 51.9 %collective-permute-start.6 = (bf16[512,2048]{1,0:T(8,128)(2,1)}, bf16[512,2048]{1,0:T(8,128)(2,1)}, u32[]{:S(2)}, u32[]{:S(2)}) collective-permute-start(bf16[512,2048]{1,0:T(8,128)(2,1)} %pad_maximum_fusion.refs_0_), channel_id=1, source_target_pairs={{0,4},{2,6},{4,0},{6,2},{1,5},{3,7},{5,1},{7,3},{8,12},{10,14},{12... | collective-permute-start | bytes 6291464 | tf_op jit(solution)/shard_map/ctx_2/ppermute | solution.py:530
  21.6 50.4 %collective-permute-start.7 = (bf16[512,2048]{1,0:T(8,128)(2,1)}, bf16[512,2048]{1,0:T(8,128)(2,1)}, u32[]{:S(2)}, u32[]{:S(2)}) collective-permute-start(bf16[512,2048]{1,0:T(8,128)(2,1)} %pad_maximum_fusion.refs_0_), channel_id=1, source_target_pairs={{0,2},{2,0},{4,6},{6,4},{1,3},{3,1},{5,7},{7,5},{8,10},{10,8},{12,... | collective-permute-start | bytes 6291464 | tf_op jit(solution)/shard_map/ctx_1/ppermute | solution.py:530
  21.6 47.9 %collective-permute-start.3 = (bf16[512,1024]{1,0:T(8,128)(2,1)S(1)}, bf16[512,1024]{1,0:T(8,128)(2,1)S(1)}, u32[]{:S(2)}, u32[]{:S(2)}) collective-permute-start(bf16[512,1024]{1,0:T(8,128)(2,1)S(1)} %laid.1.refs_0_), channel_id=1, source_target_pairs={{0,8},{8,0},{16,24},{24,16},{1,9},{9,1},{17,25},{25,17},{2,10},{10... | collective-permute-start | bytes 3145736 | tf_op jit(solution)/shard_map/fsdp_1/ppermute | solution.py:530
  23.2 48.8 %collective-permute-start.4 = (bf16[512,1024]{1,0:T(8,128)(2,1)S(1)}, bf16[512,1024]{1,0:T(8,128)(2,1)}, u32[]{:S(2)}, u32[]{:S(2)}) collective-permute-start(bf16[512,1024]{1,0:T(8,128)(2,1)S(1)} %laid.1.refs_0_), channel_id=1, source_target_pairs={{0,16},{8,24},{16,0},{24,8},{1,17},{9,25},{17,1},{25,9},{2,18},{10... | collective-permute-start | bytes 3145736 | tf_op jit(solution)/shard_map/fsdp_2/ppermute | solution.py:530
  113.9 63.7 %collective-permute-start.17 = (bf16[512,1024]{1,0:T(8,128)(2,1)S(1)}, bf16[512,1024]{1,0:T(8,128)(2,1)}, u32[]{:S(2)}, u32[]{:S(2)}) collective-permute-start(bf16[512,1024]{1,0:T(8,128)(2,1)S(1)} %bitcast.31), channel_id=1, source_target_pairs={{0,8},{8,0},{16,24},{24,16},{1,9},{9,1},{17,25},{25,17},{2,10},{10... | collective-permute-start | bytes 3145736 | tf_op jit(solution)/shard_map/fsdp_1/ppermute | solution.py:530
  114.4 63.2 %collective-permute-start.18 = (bf16[512,1024]{1,0:T(8,128)(2,1)S(1)}, bf16[512,1024]{1,0:T(8,128)(2,1)}, u32[]{:S(2)}, u32[]{:S(2)}) collective-permute-start(bf16[512,1024]{1,0:T(8,128)(2,1)S(1)} %bitcast.32), channel_id=1, source_target_pairs={{0,16},{8,24},{16,0},{24,8},{1,17},{9,25},{17,1},{25,9},{2,18},{10... | collective-permute-start | bytes 3145736 | tf_op jit(solution)/shard_map/fsdp_2/ppermute | solution.py:530
  117.0 60.6 %all-to-all-start.1 = ((bf16[4,128,1024]{2,1,0:T(8,128)(2,1)}), bf16[4,128,1024]{2,1,0:T(8,128)(2,1)}, u32[]{:S(2)}, u32[]{:S(2)}) async-start(bf16[4,128,1024]{2,1,0:T(8,128)(2,1)} %copy-done.12), calls=%async_computation.1 | async-start | bytes 2097152 | tf_op jit(solution)/shard_map/all_to_all | solution.py:895
  177.6 49.0 %collective-permute-start.19 = (bf16[512,1024]{1,0:T(8,128)(2,1)}, bf16[512,1024]{1,0:T(8,128)(2,1)S(1)}, u32[]{:S(2)}, u32[]{:S(2)}) collective-permute-start(bf16[512,1024]{1,0:T(8,128)(2,1)} %bitcast.6.refs_0_), channel_id=1, source_target_pairs={{0,8},{8,16},{16,24},{1,9},{9,17},{17,25},{2,10},{10,18},{18,26},{... | collective-permute-start | bytes 3145736 | tf_op jit(solution)/shard_map/line/ppermute | solution.py:543
  179.7 46.9 %collective-permute-start.20 = (bf16[512,1024]{1,0:T(8,128)(2,1)}, bf16[512,1024]{1,0:T(8,128)(2,1)}, u32[]{:S(2)}, u32[]{:S(2)}) collective-permute-start(bf16[512,1024]{1,0:T(8,128)(2,1)} %bitcast.6.refs_0_), channel_id=1, source_target_pairs={{8,0},{16,8},{24,16},{9,1},{17,9},{25,17},{10,2},{18,10},{26,18},{... | collective-permute-start | bytes 3145736 | tf_op jit(solution)/shard_map/line/ppermute | solution.py:543
  181.3 48.3 %collective-permute-start.21 = (bf16[512,1024]{1,0:T(8,128)(2,1)}, bf16[512,1024]{1,0:T(8,128)(2,1)}, u32[]{:S(2)}, u32[]{:S(2)}) collective-permute-start(bf16[512,1024]{1,0:T(8,128)(2,1)} %collective-permute-done.18.refs_2_), channel_id=1, source_target_pairs={{0,8},{8,0},{16,24},{24,16},{1,9},{9,1},{17,25},{25,17},{2,10},{10... | collective-permute-start | bytes 3145736 | tf_op jit(solution)/shard_map/fsdp_1/ppermute | solution.py:530
  229.6 44.8 %collective-permute-start.22 = (bf16[512,1024]{1,0:T(8,128)(2,1)S(1)}, bf16[512,1024]{1,0:T(8,128)(2,1)}, u32[]{:S(2)}, u32[]{:S(2)}) collective-permute-start(bf16[512,1024]{1,0:T(8,128)(2,1)S(1)} %collective-permute-done.19.refs_1_), channel_id=1, source_target_pairs={{8,16},{16,24},{9,17},{17,25},{10,18},{18,26},{11,19},{19,27},{12,... | collective-permute-start | bytes 3145736 | tf_op jit(solution)/shard_map/line/ppermute | solution.py:543
  231.2 43.2 %collective-permute-start.23 = (bf16[512,1024]{1,0:T(8,128)(2,1)}, bf16[512,1024]{1,0:T(8,128)(2,1)}, u32[]{:S(2)}, u32[]{:S(2)}) collective-permute-start(bf16[512,1024]{1,0:T(8,128)(2,1)} %collective-permute-done.20.refs_2_), channel_id=1, source_target_pairs={{8,0},{16,8},{9,1},{17,9},{10,2},{18,10},{11,3},{19,11},{12,4},{20... | collective-permute-start | bytes 3145736 | tf_op jit(solution)/shard_map/line/ppermute | solution.py:543
  232.5 41.9 %collective-permute-start.24 = (bf16[512,1024]{1,0:T(8,128)(2,1)}, bf16[512,1024]{1,0:T(8,128)(2,1)}, u32[]{:S(2)}, u32[]{:S(2)}) collective-permute-start(bf16[512,1024]{1,0:T(8,128)(2,1)} %bitcast.29), channel_id=1, source_target_pairs={{0,8},{24,16},{1,9},{25,17},{2,10},{26,18},{3,11},{27,19},{4,12},{... | collective-permute-start | bytes 3145736 | tf_op jit(solution)/shard_map/line/ppermute | solution.py:543
  274.4 39.1 %collective-permute-start.25 = (bf16[512,1024]{1,0:T(8,128)(2,1)}, bf16[512,1024]{1,0:T(8,128)(2,1)S(1)}, u32[]{:S(2)}, u32[]{:S(2)}) collective-permute-start(bf16[512,1024]{1,0:T(8,128)(2,1)} %collective-permute-done.22.refs_3_), channel_id=1, source_target_pairs={{16,24},{17,25},{18,26},{19,27},{20,28},{21,29},{22,30},{23,31}} | collective-permute-start | bytes 3145736 | tf_op jit(solution)/shard_map/line/ppermute | solution.py:543
  275.1 38.4 %collective-permute-start.26 = (bf16[512,1024]{1,0:T(8,128)(2,1)}, bf16[512,1024]{1,0:T(8,128)(2,1)}, u32[]{:S(2)}, u32[]{:S(2)}) collective-permute-start(bf16[512,1024]{1,0:T(8,128)(2,1)} %collective-permute-done.23.refs_4_), channel_id=1, source_target_pairs={{8,0},{9,1},{10,2},{11,3},{12,4},{13,5},{14,6},{15,7}} | collective-permute-start | bytes 3145736 | tf_op jit(solution)/shard_map/line/ppermute | solution.py:543
  313.5 48.8 %collective-permute-start.29 = (bf16[512,1024]{1,0:T(8,128)(2,1)S(1)}, bf16[512,1024]{1,0:T(8,128)(2,1)S(1)}, u32[]{:S(2)}, u32[]{:S(2)}) collective-permute-start(bf16[512,1024]{1,0:T(8,128)(2,1)S(1)} %bitcast.34), channel_id=1, source_target_pairs={{0,8},{24,16},{1,9},{25,17},{2,10},{26,18},{3,11},{27,19},{4,12},{... | collective-permute-start | bytes 3145736 | tf_op jit(solution)/shard_map/line/ppermute | solution.py:543
  322.4 40.0 %collective-permute-start.30 = (bf16[512,1024]{1,0:T(8,128)(2,1)}, bf16[512,1024]{1,0:T(8,128)(2,1)S(1)}, u32[]{:S(2)}, u32[]{:S(2)}) collective-permute-start(bf16[512,1024]{1,0:T(8,128)(2,1)} %get-tuple-element.384), channel_id=1, source_target_pairs={{0,8},{8,16},{16,24},{1,9},{9,17},{17,25},{2,10},{10,18},{18,26},{... | collective-permute-start | bytes 3145736 | tf_op jit(solution)/shard_map/line/ppermute | solution.py:543
  323.7 39.6 %collective-permute-start.31 = (bf16[512,1024]{1,0:T(8,128)(2,1)}, bf16[512,1024]{1,0:T(8,128)(2,1)S(1)}, u32[]{:S(2)}, u32[]{:S(2)}) collective-permute-start(bf16[512,1024]{1,0:T(8,128)(2,1)} %get-tuple-element.385), channel_id=1, source_target_pairs={{8,0},{16,8},{24,16},{9,1},{17,9},{25,17},{10,2},{18,10},{26,18},{... | collective-permute-start | bytes 3145736 | tf_op jit(solution)/shard_map/line/ppermute | solution.py:543
  376.2 44.3 %collective-permute-start.37 = (bf16[512,1024]{1,0:T(8,128)(2,1)S(1)}, bf16[512,1024]{1,0:T(8,128)(2,1)S(1)}, u32[]{:S(2)}, u32[]{:S(2)}) collective-permute-start(bf16[512,1024]{1,0:T(8,128)(2,1)S(1)} %second.3), channel_id=1, source_target_pairs={{0,8},{8,16},{1,9},{9,17},{2,10},{10,18},{3,11},{11,19},{4,12},{12... | collective-permute-start | bytes 3145736 | tf_op jit(solution)/shard_map/line/ppermute | solution.py:543
  381.1 39.5 %collective-permute-start.38 = (bf16[512,1024]{1,0:T(8,128)(2,1)S(1)}, bf16[512,1024]{1,0:T(8,128)(2,1)S(1)}, u32[]{:S(2)}, u32[]{:S(2)}) collective-permute-start(bf16[512,1024]{1,0:T(8,128)(2,1)S(1)} %second.3), channel_id=1, source_target_pairs={{16,8},{24,16},{17,9},{25,17},{18,10},{26,18},{19,11},{27,19},{20,... | collective-permute-start | bytes 3145736 | tf_op jit(solution)/shard_map/line/ppermute | solution.py:543
  381.8 43.8 %collective-permute-start.39 = (bf16[512,1024]{1,0:T(8,128)(2,1)S(1)}, bf16[512,1024]{1,0:T(8,128)(2,1)S(1)}, u32[]{:S(2)}, u32[]{:S(2)}) collective-permute-start(bf16[512,1024]{1,0:T(8,128)(2,1)S(1)} %bitcast.38), channel_id=1, source_target_pairs={{0,8},{24,16},{1,9},{25,17},{2,10},{26,18},{3,11},{27,19},{4,12},{... | collective-permute-start | bytes 3145736 | tf_op jit(solution)/shard_map/line/ppermute | solution.py:543
  431.6 50.2 %collective-permute-start.40 = (bf16[1024,1024]{1,0:T(8,128)(2,1)}, bf16[1024,1024]{1,0:T(8,128)(2,1)S(1)}, u32[]{:S(2)}, u32[]{:S(2)}) collective-permute-start(bf16[1024,1024]{1,0:T(8,128)(2,1)} %get-tuple-element.429), channel_id=1, source_target_pairs={{0,8},{8,16},{16,24},{1,9},{9,17},{17,25},{2,10},{10,18},{18,26},{... | collective-permute-start | bytes 6291464 | tf_op jit(solution)/shard_map/line/ppermute | solution.py:543
  436.1 52.1 %collective-permute-start.41 = (bf16[1024,1024]{1,0:T(8,128)(2,1)}, bf16[1024,1024]{1,0:T(8,128)(2,1)}, u32[]{:S(2)}, u32[]{:S(2)}) collective-permute-start(bf16[1024,1024]{1,0:T(8,128)(2,1)} %get-tuple-element.430), channel_id=1, source_target_pairs={{8,0},{16,8},{24,16},{9,1},{17,9},{25,17},{10,2},{18,10},{26,18},{... | collective-permute-start | bytes 6291464 | tf_op jit(solution)/shard_map/line/ppermute | solution.py:543
  (73 other events, 925.8 us)

commit v4 on v3

--- a/solution.py
+++ b/solution.py
@@ -530,10 +530,13 @@
         return lax.ppermute(values, axis, [(place, place ^ bit) for place in range(size)])
 
 
-def total(values, axis):
+def total(values, axis, *between):
+    between = list(between)
     bit = 1
     while bit < lax.axis_size(axis):
         values = values + swap(values, axis, bit)
+        if between:
+            values = hold(values, between.pop(0))
         bit *= 2
     return values
 
@@ -622,26 +625,26 @@
             second_of(place, first, second, sum_of(got))
             for first, second, got in zip(refs[::3], refs[1::3], refs[2::3])
         ]
-        return [jnp.concatenate(sent, axis=0)]
-
-    sent = pointwise(
-        "second", choose, [place], inputs, [((len(sums) * rows, columns), jnp.bfloat16)]
-    )[0]
+        return [jnp.stack(sent)]
+
+    shape = (len(sums), rows, columns)
+    sent = pointwise("second", choose, [place], inputs, [(shape, jnp.bfloat16)])[0]
+    sent = sent.reshape(-1, columns)
     return [move(sent, UP[:2]), move(sent, DOWN[1:])]
 
 
 def reduce_third(parts, got, place, new=None):
     first, rest = parts
     rows, columns = first.shape
-    shape = (rows if new is None else 2 * rows, columns)
+    shape = (1 if new is None else 2, rows, columns)
 
     def choose(place, second, third, upward, downward, *others):
         sent = third_of(place, second, third, upward, downward)
         if not others:
-            return sent
+            return [item[None] for item in sent]
         first, second, got = others
         other = second_of(place, first, second, sum_of(got))
-        return [jnp.concatenate([item, other], axis=0) for item in sent]
+        return [jnp.stack([item, other]) for item in sent]
 
     inputs = [(rest, 1, 0), (rest, 1, 1), *got]
     if new is not None:
@@ -649,6 +652,7 @@
     upward, downward = pointwise(
         "third", choose, [place], inputs, [(shape, jnp.bfloat16)] * 2
     )
+    upward, downward = upward.reshape(-1, columns), downward.reshape(-1, columns)
     return [move(upward, UP), move(downward, DOWN)], upward
 
 
@@ -1024,11 +1028,11 @@
     live.rows = gather_first(live.rows)
     live.places = local_places(live.positions)
     live.turning = turning(live.places)
+    live.down = pieces("down", live.weights[1])
     tick(live)
     live.attention = square_second(live.attention)
     live.normed, live.grads = gather_third(gather_second(live.rows))
     live.up = gather_rows_of(pieces("up", live.weights[0]))
-    live.down = pieces("down", live.weights[1])
     del live.rows
     tick(live)
     live.up = square_first(live.up)
@@ -1168,7 +1172,10 @@
     up_sum = trade_back(reduce_last(live.up_parts, live.up_sum))
     (down_weight_grad,) = finish(live.both, "down", 1, 2)
     qkv_weight_grad, out_weight_grad = finish(live.both, "attention", 0, 2)
-    sums = total(total(live.sums, FSDP), CTX)
+    sums = total(
+        live.sums, FSDP, down_weight_grad, (qkv_weight_grad, out_weight_grad)
+    )
+    sums = total(sums, CTX)
     (up_weight_grad,) = finish(up_sum, "up")
     bias_sums = sums[: -3 * D]
     norm_sums = sums[-3 * D :].reshape(3, D)

time: 570 us -> 567 us (level)
  transfers between devices with their start and end apart: 58 -> 58, of which waited for: 17 -> 20; matrix products, arithmetic and copies ran while one was open for 4% -> 4% of each run, Pallas kernels for 50% -> 50%
where the time goes in v4:
time: 567 us; the launch traced here: 558 us
  Pallas kernels  292 us (51%)
  waiting for transfers between devices  124 us (22%)
  starting transfers between devices  99.5 us (18%)
  local copies, waits for them, and re-layouts  28 us (5%)
  other arithmetic  13 us (2%)
    pallas_call x6, Pallas kernels, row_call(): pl.pallas_call(kernel, grid=(count,), in_specs=[pl.BlockSpec((size, item....  93.2 us
    ppermute x35, waiting for transfers between devices, swap(): lax.ppermute(values, axis, [(place, place ^ bit) for place in range(size)])  79.2 us
    pallas_call x2, Pallas kernels, attention(): pl.pallas_call(attention_kernel, grid_spec=pltpu.PrefetchScalarGridSpec(n...  67.8 us
    ppermute x19, starting transfers between devices, move(): return lax.ppermute(values, FSDP, pairs)  53.5 us
    pallas_call x6, Pallas kernels, grad_pieces(): pl.pallas_call(functools.partial(grad_kernel, [len(rights) for _, rights...  50.5 us
    ppermute x19, waiting for transfers between devices, move(): return lax.ppermute(values, FSDP, pairs)  43.6 us
    pallas_call x14, Pallas kernels, pointwise(): pl.pallas_call(kernel, grid=(1,), in_specs=[pl.BlockSpec(memory_space=plt...  42.2 us
    ppermute x35, starting transfers between devices, swap(): lax.ppermute(values, axis, [(place, place ^ bit) for place in range(size)])  30.1 us
  transfers between devices with their start and end apart: 58, of which 20 were waited for; matrix products, arithmetic and copies ran while one was open for 4% of the time, Pallas kernels for 50%

profile of v4, /device:TPU:0, one launch (start us, length us, event | category | flops | bytes accessed | tf_op | source)
XLA Modules:
  0.0 558.1 jit_solution(1643148949842863120)
XLA Ops:
  28.9 5.6 fusion.6
  34.5 35.0 %collective-permute-done.3.refs_1_ = bf16[512,1024]{1,0:T(8,128)(2,1)S(1)} collective-permute-done((bf16[512,1024]{1,0:T(8,128)(2,1)S(1)}, bf16[512,1024]{1,0:T(8,128)(2,1)S(1)}, u32[]{:S(2)}, u32[]{:S(2)}) %collective-permute-start.3) | collective-permute-done | bytes 1048608 | tf_op jit(solution)/shard_map/fsdp_1/ppermute | solution.py:530
  83.3 6.2 %stack.2.refs_3_ = bf16[2048,2048]{1,0:T(8,128)(2,1)} custom-call(bf16[512,2048]{1,0:T(8,128)(2,1)} %pad_maximum_fusion.refs_0_, bf16[512,2048]{1,0:T(8,128)(2,1)} %collective-permute-done.5.refs_1_, bf16[512,2048]{1,0:T(8,128)(2,1)} %collective-permute-done.6.refs_2_, bf16[512,2048]{1,0:T(8,128)(2,1)} %collective-permute-done.7.refs_3_, ...), custom_call_target="tpu_custom_call" | custom-call | tf_op jit(solution)/shard_map/stack/pallas_call | solution.py:432
  89.5 6.2 %stack.3.refs_3_ = bf16[2048,2048]{1,0:T(8,128)(2,1)} custom-call(bf16[512,2048]{1,0:T(8,128)(2,1)} %pad_maximum_fusion.refs_0_, bf16[512,2048]{1,0:T(8,128)(2,1)} %collective-permute-done.5.refs_1_, bf16[512,2048]{1,0:T(8,128)(2,1)} %collective-permute-done.6.refs_2_, bf16[512,2048]{1,0:T(8,128)(2,1)} %collective-permute-done.7.refs_3_, ...), custom_call_target="tpu_custom_call" | custom-call | tf_op jit(solution)/shard_map/stack/pallas_call | solution.py:432
  95.7 7.8 %collective-permute-done.9.refs_0_ = bf16[256,2048]{1,0:T(8,128)(2,1)} collective-permute-done((bf16[256,2048]{1,0:T(8,128)(2,1)}, bf16[256,2048]{1,0:T(8,128)(2,1)}, u32[]{:S(2)}, u32[]{:S(2)}) %collective-permute-start.9) | collective-permute-done | bytes 1048608 | tf_op jit(solution)/shard_map/ctx_2/ppermute | solution.py:530
  127.5 15.4 %project.1 = (bf16[2048,256]{1,0:T(8,128)(2,1)}, bf16[2048,256]{1,0:T(8,128)(2,1)}, bf16[2048,256]{1,0:T(8,128)(2,1)}, bf16[256,2048]{1,0:T(8,128)(2,1)}, bf16[2...) custom-call(bf16[2048,2048]{1,0:T(8,128)(2,1)} %fill.3.normed.refs_0_, ...), custom_call_target="tpu_custom_call" | custom-call | tf_op jit(solution)/shard_map/project/pallas_call | solution.py:232
  143.5 33.9 %attention_0.1 = (bf16[2048,256]{1,0:T(8,128)(2,1)}, bf16[2048,256]{1,0:T(8,128)(2,1)}, bf16[2048,256]{1,0:T(8,128)(2,1)}, bf16[2048,256]{1,0:T(8,128)(2,1)}) custom-call(s32[8]{0:T(128)} %select_reduce_fusion.order, bf16[2048,256]{1,0:T(8,128)(2,1)} %get-tuple-element.305.query_in, bf16[2048,256]{1,0:T(8,128)(2,1)} %get-tuple-element.306.key_all, ...), custom_call_target="tpu_custom_call" | custom-call | tf_op jit(solution)/shard_map/attention_0/pallas_call | solution.py:182
  184.9 34.0 %attention_1.1 = (bf16[2048,256]{1,0:T(8,128)(2,1)}, bf16[2048,256]{1,0:T(8,128)(2,1)}, bf16[2048,256]{1,0:T(8,128)(2,1)}, bf16[2048,256]{1,0:T(8,128)(2,1)}) custom-call(s32[8]{0:T(128)} %select_reduce_fusion.order, bf16[2048,256]{1,0:T(8,128)(2,1)} %get-tuple-element.305.query_in, ...), custom_call_target="tpu_custom_call", output_to_operand_aliasing={{0}: (10, {}), {1}: (11, {}), {2}: (12, {}), {3}: (13, {})} | custom-call | tf_op jit(solution)/shard_map/attention_1/pallas_call | solution.py:182
  218.8 7.5 %grad_0.3 = bf16[1,512,1024]{2,1,0:T(8,128)(2,1)} custom-call(s32[4]{0:T(128)} %fusion.7.turns, bf16[2048,2048]{1,0:T(8,128)(2,1)} %fill.3.normed.refs_0_, bf16[2048,256]{1,0:T(8,128)(2,1)} %get-tuple-element.358.refs_1_.refs_0_, bf16[2048,256]{1,0:T(8,128)(2,1)} %get-tuple-element.359.refs_2_.refs_1_, bf16[2048,256]{1,0:T(8,128)(2,1)} %get-tuple-element.360.refs_3_.refs_2_, ...), custom_call_target="tpu_custom_call" | custom-call | tf_op jit(solution)/shard_map/grad_0/pallas_call | solution.py:375
  232.2 7.2 %collective-permute-start.24 = (bf16[512,1024]{1,0:T(8,128)(2,1)}, bf16[512,1024]{1,0:T(8,128)(2,1)}, u32[]{:S(2)}, u32[]{:S(2)}) collective-permute-start(bf16[512,1024]{1,0:T(8,128)(2,1)} %bitcast.37), channel_id=1, source_target_pairs={{0,8},{24,16},{1,9},{25,17},{2,10},{26,18},{3,11},{27,19},{4,12},{... | collective-permute-start | bytes 3145736 | tf_op jit(solution)/shard_map/line/ppermute | solution.py:546
  244.1 17.6 %hidden.1 = (bf16[2048,1024]{1,0:T(8,128)(2,1)S(1)}, bf16[2048,1024]{1,0:T(8,128)(2,1)}) custom-call(bf16[2048,2048]{1,0:T(8,128)(2,1)} %fill.3.normed.refs_0_, bf16[2048,1024]{1,0:T(8,128)(2,1)} %in_square.3.weight.refs_2_, f32[1,1024]{1,0:T(1,128)S(1)} %bitcast.53), custom_call_target="tpu_custom_call" | custom-call | tf_op jit(solution)/shard_map/hidden/pallas_call | solution.py:232
  261.7 12.4 %grad_1.3.refs_2_.refs_1_.refs_0_ = bf16[3,512,1024]{2,1,0:T(8,128)(2,1)} custom-call(s32[4]{0:T(128)S(1)} %copy-done.30, bf16[2048,2048]{1,0:T(8,128)(2,1)} %fill.3.normed.refs_0_, bf16[2048,256]{1,0:T(8,128)(2,1)S(1)} %copy-done.7, bf16[2048,256]{1,0:T(8,128)(2,1)S(1)} %copy-done.8, bf16[2048,256]{1,0:T(8,128)(2,1)S(1)} %copy-done.9, ...), custom_call_target="tpu_custom_call" | custom-call | tf_op jit(solution)/shard_map/grad_1/pallas_call | solution.py:375
  278.2 5.6 %collective-permute-start.27 = (bf16[512,1024]{1,0:T(8,128)(2,1)S(1)}, bf16[512,1024]{1,0:T(8,128)(2,1)S(1)}, u32[]{:S(2)}, u32[]{:S(2)}) collective-permute-start(bf16[512,1024]{1,0:T(8,128)(2,1)S(1)} %bitcast.50), channel_id=1, source_target_pairs={{0,8},{8,16},{1,9},{9,17},{2,10},{10,18},{3,11},{11,19},{4,12},{12... | collective-permute-start | bytes 3145736 | tf_op jit(solution)/shard_map/line/ppermute | solution.py:546
  289.5 10.5 %grad_1.4.refs_2_.refs_1_ = bf16[3,512,1024]{2,1,0:T(8,128)(2,1)S(1)} custom-call(s32[4]{0:T(128)S(1)} %copy-done.30, bf16[2048,2048]{1,0:T(8,128)(2,1)} %fill.2.grads.refs_4_.refs_0_, bf16[2048,1024]{1,0:T(8,128)(2,1)} %copy-done.4), custom_call_target="tpu_custom_call" | custom-call | tf_op jit(solution)/shard_map/grad_1/pallas_call | solution.py:375
  301.7 11.6 %back.3 = (bf16[2048,2048]{1,0:T(8,128)(2,1)}, f32[3,256]{1,0:T(4,128)S(1)}) custom-call(bf16[2048,256]{1,0:T(8,128)(2,1)S(1)} %copy-done.7, bf16[2048,256]{1,0:T(8,128)(2,1)S(1)} %copy-done.8, bf16[2048,256]{1,0:T(8,128)(2,1)S(1)} %copy-done.9, bf16[2048,1024]{1,0:T(8,128)(2,1)} %in_square.2.weight.refs_3_), custom_call_target="tpu_custom_call" | custom-call | tf_op jit(solution)/shard_map/back/pallas_call | solution.py:232
  329.3 12.9 %hidden_grad.1 = (bf16[2048,1024]{1,0:T(8,128)(2,1)S(1)}, f32[1,1024]{1,0:T(1,128)S(1)}) custom-call(bf16[2048,2048]{1,0:T(8,128)(2,1)} %fill.2.grads.refs_4_.refs_0_, bf16[2048,1024]{1,0:T(8,128)(2,1)} %get-tuple-element.388.slope, bf16[2048,1024]{1,0:T(8,128)(2,1)} %in_line.1.refs_2_.weight), custom_call_target="tpu_custom_call" | custom-call | tf_op jit(solution)/shard_map/hidden_grad/pallas_call | solution.py:232
  342.2 19.9 %back.4 = (bf16[1024,2048]{1,0:T(8,128)(2,1)}, bf16[1024,2048]{1,0:T(8,128)(2,1)}) custom-call(bf16[2048,1024]{1,0:T(8,128)(2,1)} %copy-done.4, bf16[2048,256]{1,0:T(8,128)(2,1)S(1)} %copy-done.10, bf16[2048,1024]{1,0:T(8,128)(2,1)} %in_line.1.refs_2_.weight, bf16[2048,1024]{1,0:T(8,128)(2,1)} %in_square.2.weight.refs_3_), custom_call_target="tpu_custom_call" | custom-call | tf_op jit(solution)/shard_map/back/pallas_call | solution.py:232
  392.5 10.5 %grad_1.5.refs_6_.refs_1_.refs_2_.refs_0_ = bf16[3,512,1024]{2,1,0:T(8,128)(2,1)S(1)} custom-call(s32[4]{0:T(128)S(1)} %copy-done.30, bf16[2048,2048]{1,0:T(8,128)(2,1)} %fill.3.normed.refs_0_, bf16[2048,1024]{1,0:T(8,128)(2,1)} %copy-done.5), custom_call_target="tpu_custom_call" | custom-call | tf_op jit(solution)/shard_map/grad_1/pallas_call | solution.py:375
  404.6 15.8 %back.5 = (bf16[1024,2048]{1,0:T(8,128)(2,1)}, bf16[1024,2048]{1,0:T(8,128)(2,1)}) custom-call(bf16[2048,1024]{1,0:T(8,128)(2,1)} %copy-done.5, bf16[2048,2048]{1,0:T(8,128)(2,1)} %get-tuple-element.413.refs_1_, bf16[2048,1024]{1,0:T(8,128)(2,1)} %in_square.3.weight.refs_2_), custom_call_target="tpu_custom_call" | custom-call | tf_op jit(solution)/shard_map/back/pallas_call | solution.py:232
  440.5 12.2 %collective-permute-done.43.refs_4_ = bf16[128,2048]{1,0:T(8,128)(2,1)S(1)} collective-permute-done((bf16[128,2048]{1,0:T(8,128)(2,1)S(1)}, bf16[128,2048]{1,0:T(8,128)(2,1)S(1)}, u32[]{:S(2)}, u32[]{:S(2)}) %collective-permute-start.43) | collective-permute-done | bytes 524320 | tf_op jit(solution)/shard_map/tp_1/ppermute | solution.py:530
  463.2 18.4 %collective-permute-done.40.refs_3_.refs_2_ = bf16[1024,1024]{1,0:T(8,128)(2,1)S(1)} collective-permute-done((bf16[1024,1024]{1,0:T(8,128)(2,1)}, bf16[1024,1024]{1,0:T(8,128)(2,1)S(1)}, u32[]{:S(2)}, u32[]{:S(2)}) %collective-permute-start.40) | collective-permute-done | bytes 2097184 | tf_op jit(solution)/shard_map/line/ppermute | solution.py:546
  481.6 6.3 %collective-permute-done.41.refs_4_.refs_3_ = bf16[1024,1024]{1,0:T(8,128)(2,1)} collective-permute-done((bf16[1024,1024]{1,0:T(8,128)(2,1)}, bf16[1024,1024]{1,0:T(8,128)(2,1)}, u32[]{:S(2)}, u32[]{:S(2)}) %collective-permute-start.41) | collective-permute-done | bytes 2097184 | tf_op jit(solution)/shard_map/line/ppermute | solution.py:546
  505.7 5.8 %tokens_grad.1 = (f32[256,2048]{1,0:T(8,128)}, f32[3,2048]{1,0:T(4,128)S(1)}) custom-call(bf16[256,2048]{1,0:T(8,128)(2,1)S(1)} %bitcast.35, bf16[256,2048]{1,0:T(8,128)(2,1)S(1)} %bitcast.45, bf16[1,2048]{1,0:T(2,128)(2,1)S(1)} %broadcast_in_dim.75.refs_2_, bf16[1024,2048]{1,0:T(8,128)(2,1)} %get-tuple-element.461.refs_0_.refs_2_.refs_3_, ...), custom_call_target="tpu_custom_call" | custom-call | tf_op jit(solution)/shard_map/tokens_grad/pallas_call | solution.py:404
  517.7 8.8 %collective-permute-done.48.refs_1_ = bf16[512,1024]{1,0:T(8,128)(2,1)} collective-permute-done((bf16[512,1024]{1,0:T(8,128)(2,1)}, bf16[512,1024]{1,0:T(8,128)(2,1)}, u32[]{:S(2)}, u32[]{:S(2)}) %collective-permute-start.48) | collective-permute-done | bytes 1048608 | tf_op jit(solution)/shard_map/line/ppermute | solution.py:546
  (260 shorter events, 229.2 us)
Async XLA Ops:
  18.5 53.5 %collective-permute-start.5 = (bf16[512,2048]{1,0:T(8,128)(2,1)}, bf16[512,2048]{1,0:T(8,128)(2,1)}, u32[]{:S(2)}, u32[]{:S(2)}) collective-permute-start(bf16[512,2048]{1,0:T(8,128)(2,1)} %pad_maximum_fusion.refs_0_), channel_id=1, source_target_pairs={{0,1},{1,0},{2,3},{3,2},{4,5},{5,4},{6,7},{7,6},{8,9},{9,8},{10,11... | collective-permute-start | bytes 6291464 | tf_op jit(solution)/shard_map/tp_1/ppermute | solution.py:530
  20.1 51.9 %collective-permute-start.6 = (bf16[512,2048]{1,0:T(8,128)(2,1)}, bf16[512,2048]{1,0:T(8,128)(2,1)}, u32[]{:S(2)}, u32[]{:S(2)}) collective-permute-start(bf16[512,2048]{1,0:T(8,128)(2,1)} %pad_maximum_fusion.refs_0_), channel_id=1, source_target_pairs={{0,4},{2,6},{4,0},{6,2},{1,5},{3,7},{5,1},{7,3},{8,12},{10,14},{12... | collective-permute-start | bytes 6291464 | tf_op jit(solution)/shard_map/ctx_2/ppermute | solution.py:530
  21.6 50.4 %collective-permute-start.7 = (bf16[512,2048]{1,0:T(8,128)(2,1)}, bf16[512,2048]{1,0:T(8,128)(2,1)}, u32[]{:S(2)}, u32[]{:S(2)}) collective-permute-start(bf16[512,2048]{1,0:T(8,128)(2,1)} %pad_maximum_fusion.refs_0_), channel_id=1, source_target_pairs={{0,2},{2,0},{4,6},{6,4},{1,3},{3,1},{5,7},{7,5},{8,10},{10,8},{12,... | collective-permute-start | bytes 6291464 | tf_op jit(solution)/shard_map/ctx_1/ppermute | solution.py:530
  21.6 47.9 %collective-permute-start.3 = (bf16[512,1024]{1,0:T(8,128)(2,1)S(1)}, bf16[512,1024]{1,0:T(8,128)(2,1)S(1)}, u32[]{:S(2)}, u32[]{:S(2)}) collective-permute-start(bf16[512,1024]{1,0:T(8,128)(2,1)S(1)} %laid.1.refs_0_), channel_id=1, source_target_pairs={{0,8},{8,0},{16,24},{24,16},{1,9},{9,1},{17,25},{25,17},{2,10},{10... | collective-permute-start | bytes 3145736 | tf_op jit(solution)/shard_map/fsdp_1/ppermute | solution.py:530
  23.2 48.8 %collective-permute-start.4 = (bf16[512,1024]{1,0:T(8,128)(2,1)S(1)}, bf16[512,1024]{1,0:T(8,128)(2,1)}, u32[]{:S(2)}, u32[]{:S(2)}) collective-permute-start(bf16[512,1024]{1,0:T(8,128)(2,1)S(1)} %laid.1.refs_0_), channel_id=1, source_target_pairs={{0,16},{8,24},{16,0},{24,8},{1,17},{9,25},{17,1},{25,9},{2,18},{10... | collective-permute-start | bytes 3145736 | tf_op jit(solution)/shard_map/fsdp_2/ppermute | solution.py:530
  113.8 63.6 %collective-permute-start.17 = (bf16[512,1024]{1,0:T(8,128)(2,1)S(1)}, bf16[512,1024]{1,0:T(8,128)(2,1)}, u32[]{:S(2)}, u32[]{:S(2)}) collective-permute-start(bf16[512,1024]{1,0:T(8,128)(2,1)S(1)} %bitcast.39), channel_id=1, source_target_pairs={{0,8},{8,0},{16,24},{24,16},{1,9},{9,1},{17,25},{25,17},{2,10},{10... | collective-permute-start | bytes 3145736 | tf_op jit(solution)/shard_map/fsdp_1/ppermute | solution.py:530
  114.2 63.2 %collective-permute-start.18 = (bf16[512,1024]{1,0:T(8,128)(2,1)S(1)}, bf16[512,1024]{1,0:T(8,128)(2,1)}, u32[]{:S(2)}, u32[]{:S(2)}) collective-permute-start(bf16[512,1024]{1,0:T(8,128)(2,1)S(1)} %bitcast.40), channel_id=1, source_target_pairs={{0,16},{8,24},{16,0},{24,8},{1,17},{9,25},{17,1},{25,9},{2,18},{10... | collective-permute-start | bytes 3145736 | tf_op jit(solution)/shard_map/fsdp_2/ppermute | solution.py:530
  116.8 60.6 %all-to-all-start.1 = ((bf16[4,128,1024]{2,1,0:T(8,128)(2,1)}), bf16[4,128,1024]{2,1,0:T(8,128)(2,1)}, u32[]{:S(2)}, u32[]{:S(2)}) async-start(bf16[4,128,1024]{2,1,0:T(8,128)(2,1)} %copy-done.12), calls=%async_computation.1 | async-start | bytes 2097152 | tf_op jit(solution)/shard_map/all_to_all | solution.py:899
  177.4 48.9 %collective-permute-start.19 = (bf16[512,1024]{1,0:T(8,128)(2,1)}, bf16[512,1024]{1,0:T(8,128)(2,1)S(1)}, u32[]{:S(2)}, u32[]{:S(2)}) collective-permute-start(bf16[512,1024]{1,0:T(8,128)(2,1)} %bitcast.6.refs_0_), channel_id=1, source_target_pairs={{0,8},{8,16},{16,24},{1,9},{9,17},{17,25},{2,10},{10,18},{18,26},{... | collective-permute-start | bytes 3145736 | tf_op jit(solution)/shard_map/line/ppermute | solution.py:546
  179.4 46.9 %collective-permute-start.20 = (bf16[512,1024]{1,0:T(8,128)(2,1)}, bf16[512,1024]{1,0:T(8,128)(2,1)}, u32[]{:S(2)}, u32[]{:S(2)}) collective-permute-start(bf16[512,1024]{1,0:T(8,128)(2,1)} %bitcast.6.refs_0_), channel_id=1, source_target_pairs={{8,0},{16,8},{24,16},{9,1},{17,9},{25,17},{10,2},{18,10},{26,18},{... | collective-permute-start | bytes 3145736 | tf_op jit(solution)/shard_map/line/ppermute | solution.py:546
  181.0 48.3 %collective-permute-start.21 = (bf16[512,1024]{1,0:T(8,128)(2,1)}, bf16[512,1024]{1,0:T(8,128)(2,1)}, u32[]{:S(2)}, u32[]{:S(2)}) collective-permute-start(bf16[512,1024]{1,0:T(8,128)(2,1)} %collective-permute-done.18.refs_2_), channel_id=1, source_target_pairs={{0,8},{8,0},{16,24},{24,16},{1,9},{9,1},{17,25},{25,17},{2,10},{10... | collective-permute-start | bytes 3145736 | tf_op jit(solution)/shard_map/fsdp_1/ppermute | solution.py:530
  229.3 44.9 %collective-permute-start.22 = (bf16[512,1024]{1,0:T(8,128)(2,1)S(1)}, bf16[512,1024]{1,0:T(8,128)(2,1)}, u32[]{:S(2)}, u32[]{:S(2)}) collective-permute-start(bf16[512,1024]{1,0:T(8,128)(2,1)S(1)} %collective-permute-done.19.refs_1_), channel_id=1, source_target_pairs={{8,16},{16,24},{9,17},{17,25},{10,18},{18,26},{11,19},{19,27},{12,... | collective-permute-start | bytes 3145736 | tf_op jit(solution)/shard_map/line/ppermute | solution.py:546
  230.9 43.3 %collective-permute-start.23 = (bf16[512,1024]{1,0:T(8,128)(2,1)}, bf16[512,1024]{1,0:T(8,128)(2,1)}, u32[]{:S(2)}, u32[]{:S(2)}) collective-permute-start(bf16[512,1024]{1,0:T(8,128)(2,1)} %collective-permute-done.20.refs_2_), channel_id=1, source_target_pairs={{8,0},{16,8},{9,1},{17,9},{10,2},{18,10},{11,3},{19,11},{12,4},{20... | collective-permute-start | bytes 3145736 | tf_op jit(solution)/shard_map/line/ppermute | solution.py:546
  232.2 42.0 %collective-permute-start.24 = (bf16[512,1024]{1,0:T(8,128)(2,1)}, bf16[512,1024]{1,0:T(8,128)(2,1)}, u32[]{:S(2)}, u32[]{:S(2)}) collective-permute-start(bf16[512,1024]{1,0:T(8,128)(2,1)} %bitcast.37), channel_id=1, source_target_pairs={{0,8},{24,16},{1,9},{25,17},{2,10},{26,18},{3,11},{27,19},{4,12},{... | collective-permute-start | bytes 3145736 | tf_op jit(solution)/shard_map/line/ppermute | solution.py:546
  274.2 39.1 %collective-permute-start.25 = (bf16[512,1024]{1,0:T(8,128)(2,1)}, bf16[512,1024]{1,0:T(8,128)(2,1)S(1)}, u32[]{:S(2)}, u32[]{:S(2)}) collective-permute-start(bf16[512,1024]{1,0:T(8,128)(2,1)} %collective-permute-done.22.refs_3_), channel_id=1, source_target_pairs={{16,24},{17,25},{18,26},{19,27},{20,28},{21,29},{22,30},{23,31}} | collective-permute-start | bytes 3145736 | tf_op jit(solution)/shard_map/line/ppermute | solution.py:546
  274.9 38.4 %collective-permute-start.26 = (bf16[512,1024]{1,0:T(8,128)(2,1)}, bf16[512,1024]{1,0:T(8,128)(2,1)}, u32[]{:S(2)}, u32[]{:S(2)}) collective-permute-start(bf16[512,1024]{1,0:T(8,128)(2,1)} %collective-permute-done.23.refs_4_), channel_id=1, source_target_pairs={{8,0},{9,1},{10,2},{11,3},{12,4},{13,5},{14,6},{15,7}} | collective-permute-start | bytes 3145736 | tf_op jit(solution)/shard_map/line/ppermute | solution.py:546
  313.3 48.8 %collective-permute-start.29 = (bf16[512,1024]{1,0:T(8,128)(2,1)S(1)}, bf16[512,1024]{1,0:T(8,128)(2,1)S(1)}, u32[]{:S(2)}, u32[]{:S(2)}) collective-permute-start(bf16[512,1024]{1,0:T(8,128)(2,1)S(1)} %bitcast.42), channel_id=1, source_target_pairs={{0,8},{24,16},{1,9},{25,17},{2,10},{26,18},{3,11},{27,19},{4,12},{... | collective-permute-start | bytes 3145736 | tf_op jit(solution)/shard_map/line/ppermute | solution.py:546
  322.1 40.0 %collective-permute-start.30 = (bf16[512,1024]{1,0:T(8,128)(2,1)}, bf16[512,1024]{1,0:T(8,128)(2,1)S(1)}, u32[]{:S(2)}, u32[]{:S(2)}) collective-permute-start(bf16[512,1024]{1,0:T(8,128)(2,1)} %bitcast.12), channel_id=1, source_target_pairs={{0,8},{8,16},{16,24},{1,9},{9,17},{17,25},{2,10},{10,18},{18,26},{... | collective-permute-start | bytes 3145736 | tf_op jit(solution)/shard_map/line/ppermute | solution.py:546
  323.5 39.6 %collective-permute-start.31 = (bf16[512,1024]{1,0:T(8,128)(2,1)}, bf16[512,1024]{1,0:T(8,128)(2,1)S(1)}, u32[]{:S(2)}, u32[]{:S(2)}) collective-permute-start(bf16[512,1024]{1,0:T(8,128)(2,1)} %bitcast.13), channel_id=1, source_target_pairs={{8,0},{16,8},{24,16},{9,1},{17,9},{25,17},{10,2},{18,10},{26,18},{... | collective-permute-start | bytes 3145736 | tf_op jit(solution)/shard_map/line/ppermute | solution.py:546
  376.0 44.4 %collective-permute-start.37 = (bf16[512,1024]{1,0:T(8,128)(2,1)S(1)}, bf16[512,1024]{1,0:T(8,128)(2,1)S(1)}, u32[]{:S(2)}, u32[]{:S(2)}) collective-permute-start(bf16[512,1024]{1,0:T(8,128)(2,1)S(1)} %bitcast.48), channel_id=1, source_target_pairs={{0,8},{8,16},{1,9},{9,17},{2,10},{10,18},{3,11},{11,19},{4,12},{12... | collective-permute-start | bytes 3145736 | tf_op jit(solution)/shard_map/line/ppermute | solution.py:546
  380.9 39.5 %collective-permute-start.38 = (bf16[512,1024]{1,0:T(8,128)(2,1)S(1)}, bf16[512,1024]{1,0:T(8,128)(2,1)S(1)}, u32[]{:S(2)}, u32[]{:S(2)}) collective-permute-start(bf16[512,1024]{1,0:T(8,128)(2,1)S(1)} %bitcast.49), channel_id=1, source_target_pairs={{16,8},{24,16},{17,9},{25,17},{18,10},{26,18},{19,11},{27,19},{20,... | collective-permute-start | bytes 3145736 | tf_op jit(solution)/shard_map/line/ppermute | solution.py:546
  381.6 43.8 %collective-permute-start.39 = (bf16[512,1024]{1,0:T(8,128)(2,1)S(1)}, bf16[512,1024]{1,0:T(8,128)(2,1)S(1)}, u32[]{:S(2)}, u32[]{:S(2)}) collective-permute-start(bf16[512,1024]{1,0:T(8,128)(2,1)S(1)} %bitcast.46), channel_id=1, source_target_pairs={{0,8},{24,16},{1,9},{25,17},{2,10},{26,18},{3,11},{27,19},{4,12},{... | collective-permute-start | bytes 3145736 | tf_op jit(solution)/shard_map/line/ppermute | solution.py:546
  431.3 50.2 %collective-permute-start.40 = (bf16[1024,1024]{1,0:T(8,128)(2,1)}, bf16[1024,1024]{1,0:T(8,128)(2,1)S(1)}, u32[]{:S(2)}, u32[]{:S(2)}) collective-permute-start(bf16[1024,1024]{1,0:T(8,128)(2,1)} %bitcast.62), channel_id=1, source_target_pairs={{0,8},{8,16},{16,24},{1,9},{9,17},{17,25},{2,10},{10,18},{18,26},{... | collective-permute-start | bytes 6291464 | tf_op jit(solution)/shard_map/line/ppermute | solution.py:546
  435.9 52.1 %collective-permute-start.41 = (bf16[1024,1024]{1,0:T(8,128)(2,1)}, bf16[1024,1024]{1,0:T(8,128)(2,1)}, u32[]{:S(2)}, u32[]{:S(2)}) collective-permute-start(bf16[1024,1024]{1,0:T(8,128)(2,1)} %bitcast.61), channel_id=1, source_target_pairs={{8,0},{16,8},{24,16},{9,1},{17,9},{25,17},{10,2},{18,10},{26,18},{... | collective-permute-start | bytes 6291464 | tf_op jit(solution)/shard_map/line/ppermute | solution.py:546
  (73 other events, 900.1 us)

commit v5 on v4

--- a/solution.py
+++ b/solution.py
@@ -671,6 +671,16 @@
     return lax.axis_size(CTX) == 4 and lax.axis_size(TP) == 2
 
 
+def cut(parts):
+    return pointwise(
+        "cut",
+        lambda *refs: [ref[...] for ref in refs],
+        [],
+        parts,
+        [((rows, array.shape[1]), array.dtype) for array, rows, _ in parts],
+    )
+
+
 def gather_first(own):
     if not paired():
         return [own]
@@ -681,7 +691,8 @@
     if not paired():
         return got
     size = got[0].shape[0] // 2
-    corner = [swap(got[1][:size], CTX, 2), swap(got[2][size:], TP, 1)]
+    sent = cut([(got[1], size, 0), (got[2], size, 1)])
+    corner = [swap(sent[0], CTX, 2), swap(sent[1], TP, 1)]
     return got + [swap(got[1], CTX, 1), swap(got[2], CTX, 1)] + corner
 
 
@@ -705,10 +716,11 @@
         ]
         results.append(stack(parts, 8 * size))
     corner, results = lax.optimization_barrier((corner, results))
+    sent = cut([(item, half, at) for item in corner for at in (0, 1)])
     for which in range(2):
         parts = [(corner[which], 3 * size)]
-        for at in (0, half):
-            parts.append((swap(corner[which][at : at + half], CTX, 1), 7 * size + at))
+        for at in (0, 1):
+            parts.append((swap(sent[2 * which + at], CTX, 1), 7 * size + at * half))
         results[which] = fill(results[which], parts)
     return results
 

time: 567 us -> 565 us (level)
  local copies, waits for them, and re-layouts: 28 us -> 19.6 us
    slice x4 -> x0, local copies, waits for them, and re-layouts: 7.2 us -> none  [the longest x2 4.61 us: gather_second(): corner = [swap(got[1][:size], CTX, 2), swap(got[2][size:], TP, 1)]]
    pallas_call x14 -> x16, Pallas kernels: 42.2 us -> 46.8 us  [pointwise(): pl.pallas_call(kernel, grid=(1,), in_specs=[pl.BlockSpec(memory_space=plt...]
    unnamed x81 -> x75, local copies, waits for them, and re-layouts: 16.7 us -> 15.5 us
  transfers between devices with their start and end apart: 58 -> 58, of which waited for: 20 -> 21; matrix products, arithmetic and copies ran while one was open for 4% -> 3% of each run, Pallas kernels for 50% -> 51%
where the time goes in v5:
time: 565 us; the launch traced here: 557 us
  Pallas kernels  295 us (52%)
  waiting for transfers between devices  126 us (22%)
  starting transfers between devices  100 us (18%)
  local copies, waits for them, and re-layouts  19.6 us (3%)
  other arithmetic  13 us (2%)
    pallas_call x6, Pallas kernels, row_call(): pl.pallas_call(kernel, grid=(count,), in_specs=[pl.BlockSpec((size, item....  93.2 us
    ppermute x35, waiting for transfers between devices, swap(): lax.ppermute(values, axis, [(place, place ^ bit) for place in range(size)])  79.8 us
    pallas_call x2, Pallas kernels, attention(): pl.pallas_call(attention_kernel, grid_spec=pltpu.PrefetchScalarGridSpec(n...  67.9 us
    ppermute x19, starting transfers between devices, move(): return lax.ppermute(values, FSDP, pairs)  54.4 us
    pallas_call x6, Pallas kernels, grad_pieces(): pl.pallas_call(functools.partial(grad_kernel, [len(rights) for _, rights...  50.2 us
    pallas_call x16, Pallas kernels, pointwise(): pl.pallas_call(kernel, grid=(1,), in_specs=[pl.BlockSpec(memory_space=plt...  46.8 us
    ppermute x19, waiting for transfers between devices, move(): return lax.ppermute(values, FSDP, pairs)  44.5 us
    ppermute x35, starting transfers between devices, swap(): lax.ppermute(values, axis, [(place, place ^ bit) for place in range(size)])  30.1 us
  transfers between devices with their start and end apart: 58, of which 21 were waited for; matrix products, arithmetic and copies ran while one was open for 3% of the time, Pallas kernels for 51%

profile of v5, /device:TPU:0, one launch (start us, length us, event | category | flops | bytes accessed | tf_op | source)
XLA Modules:
  0.0 556.6 jit_solution(13729495554163039399)
XLA Ops:
  28.9 5.6 fusion.6
  34.5 35.0 %collective-permute-done.3.refs_1_ = bf16[512,1024]{1,0:T(8,128)(2,1)S(1)} collective-permute-done((bf16[512,1024]{1,0:T(8,128)(2,1)S(1)}, bf16[512,1024]{1,0:T(8,128)(2,1)S(1)}, u32[]{:S(2)}, u32[]{:S(2)}) %collective-permute-start.3) | collective-permute-done | bytes 1048608 | tf_op jit(solution)/shard_map/fsdp_1/ppermute | solution.py:530
  82.3 6.2 %stack.2.refs_3_ = bf16[2048,2048]{1,0:T(8,128)(2,1)} custom-call(bf16[512,2048]{1,0:T(8,128)(2,1)} %pad_maximum_fusion.refs_0_, bf16[512,2048]{1,0:T(8,128)(2,1)} %collective-permute-done.5.refs_0_.refs_1_, bf16[512,2048]{1,0:T(8,128)(2,1)} %collective-permute-done.6.refs_1_.refs_2_, bf16[512,2048]{1,0:T(8,128)(2,1)} %collective-permute-done.7.refs_3_, ...), custom_call_target="tpu_custom_call" | custom-call | tf_op jit(solution)/shard_map/stack/pallas_call | solution.py:432
  88.5 6.2 %stack.3.refs_3_ = bf16[2048,2048]{1,0:T(8,128)(2,1)} custom-call(bf16[512,2048]{1,0:T(8,128)(2,1)} %pad_maximum_fusion.refs_0_, bf16[512,2048]{1,0:T(8,128)(2,1)} %collective-permute-done.5.refs_0_.refs_1_, bf16[512,2048]{1,0:T(8,128)(2,1)} %collective-permute-done.6.refs_1_.refs_2_, bf16[512,2048]{1,0:T(8,128)(2,1)} %collective-permute-done.7.refs_3_, ...), custom_call_target="tpu_custom_call" | custom-call | tf_op jit(solution)/shard_map/stack/pallas_call | solution.py:432
  94.7 7.0 %collective-permute-done.9.refs_0_.refs_1_ = bf16[256,2048]{1,0:T(8,128)(2,1)S(1)} collective-permute-done((bf16[256,2048]{1,0:T(8,128)(2,1)}, bf16[256,2048]{1,0:T(8,128)(2,1)S(1)}, u32[]{:S(2)}, u32[]{:S(2)}) %collective-permute-start.9) | collective-permute-done | bytes 1048608 | tf_op jit(solution)/shard_map/ctx_2/ppermute | solution.py:530
  125.2 15.4 %project.1 = (bf16[2048,256]{1,0:T(8,128)(2,1)}, bf16[2048,256]{1,0:T(8,128)(2,1)}, bf16[2048,256]{1,0:T(8,128)(2,1)}, bf16[256,2048]{1,0:T(8,128)(2,1)}, bf16[2...) custom-call(bf16[2048,2048]{1,0:T(8,128)(2,1)} %fill.3.normed.refs_0_, ...), custom_call_target="tpu_custom_call" | custom-call | tf_op jit(solution)/shard_map/project/pallas_call | solution.py:232
  141.2 33.9 %attention_0.1 = (bf16[2048,256]{1,0:T(8,128)(2,1)}, bf16[2048,256]{1,0:T(8,128)(2,1)}, bf16[2048,256]{1,0:T(8,128)(2,1)}, bf16[2048,256]{1,0:T(8,128)(2,1)}) custom-call(s32[8]{0:T(128)} %select_reduce_fusion.order, bf16[2048,256]{1,0:T(8,128)(2,1)} %get-tuple-element.317.query_in, bf16[2048,256]{1,0:T(8,128)(2,1)} %get-tuple-element.318.key_all, ...), custom_call_target="tpu_custom_call" | custom-call | tf_op jit(solution)/shard_map/attention_0/pallas_call | solution.py:182
  182.6 34.0 %attention_1.1 = (bf16[2048,256]{1,0:T(8,128)(2,1)}, bf16[2048,256]{1,0:T(8,128)(2,1)}, bf16[2048,256]{1,0:T(8,128)(2,1)}, bf16[2048,256]{1,0:T(8,128)(2,1)}) custom-call(s32[8]{0:T(128)} %select_reduce_fusion.order, bf16[2048,256]{1,0:T(8,128)(2,1)} %get-tuple-element.317.query_in, ...), custom_call_target="tpu_custom_call", output_to_operand_aliasing={{0}: (10, {}), {1}: (11, {}), {2}: (12, {}), {3}: (13, {})} | custom-call | tf_op jit(solution)/shard_map/attention_1/pallas_call | solution.py:182
  216.6 7.5 %grad_0.3 = bf16[1,512,1024]{2,1,0:T(8,128)(2,1)} custom-call(s32[4]{0:T(128)} %fusion.7.turns, bf16[2048,2048]{1,0:T(8,128)(2,1)} %fill.3.normed.refs_0_, bf16[2048,256]{1,0:T(8,128)(2,1)} %get-tuple-element.370.refs_1_.refs_0_, bf16[2048,256]{1,0:T(8,128)(2,1)} %get-tuple-element.371.refs_2_.refs_1_, bf16[2048,256]{1,0:T(8,128)(2,1)} %get-tuple-element.372.refs_3_.refs_2_, ...), custom_call_target="tpu_custom_call" | custom-call | tf_op jit(solution)/shard_map/grad_0/pallas_call | solution.py:375
  229.8 7.2 %collective-permute-start.24 = (bf16[512,1024]{1,0:T(8,128)(2,1)}, bf16[512,1024]{1,0:T(8,128)(2,1)}, u32[]{:S(2)}, u32[]{:S(2)}) collective-permute-start(bf16[512,1024]{1,0:T(8,128)(2,1)} %bitcast.37), channel_id=1, source_target_pairs={{0,8},{24,16},{1,9},{25,17},{2,10},{26,18},{3,11},{27,19},{4,12},{... | collective-permute-start | bytes 3145736 | tf_op jit(solution)/shard_map/line/ppermute | solution.py:546
  241.9 17.6 %hidden.1 = (bf16[2048,1024]{1,0:T(8,128)(2,1)S(1)}, bf16[2048,1024]{1,0:T(8,128)(2,1)}) custom-call(bf16[2048,2048]{1,0:T(8,128)(2,1)} %fill.3.normed.refs_0_, bf16[2048,1024]{1,0:T(8,128)(2,1)} %in_square.3.weight.refs_2_, f32[1,1024]{1,0:T(1,128)S(1)} %bitcast.53), custom_call_target="tpu_custom_call" | custom-call | tf_op jit(solution)/shard_map/hidden/pallas_call | solution.py:232
  259.6 12.4 %grad_1.3.refs_2_.refs_1_.refs_0_ = bf16[3,512,1024]{2,1,0:T(8,128)(2,1)} custom-call(s32[4]{0:T(128)S(1)} %copy-done.28, bf16[2048,2048]{1,0:T(8,128)(2,1)} %fill.3.normed.refs_0_, bf16[2048,256]{1,0:T(8,128)(2,1)S(1)} %copy-done.7, bf16[2048,256]{1,0:T(8,128)(2,1)S(1)} %copy-done.8, bf16[2048,256]{1,0:T(8,128)(2,1)S(1)} %copy-done.9, ...), custom_call_target="tpu_custom_call" | custom-call | tf_op jit(solution)/shard_map/grad_1/pallas_call | solution.py:375
  276.9 5.6 %collective-permute-start.27 = (bf16[512,1024]{1,0:T(8,128)(2,1)S(1)}, bf16[512,1024]{1,0:T(8,128)(2,1)S(1)}, u32[]{:S(2)}, u32[]{:S(2)}) collective-permute-start(bf16[512,1024]{1,0:T(8,128)(2,1)S(1)} %bitcast.50), channel_id=1, source_target_pairs={{0,8},{8,16},{1,9},{9,17},{2,10},{10,18},{3,11},{11,19},{4,12},{12... | collective-permute-start | bytes 3145736 | tf_op jit(solution)/shard_map/line/ppermute | solution.py:546
  288.3 10.5 %grad_1.4.refs_2_.refs_1_ = bf16[3,512,1024]{2,1,0:T(8,128)(2,1)S(1)} custom-call(s32[4]{0:T(128)S(1)} %copy-done.28, bf16[2048,2048]{1,0:T(8,128)(2,1)} %fill.2.grads.refs_4_.refs_0_, bf16[2048,1024]{1,0:T(8,128)(2,1)} %copy-done.4), custom_call_target="tpu_custom_call" | custom-call | tf_op jit(solution)/shard_map/grad_1/pallas_call | solution.py:375
  300.4 11.6 %back.3 = (bf16[2048,2048]{1,0:T(8,128)(2,1)}, f32[3,256]{1,0:T(4,128)S(1)}) custom-call(bf16[2048,256]{1,0:T(8,128)(2,1)S(1)} %copy-done.7, bf16[2048,256]{1,0:T(8,128)(2,1)S(1)} %copy-done.8, bf16[2048,256]{1,0:T(8,128)(2,1)S(1)} %copy-done.9, bf16[2048,1024]{1,0:T(8,128)(2,1)} %in_square.2.weight.refs_3_), custom_call_target="tpu_custom_call" | custom-call | tf_op jit(solution)/shard_map/back/pallas_call | solution.py:232
  327.7 12.9 %hidden_grad.1 = (bf16[2048,1024]{1,0:T(8,128)(2,1)S(1)}, f32[1,1024]{1,0:T(1,128)S(1)}) custom-call(bf16[2048,2048]{1,0:T(8,128)(2,1)} %fill.2.grads.refs_4_.refs_0_, bf16[2048,1024]{1,0:T(8,128)(2,1)} %get-tuple-element.400.slope, bf16[2048,1024]{1,0:T(8,128)(2,1)} %in_line.1.refs_2_.weight), custom_call_target="tpu_custom_call" | custom-call | tf_op jit(solution)/shard_map/hidden_grad/pallas_call | solution.py:232
  340.6 19.9 %back.4 = (bf16[1024,2048]{1,0:T(8,128)(2,1)}, bf16[1024,2048]{1,0:T(8,128)(2,1)}) custom-call(bf16[2048,1024]{1,0:T(8,128)(2,1)} %copy-done.4, bf16[2048,256]{1,0:T(8,128)(2,1)S(1)} %copy-done.10, bf16[2048,1024]{1,0:T(8,128)(2,1)} %in_line.1.refs_2_.weight, bf16[2048,1024]{1,0:T(8,128)(2,1)} %in_square.2.weight.refs_3_), custom_call_target="tpu_custom_call" | custom-call | tf_op jit(solution)/shard_map/back/pallas_call | solution.py:232
  390.9 10.5 %grad_1.5.refs_6_.refs_1_.refs_2_.refs_0_ = bf16[3,512,1024]{2,1,0:T(8,128)(2,1)S(1)} custom-call(s32[4]{0:T(128)S(1)} %copy-done.28, bf16[2048,2048]{1,0:T(8,128)(2,1)} %fill.3.normed.refs_0_, bf16[2048,1024]{1,0:T(8,128)(2,1)} %copy-done.5), custom_call_target="tpu_custom_call" | custom-call | tf_op jit(solution)/shard_map/grad_1/pallas_call | solution.py:375
  403.0 15.8 %back.5 = (bf16[1024,2048]{1,0:T(8,128)(2,1)}, bf16[1024,2048]{1,0:T(8,128)(2,1)}) custom-call(bf16[2048,1024]{1,0:T(8,128)(2,1)} %copy-done.5, bf16[2048,2048]{1,0:T(8,128)(2,1)} %get-tuple-element.425.refs_1_, bf16[2048,1024]{1,0:T(8,128)(2,1)} %in_square.3.weight.refs_2_), custom_call_target="tpu_custom_call" | custom-call | tf_op jit(solution)/shard_map/back/pallas_call | solution.py:232
  439.0 12.2 %collective-permute-done.43.refs_4_ = bf16[128,2048]{1,0:T(8,128)(2,1)S(1)} collective-permute-done((bf16[128,2048]{1,0:T(8,128)(2,1)S(1)}, bf16[128,2048]{1,0:T(8,128)(2,1)S(1)}, u32[]{:S(2)}, u32[]{:S(2)}) %collective-permute-start.43) | collective-permute-done | bytes 524320 | tf_op jit(solution)/shard_map/tp_1/ppermute | solution.py:530
  460.8 19.2 %collective-permute-done.40.refs_3_.refs_2_ = bf16[1024,1024]{1,0:T(8,128)(2,1)S(1)} collective-permute-done((bf16[1024,1024]{1,0:T(8,128)(2,1)}, bf16[1024,1024]{1,0:T(8,128)(2,1)S(1)}, u32[]{:S(2)}, u32[]{:S(2)}) %collective-permute-start.40) | collective-permute-done | bytes 2097184 | tf_op jit(solution)/shard_map/line/ppermute | solution.py:546
  480.0 6.3 %collective-permute-done.41.refs_4_.refs_3_ = bf16[1024,1024]{1,0:T(8,128)(2,1)} collective-permute-done((bf16[1024,1024]{1,0:T(8,128)(2,1)}, bf16[1024,1024]{1,0:T(8,128)(2,1)}, u32[]{:S(2)}, u32[]{:S(2)}) %collective-permute-start.41) | collective-permute-done | bytes 2097184 | tf_op jit(solution)/shard_map/line/ppermute | solution.py:546
  504.1 5.8 %tokens_grad.1 = (f32[256,2048]{1,0:T(8,128)}, f32[3,2048]{1,0:T(4,128)S(1)}) custom-call(bf16[256,2048]{1,0:T(8,128)(2,1)S(1)} %bitcast.35, bf16[256,2048]{1,0:T(8,128)(2,1)S(1)} %bitcast.45, bf16[1,2048]{1,0:T(2,128)(2,1)S(1)} %broadcast_in_dim.75.refs_2_, bf16[1024,2048]{1,0:T(8,128)(2,1)} %get-tuple-element.473.refs_0_.refs_2_.refs_3_, ...), custom_call_target="tpu_custom_call" | custom-call | tf_op jit(solution)/shard_map/tokens_grad/pallas_call | solution.py:404
  516.1 8.7 %collective-permute-done.48.refs_1_ = bf16[512,1024]{1,0:T(8,128)(2,1)} collective-permute-done((bf16[512,1024]{1,0:T(8,128)(2,1)}, bf16[512,1024]{1,0:T(8,128)(2,1)}, u32[]{:S(2)}, u32[]{:S(2)}) %collective-permute-start.48) | collective-permute-done | bytes 1048608 | tf_op jit(solution)/shard_map/line/ppermute | solution.py:546
  (252 shorter events, 227.6 us)
Async XLA Ops:
  18.5 53.5 %collective-permute-start.5 = (bf16[512,2048]{1,0:T(8,128)(2,1)}, bf16[512,2048]{1,0:T(8,128)(2,1)}, u32[]{:S(2)}, u32[]{:S(2)}) collective-permute-start(bf16[512,2048]{1,0:T(8,128)(2,1)} %pad_maximum_fusion.refs_0_), channel_id=1, source_target_pairs={{0,1},{1,0},{2,3},{3,2},{4,5},{5,4},{6,7},{7,6},{8,9},{9,8},{10,11... | collective-permute-start | bytes 6291464 | tf_op jit(solution)/shard_map/tp_1/ppermute | solution.py:530
  20.1 51.9 %collective-permute-start.6 = (bf16[512,2048]{1,0:T(8,128)(2,1)}, bf16[512,2048]{1,0:T(8,128)(2,1)}, u32[]{:S(2)}, u32[]{:S(2)}) collective-permute-start(bf16[512,2048]{1,0:T(8,128)(2,1)} %pad_maximum_fusion.refs_0_), channel_id=1, source_target_pairs={{0,4},{2,6},{4,0},{6,2},{1,5},{3,7},{5,1},{7,3},{8,12},{10,14},{12... | collective-permute-start | bytes 6291464 | tf_op jit(solution)/shard_map/ctx_2/ppermute | solution.py:530
  21.6 50.4 %collective-permute-start.7 = (bf16[512,2048]{1,0:T(8,128)(2,1)}, bf16[512,2048]{1,0:T(8,128)(2,1)}, u32[]{:S(2)}, u32[]{:S(2)}) collective-permute-start(bf16[512,2048]{1,0:T(8,128)(2,1)} %pad_maximum_fusion.refs_0_), channel_id=1, source_target_pairs={{0,2},{2,0},{4,6},{6,4},{1,3},{3,1},{5,7},{7,5},{8,10},{10,8},{12,... | collective-permute-start | bytes 6291464 | tf_op jit(solution)/shard_map/ctx_1/ppermute | solution.py:530
  21.6 47.9 %collective-permute-start.3 = (bf16[512,1024]{1,0:T(8,128)(2,1)S(1)}, bf16[512,1024]{1,0:T(8,128)(2,1)S(1)}, u32[]{:S(2)}, u32[]{:S(2)}) collective-permute-start(bf16[512,1024]{1,0:T(8,128)(2,1)S(1)} %laid.1.refs_0_), channel_id=1, source_target_pairs={{0,8},{8,0},{16,24},{24,16},{1,9},{9,1},{17,25},{25,17},{2,10},{10... | collective-permute-start | bytes 3145736 | tf_op jit(solution)/shard_map/fsdp_1/ppermute | solution.py:530
  23.2 48.8 %collective-permute-start.4 = (bf16[512,1024]{1,0:T(8,128)(2,1)S(1)}, bf16[512,1024]{1,0:T(8,128)(2,1)}, u32[]{:S(2)}, u32[]{:S(2)}) collective-permute-start(bf16[512,1024]{1,0:T(8,128)(2,1)S(1)} %laid.1.refs_0_), channel_id=1, source_target_pairs={{0,16},{8,24},{16,0},{24,8},{1,17},{9,25},{17,1},{25,9},{2,18},{10... | collective-permute-start | bytes 3145736 | tf_op jit(solution)/shard_map/fsdp_2/ppermute | solution.py:530
  112.2 62.9 %collective-permute-start.17 = (bf16[512,1024]{1,0:T(8,128)(2,1)}, bf16[512,1024]{1,0:T(8,128)(2,1)}, u32[]{:S(2)}, u32[]{:S(2)}) collective-permute-start(bf16[512,1024]{1,0:T(8,128)(2,1)} %bitcast.5.refs_0_), channel_id=1, source_target_pairs={{0,8},{8,0},{16,24},{24,16},{1,9},{9,1},{17,25},{25,17},{2,10},{10... | collective-permute-start | bytes 3145736 | tf_op jit(solution)/shard_map/fsdp_1/ppermute | solution.py:530
  112.7 62.5 %collective-permute-start.18 = (bf16[512,1024]{1,0:T(8,128)(2,1)}, bf16[512,1024]{1,0:T(8,128)(2,1)}, u32[]{:S(2)}, u32[]{:S(2)}) collective-permute-start(bf16[512,1024]{1,0:T(8,128)(2,1)} %bitcast.5.refs_0_), channel_id=1, source_target_pairs={{0,16},{8,24},{16,0},{24,8},{1,17},{9,25},{17,1},{25,9},{2,18},{10... | collective-permute-start | bytes 3145736 | tf_op jit(solution)/shard_map/fsdp_2/ppermute | solution.py:530
  115.2 59.8 %all-to-all-start.1 = ((bf16[4,128,1024]{2,1,0:T(8,128)(2,1)}), bf16[4,128,1024]{2,1,0:T(8,128)(2,1)S(1)}, u32[]{:S(2)}, u32[]{:S(2)}) async-start(bf16[4,128,1024]{2,1,0:T(8,128)(2,1)} %copy-done.12), calls=%async_computation.1 | async-start | bytes 2097152 | tf_op jit(solution)/shard_map/all_to_all | solution.py:911
  175.1 49.0 %collective-permute-start.19 = (bf16[512,1024]{1,0:T(8,128)(2,1)S(1)}, bf16[512,1024]{1,0:T(8,128)(2,1)S(1)}, u32[]{:S(2)}, u32[]{:S(2)}) collective-permute-start(bf16[512,1024]{1,0:T(8,128)(2,1)S(1)} %bitcast.39), channel_id=1, source_target_pairs={{0,8},{8,16},{16,24},{1,9},{9,17},{17,25},{2,10},{10,18},{18,26},{... | collective-permute-start | bytes 3145736 | tf_op jit(solution)/shard_map/line/ppermute | solution.py:546
  177.1 47.0 %collective-permute-start.20 = (bf16[512,1024]{1,0:T(8,128)(2,1)S(1)}, bf16[512,1024]{1,0:T(8,128)(2,1)}, u32[]{:S(2)}, u32[]{:S(2)}) collective-permute-start(bf16[512,1024]{1,0:T(8,128)(2,1)S(1)} %bitcast.40), channel_id=1, source_target_pairs={{8,0},{16,8},{24,16},{9,1},{17,9},{25,17},{10,2},{18,10},{26,18},{... | collective-permute-start | bytes 3145736 | tf_op jit(solution)/shard_map/line/ppermute | solution.py:546
  178.7 48.1 %collective-permute-start.21 = (bf16[512,1024]{1,0:T(8,128)(2,1)}, bf16[512,1024]{1,0:T(8,128)(2,1)}, u32[]{:S(2)}, u32[]{:S(2)}) collective-permute-start(bf16[512,1024]{1,0:T(8,128)(2,1)} %collective-permute-done.18.refs_2_), channel_id=1, source_target_pairs={{0,8},{8,0},{16,24},{24,16},{1,9},{9,1},{17,25},{25,17},{2,10},{10... | collective-permute-start | bytes 3145736 | tf_op jit(solution)/shard_map/fsdp_1/ppermute | solution.py:530
  226.8 45.2 %collective-permute-start.22 = (bf16[512,1024]{1,0:T(8,128)(2,1)S(1)}, bf16[512,1024]{1,0:T(8,128)(2,1)}, u32[]{:S(2)}, u32[]{:S(2)}) collective-permute-start(bf16[512,1024]{1,0:T(8,128)(2,1)S(1)} %collective-permute-done.19.refs_1_), channel_id=1, source_target_pairs={{8,16},{16,24},{9,17},{17,25},{10,18},{18,26},{11,19},{19,27},{12,... | collective-permute-start | bytes 3145736 | tf_op jit(solution)/shard_map/line/ppermute | solution.py:546
  228.5 43.5 %collective-permute-start.23 = (bf16[512,1024]{1,0:T(8,128)(2,1)}, bf16[512,1024]{1,0:T(8,128)(2,1)}, u32[]{:S(2)}, u32[]{:S(2)}) collective-permute-start(bf16[512,1024]{1,0:T(8,128)(2,1)} %collective-permute-done.20.refs_2_), channel_id=1, source_target_pairs={{8,0},{16,8},{9,1},{17,9},{10,2},{18,10},{11,3},{19,11},{12,4},{20... | collective-permute-start | bytes 3145736 | tf_op jit(solution)/shard_map/line/ppermute | solution.py:546
  229.8 42.3 %collective-permute-start.24 = (bf16[512,1024]{1,0:T(8,128)(2,1)}, bf16[512,1024]{1,0:T(8,128)(2,1)}, u32[]{:S(2)}, u32[]{:S(2)}) collective-permute-start(bf16[512,1024]{1,0:T(8,128)(2,1)} %bitcast.37), channel_id=1, source_target_pairs={{0,8},{24,16},{1,9},{25,17},{2,10},{26,18},{3,11},{27,19},{4,12},{... | collective-permute-start | bytes 3145736 | tf_op jit(solution)/shard_map/line/ppermute | solution.py:546
  272.1 40.0 %collective-permute-start.25 = (bf16[512,1024]{1,0:T(8,128)(2,1)}, bf16[512,1024]{1,0:T(8,128)(2,1)}, u32[]{:S(2)}, u32[]{:S(2)}) collective-permute-start(bf16[512,1024]{1,0:T(8,128)(2,1)} %collective-permute-done.22.refs_3_), channel_id=1, source_target_pairs={{16,24},{17,25},{18,26},{19,27},{20,28},{21,29},{22,30},{23,31}} | collective-permute-start | bytes 3145736 | tf_op jit(solution)/shard_map/line/ppermute | solution.py:546
  273.7 38.4 %collective-permute-start.26 = (bf16[512,1024]{1,0:T(8,128)(2,1)}, bf16[512,1024]{1,0:T(8,128)(2,1)}, u32[]{:S(2)}, u32[]{:S(2)}) collective-permute-start(bf16[512,1024]{1,0:T(8,128)(2,1)} %collective-permute-done.23.refs_4_), channel_id=1, source_target_pairs={{8,0},{9,1},{10,2},{11,3},{12,4},{13,5},{14,6},{15,7}} | collective-permute-start | bytes 3145736 | tf_op jit(solution)/shard_map/line/ppermute | solution.py:546
  312.1 48.5 %collective-permute-start.29 = (bf16[512,1024]{1,0:T(8,128)(2,1)S(1)}, bf16[512,1024]{1,0:T(8,128)(2,1)S(1)}, u32[]{:S(2)}, u32[]{:S(2)}) collective-permute-start(bf16[512,1024]{1,0:T(8,128)(2,1)S(1)} %bitcast.42), channel_id=1, source_target_pairs={{0,8},{24,16},{1,9},{25,17},{2,10},{26,18},{3,11},{27,19},{4,12},{... | collective-permute-start | bytes 3145736 | tf_op jit(solution)/shard_map/line/ppermute | solution.py:546
  320.9 39.7 %collective-permute-start.30 = (bf16[512,1024]{1,0:T(8,128)(2,1)}, bf16[512,1024]{1,0:T(8,128)(2,1)S(1)}, u32[]{:S(2)}, u32[]{:S(2)}) collective-permute-start(bf16[512,1024]{1,0:T(8,128)(2,1)} %bitcast.12), channel_id=1, source_target_pairs={{0,8},{8,16},{16,24},{1,9},{9,17},{17,25},{2,10},{10,18},{18,26},{... | collective-permute-start | bytes 3145736 | tf_op jit(solution)/shard_map/line/ppermute | solution.py:546
  322.2 39.4 %collective-permute-start.31 = (bf16[512,1024]{1,0:T(8,128)(2,1)}, bf16[512,1024]{1,0:T(8,128)(2,1)}, u32[]{:S(2)}, u32[]{:S(2)}) collective-permute-start(bf16[512,1024]{1,0:T(8,128)(2,1)} %bitcast.13), channel_id=1, source_target_pairs={{8,0},{16,8},{24,16},{9,1},{17,9},{25,17},{10,2},{18,10},{26,18},{... | collective-permute-start | bytes 3145736 | tf_op jit(solution)/shard_map/line/ppermute | solution.py:546
  374.4 44.4 %collective-permute-start.37 = (bf16[512,1024]{1,0:T(8,128)(2,1)S(1)}, bf16[512,1024]{1,0:T(8,128)(2,1)S(1)}, u32[]{:S(2)}, u32[]{:S(2)}) collective-permute-start(bf16[512,1024]{1,0:T(8,128)(2,1)S(1)} %bitcast.48), channel_id=1, source_target_pairs={{0,8},{8,16},{1,9},{9,17},{2,10},{10,18},{3,11},{11,19},{4,12},{12... | collective-permute-start | bytes 3145736 | tf_op jit(solution)/shard_map/line/ppermute | solution.py:546
  379.3 39.5 %collective-permute-start.38 = (bf16[512,1024]{1,0:T(8,128)(2,1)S(1)}, bf16[512,1024]{1,0:T(8,128)(2,1)S(1)}, u32[]{:S(2)}, u32[]{:S(2)}) collective-permute-start(bf16[512,1024]{1,0:T(8,128)(2,1)S(1)} %bitcast.49), channel_id=1, source_target_pairs={{16,8},{24,16},{17,9},{25,17},{18,10},{26,18},{19,11},{27,19},{20,... | collective-permute-start | bytes 3145736 | tf_op jit(solution)/shard_map/line/ppermute | solution.py:546
  380.1 43.8 %collective-permute-start.39 = (bf16[512,1024]{1,0:T(8,128)(2,1)S(1)}, bf16[512,1024]{1,0:T(8,128)(2,1)S(1)}, u32[]{:S(2)}, u32[]{:S(2)}) collective-permute-start(bf16[512,1024]{1,0:T(8,128)(2,1)S(1)} %bitcast.46), channel_id=1, source_target_pairs={{0,8},{24,16},{1,9},{25,17},{2,10},{26,18},{3,11},{27,19},{4,12},{... | collective-permute-start | bytes 3145736 | tf_op jit(solution)/shard_map/line/ppermute | solution.py:546
  429.8 50.2 %collective-permute-start.40 = (bf16[1024,1024]{1,0:T(8,128)(2,1)}, bf16[1024,1024]{1,0:T(8,128)(2,1)S(1)}, u32[]{:S(2)}, u32[]{:S(2)}) collective-permute-start(bf16[1024,1024]{1,0:T(8,128)(2,1)} %bitcast.62), channel_id=1, source_target_pairs={{0,8},{8,16},{16,24},{1,9},{9,17},{17,25},{2,10},{10,18},{18,26},{... | collective-permute-start | bytes 6291464 | tf_op jit(solution)/shard_map/line/ppermute | solution.py:546
  434.3 52.0 %collective-permute-start.41 = (bf16[1024,1024]{1,0:T(8,128)(2,1)}, bf16[1024,1024]{1,0:T(8,128)(2,1)}, u32[]{:S(2)}, u32[]{:S(2)}) collective-permute-start(bf16[1024,1024]{1,0:T(8,128)(2,1)} %bitcast.61), channel_id=1, source_target_pairs={{8,0},{16,8},{24,16},{9,1},{17,9},{25,17},{10,2},{18,10},{26,18},{... | collective-permute-start | bytes 6291464 | tf_op jit(solution)/shard_map/line/ppermute | solution.py:546
  (70 other events, 883.5 us)
